TPU v7x, 32 devices: a whole 2x2x4 slice. The times are simulated.
32 devices in a mesh: group: 2 (over y), role: 2 (over x), tp: 4 (over z), sub: 2 (over core).
Axes of the slice: x: 2, y: 2, z: 4, core: 2. Of those that a mesh axis runs over, the one named last changes fastest.
Arguments:
- residual: bfloat16 [128, 3072], P(('group', 'role', 'tp', 'sub')), parts along dimension 0, may hold values from -12 to 12
- query: bfloat16 [128, 3072], P(('group', 'role', 'tp', 'sub')), parts along dimension 0, may hold values from -6 to 6
- new_key: bfloat16 [128, 1024], P(('group', 'role', 'tp', 'sub')), parts along dimension 0, may hold values from -6 to 6
- new_value: bfloat16 [128, 1024], P(('group', 'role', 'tp', 'sub')), parts along dimension 0, may hold values from -6 to 6
- cache_key: bfloat16 [128, 128, 1024], P(('group', 'role', 'tp', 'sub')), parts along dimension 0, may hold values from -6 to 6
- cache_value: bfloat16 [128, 128, 1024], P(('group', 'role', 'tp', 'sub')), parts along dimension 0, may hold values from -6 to 6
- lengths: int32 [128], P(('group', 'role', 'tp', 'sub')), parts along dimension 0, may hold values from 2 to 128, as said below
- norm_gain: float32 [3072], replicated, may hold values from 0.1 to 1.9
- expert_ids: int32 [128, 2], P(('group', 'role', 'tp', 'sub')), parts along dimension 0, may hold values from 0 to 3, all different within a row; in each aligned block of 4 rows (0 to 3, 4 to 7, ...) at most 3 rows name the same one
- gate_levels: int32 [128, 2], P(('group', 'role', 'tp', 'sub')), parts along dimension 0, may hold values from 1 to 255
- gate_codes: bfloat16 [4, 3072, 8192], P('role', 'sub', 'tp'), may hold values from -7.5 to 7.5, as said below
- gate_scales: float32 [4, 24, 64], P('role', 'sub', 'tp'), may hold values from 0.0018042196 to 0.010825317
- up_codes: bfloat16 [4, 3072, 8192], P('role', 'sub', 'tp'), may hold values from -7.5 to 7.5, as said below
- up_scales: float32 [4, 24, 64], P('role', 'sub', 'tp'), may hold values from 0.0018042196 to 0.010825317
- down_codes: bfloat16 [4, 8192, 3072], P('role', 'tp', 'sub'), may hold values from -7.5 to 7.5, as said below
- down_scales: float32 [4, 64, 24], P('role', 'tp', 'sub'), may hold values from 0.0022097088 to 0.013258252
Outputs:
- mixed: bfloat16 [128, 3072], P(('group', 'role', 'tp', 'sub')), parts along dimension 0
There are 2 independent parts, one for each index of `group`. A program takes and returns all parts, laid end to end along the dimension named above; an argument that names none is the same for every part. Nothing has to cross between parts.
Inputs may be any that keep to these rules, and one draw needn't show every extreme that they name: The first lengths[r] positions of row r's cache are filled; the first row of every part fills all 128. `expert_ids`: a row's two ids differ; among the rows of one device no expert is named by more than 3 rows, and some device has an expert named by exactly 3. `gate_codes`: each entry is s * 2 ** k * (1 + m / 8) with sign s, whole k from -2 to 2 and whole m from 0 to 7. `up_codes`: each entry is s * 2 ** k * (1 + m / 8) with sign s, whole k from -2 to 2 and whole m from 0 to 7. `down_codes`: each entry is s * 2 ** k * (1 + m / 8) with sign s, whole k from -2 to 2 and whole m from 0 to 7.
All inputs are finite; a program needn't handle non-finite values.
Results may differ from a plain program's by a relative error of at most 0.014.
Values may be sent and summed in bfloat16 or wider, within the bound.
No kernel may reach another device: no remote copies, remote signals or barrier semaphores. Data moves between devices by JAX's collectives and lax.ppermute only.
A program may use at most 192 MiB of HBM per device.

v0:
```python
import math

import jax
import jax.numpy as jnp
from jax import lax
from jax.sharding import PartitionSpec as P

D = 3072
HEADS = 24
KV_HEADS = 8
HEAD_DIM = 128
EXPERTS = 4
QBLOCK = 128
CAP = 3


def dequantize(codes, scales):
    experts, rows, columns = codes.shape
    widened = jnp.repeat(scales, QBLOCK, axis=-1)
    blocked = codes.astype(jnp.float32).reshape(experts, rows // QBLOCK, QBLOCK, columns)
    return (blocked * widened[:, :, None, :]).reshape(experts, rows, columns).astype(jnp.bfloat16)


def attend(query, new_key, new_value, cache_key, cache_value, lengths):
    row_count = query.shape[0]
    positions = cache_key.shape[1]
    group_size = HEADS // KV_HEADS
    queries = query.reshape(row_count, KV_HEADS, group_size, HEAD_DIM)
    cache_keys = cache_key.reshape(row_count, positions, KV_HEADS, HEAD_DIM)
    cache_values = cache_value.reshape(row_count, positions, KV_HEADS, HEAD_DIM)
    fresh_key = new_key.reshape(row_count, KV_HEADS, HEAD_DIM)
    fresh_value = new_value.reshape(row_count, KV_HEADS, HEAD_DIM)
    factor = 1.0 / math.sqrt(HEAD_DIM)
    scores = (
        jnp.einsum("rkgd,rpkd->rkgp", queries, cache_keys, preferred_element_type=jnp.float32)
        * factor
    )
    fresh_score = (
        jnp.einsum("rkgd,rkd->rkg", queries, fresh_key, preferred_element_type=jnp.float32) * factor
    )
    valid_mask = lax.broadcasted_iota(jnp.int32, (row_count, positions), 1) < lengths[:, None]
    valid_mask = valid_mask[:, None, None, :]
    masked = jnp.where(valid_mask, scores, -1e30)
    peak_score = jnp.maximum(jnp.max(masked, axis=-1), fresh_score)
    exp_scores = jnp.where(valid_mask, jnp.exp(masked - peak_score[..., None]), 0.0)
    fresh_exp = jnp.exp(fresh_score - peak_score)
    denominator = jnp.sum(exp_scores, axis=-1) + fresh_exp
    probabilities = (exp_scores / denominator[..., None]).astype(jnp.bfloat16)
    fresh_prob = (fresh_exp / denominator).astype(jnp.bfloat16)
    attended = jnp.einsum(
        "rkgp,rpkd->rkgd", probabilities, cache_values, preferred_element_type=jnp.float32
    )
    attended = (
        attended
        + fresh_prob.astype(jnp.float32)[..., None] * fresh_value.astype(jnp.float32)[:, :, None, :]
    )
    return attended.reshape(row_count, D)


def slot_tables(expert_ids, gate_levels, capacity):
    row_count = expert_ids.shape[0]
    flat_ids = expert_ids.reshape(row_count * 2)
    onehot = (flat_ids[:, None] == jnp.arange(EXPERTS, dtype=jnp.int32)[None, :]).astype(jnp.int32)
    earlier = jnp.cumsum(onehot, axis=0) - onehot
    slot_index = jnp.sum(onehot * earlier, axis=1)
    in_slot = (slot_index[:, None] == jnp.arange(capacity, dtype=jnp.int32)[None, :]).astype(
        jnp.float32
    )
    placing = (onehot.astype(jnp.float32)[:, :, None] * in_slot[:, None, :]).reshape(
        row_count, 2, EXPERTS, capacity
    )
    levels = gate_levels.astype(jnp.float32)
    shares = levels / jnp.sum(levels, axis=1, keepdims=True)
    selection = jnp.sum(placing, axis=1)
    weighting = jnp.sum(placing * shares[:, :, None, None], axis=1)
    return (selection, weighting)


def layer_rows(row_inputs, norm_gain, weights, capacity):
    (
        residual,
        query,
        new_key,
        new_value,
        cache_key,
        cache_value,
        lengths,
        expert_ids,
        gate_levels,
    ) = row_inputs
    w_gate, w_up, w_down = weights
    stream = residual.astype(jnp.float32) + attend(
        query, new_key, new_value, cache_key, cache_value, lengths
    )
    mean_square = jnp.mean(stream * stream, axis=1, keepdims=True)
    normed = (stream * lax.rsqrt(mean_square + 1e-05) * norm_gain).astype(jnp.bfloat16)
    role_count = lax.axis_size("role")
    sub_count = lax.axis_size("sub")
    local_experts = EXPERTS // role_count
    half_width = D // sub_count
    row_count = normed.shape[0]
    selection, weighting = slot_tables(expert_ids, gate_levels, capacity)
    picked = selection.reshape(row_count, role_count, local_experts, capacity).astype(jnp.bfloat16)
    halves = normed.reshape(row_count, sub_count, half_width)
    outgoing = jnp.einsum(
        "raec,rhd->ahced", picked, halves, preferred_element_type=jnp.float32
    ).astype(jnp.bfloat16)
    arrived = lax.all_to_all(
        lax.all_to_all(outgoing, "role", split_axis=0, concat_axis=0, tiled=True),
        "sub",
        split_axis=1,
        concat_axis=1,
        tiled=True,
    )
    own_rows = role_count * sub_count * capacity
    arrived = arrived.reshape(own_rows, local_experts, half_width)
    row_piece = lax.all_gather(arrived, "tp", axis=0, tiled=True)
    gate_part = jnp.einsum("ned,edf->nef", row_piece, w_gate, preferred_element_type=jnp.float32)
    up_part = jnp.einsum("ned,edf->nef", row_piece, w_up, preferred_element_type=jnp.float32)
    partial_in = jnp.concatenate((gate_part, up_part), axis=2)
    unit_count = w_gate.shape[2]
    summed = lax.psum(partial_in.astype(jnp.bfloat16), "sub").astype(jnp.float32)
    hidden = (jax.nn.silu(summed[:, :, :unit_count]) * summed[:, :, unit_count:]).astype(
        jnp.bfloat16
    )
    returned = lax.psum_scatter(
        jnp.einsum("nef,efd->ned", hidden, w_down, preferred_element_type=jnp.float32).astype(
            jnp.bfloat16
        ),
        "tp",
        scatter_dimension=0,
        tiled=True,
    )
    expert_out = returned.reshape(role_count, sub_count, capacity, local_experts, half_width)
    returned_rows = lax.all_to_all(
        lax.all_to_all(expert_out, "role", split_axis=0, concat_axis=0, tiled=True),
        "sub",
        split_axis=1,
        concat_axis=1,
        tiled=True,
    )
    spread = weighting.reshape(row_count, role_count, local_experts, capacity)
    expert_sum = jnp.einsum("raec,ahced->rhd", spread, returned_rows.astype(jnp.float32)).reshape(
        row_count, D
    )
    return (stream + expert_sum).astype(jnp.bfloat16)


def per_device(
    residual,
    query,
    new_key,
    new_value,
    cache_key,
    cache_value,
    lengths,
    norm_gain,
    expert_ids,
    gate_levels,
    gate_codes,
    gate_scales,
    up_codes,
    up_scales,
    down_codes,
    down_scales,
):
    weights = (
        dequantize(gate_codes, gate_scales),
        dequantize(up_codes, up_scales),
        dequantize(down_codes, down_scales),
    )
    row_inputs = (
        residual,
        query,
        new_key,
        new_value,
        cache_key,
        cache_value,
        lengths,
        expert_ids,
        gate_levels,
    )
    return layer_rows(row_inputs, norm_gain, weights, CAP)


def solution(mesh):
    in_specs = (
        P(("group", "role", "tp", "sub"), None),
        P(("group", "role", "tp", "sub"), None),
        P(("group", "role", "tp", "sub"), None),
        P(("group", "role", "tp", "sub"), None),
        P(("group", "role", "tp", "sub"), None, None),
        P(("group", "role", "tp", "sub"), None, None),
        P(("group", "role", "tp", "sub")),
        P(),
        P(("group", "role", "tp", "sub"), None),
        P(("group", "role", "tp", "sub"), None),
        P("role", "sub", "tp"),
        P("role", "sub", "tp"),
        P("role", "sub", "tp"),
        P("role", "sub", "tp"),
        P("role", "tp", "sub"),
        P("role", "tp", "sub"),
    )
    out_specs = P(("group", "role", "tp", "sub"), None)
    return jax.shard_map(
        per_device, mesh=mesh, in_specs=in_specs, out_specs=out_specs, check_vma=False
    )
```

profile of v0, /device:TPU:0, one launch (start us, length us, event | category | flops | bytes accessed | tf_op | source)
XLA Modules:
  0.0 162.2 jit_solution(14392147022763181010)
XLA Ops:
  6.5 0.9 copy.66
  7.4 0.7 convert_convert_fusion
  8.1 0.7 iota_compare_fusion.3
  8.9 0.8 reshape.133
  9.6 0.7 reshape.149
  10.5 0.7 fusion.34
  11.5 0.7 convert_bitcast_fusion
  12.2 1.7 %convolution_add_fusion = f32[4,8,3,128]{3,2,1,0:T(4,128)S(1)} fusion(f32[4,8,3,128]{3,2,1,0:T(4,128)S(1)} %get-tuple-element.10, f32[4,8,128]{2,1,0:T(8,128)S(1)} %bitcast.92, f32[4,8,3]{2,1,0:T(8,128)S(1)} %get-tuple-element.8, f32[4,8,3]{2,1,0:T(8,128)S(1)} %get-tuple-element.7, f32[4,8,3]{2,1,0:T(8,128)S(1)} %multiply_maximum_fusion, ...), kind=kOutput, calls=%fused_computation.17 | convolution fusion | flops 3219456 | bytes 1164928 | tf_op jit(solution)/shard_map/rkgp,rpkd->rkgd/dot_general | solution.py:50
  13.9 0.9 multiply_reduce_fusion
  15.3 0.7 convert_reduce_fusion
  16.9 0.8 multiply_convert_fusion
  18.6 4.2 %all-to-all-start = ((bf16[2,2,3,2,1536]{4,3,2,1,0:T(2,128)(2,1)}), bf16[2,2,3,2,1536]{4,3,2,1,0:T(2,128)(2,1)S(1)}, u32[]{:S(2)}, u32[]{:S(2)}) async-start(bf16[2,2,3,2,1536]{4,3,2,1,0:T(2,128)(2,1)} %copy.74), calls=%async_computation | async-start | bytes 147456 | tf_op jit(solution)/shard_map/all_to_all | solution.py:109
  22.8 0.8 broadcast_in_dim.46
  23.9 0.8 broadcast_in_dim.47
  25.0 13.2 %fusion.1 = bf16[2,1536,2048]{2,1,0:T(8,128)(2,1)} fusion(bf16[2,1536,2048]{2,1,0:T(8,128)(2,1)} %param.26, f32[2,12,2048]{2,1,0:T(8,128)S(1)} %copy.70), kind=kLoop, calls=%fused_computation.3 | loop fusion | flops 18874368 | bytes 25362432 | tf_op jit(solution)/shard_map/convert_element_type | solution.py:21
  38.2 6.1 %fusion = bf16[2,1536,2048]{2,1,0:T(8,128)(2,1)} fusion(bf16[2,1536,2048]{2,1,0:T(8,128)(2,1)S(1)} %bitcast.84, f32[2,12,2048]{2,1,0:T(8,128)S(1)} %copy.78), kind=kLoop, calls=%fused_computation.1 | loop fusion | flops 18874368 | bytes 25362432 | tf_op jit(solution)/shard_map/convert_element_type | solution.py:21
  44.4 4.3 %all_to_all.20 = bf16[2,2,3,2,1536]{4,3,2,0,1:T(2,128)(2,1)S(1)} all-to-all(bf16[2,2,3,2,1536]{4,3,2,0,1:T(2,128)(2,1)S(1)} %copy.75), channel_id=1, replica_groups=mesh['group'=2,'role'=2,'tp'=4,'sub'=2] {'sub'}, dimensions={1} | all-to-all | bytes 147456 | tf_op jit(solution)/shard_map/all_to_all | solution.py:108
  48.7 14.8 %all_gather.3 = bf16[48,2,1536]{2,1,0:T(2,128)(2,1)S(1)} all-gather(bf16[12,2,1536]{2,1,0:T(2,128)(2,1)S(1)} %bitcast.86), channel_id=1, replica_groups=mesh['group'=2,'role'=2,'tp'=4,'sub'=2] {'tp'}, dimensions={0}, use_global_device_ids=true | all-gather | bytes 368640 | tf_op jit(solution)/shard_map/all_gather | solution.py:117
  63.5 6.9 %fusion.5 = bf16[48,2,2048]{2,0,1:T(8,128)(2,1)S(1)} fusion(bf16[2,1536,2048]{2,1,0:T(8,128)(2,1)} %fusion.1, bf16[48,2,1536]{2,1,0:T(2,128)(2,1)S(1)} %all_gather.3), kind=kOutput, calls=%fused_computation.12 | convolution fusion | flops 604176384 | bytes 13271040 | tf_op jit(solution)/shard_map/ned,edf->nef/dot_general | solution.py:118
  70.4 2.3 %fusion.6 = bf16[48,2,2048]{2,0,1:T(8,128)(2,1)S(1)} fusion(bf16[2,1536,2048]{2,1,0:T(8,128)(2,1)S(1)} %copy-done.2, bf16[48,2,1536]{2,1,0:T(2,128)(2,1)S(1)} %all_gather.3), kind=kOutput, calls=%fused_computation.13 | convolution fusion | flops 604176384 | bytes 13271040 | tf_op jit(solution)/shard_map/ned,edf->nef/dot_general | solution.py:119
  72.7 0.9 pad_maximum_fusion
  74.0 11.3 %fusion.2 = bf16[2,2048,1536]{2,1,0:T(8,128)(2,1)} fusion(bf16[2,2048,1536]{2,1,0:T(8,128)(2,1)} %param.30, f32[2,16,1536]{2,1,0:T(8,128)S(1)} %mul.128), kind=kLoop, calls=%fused_computation.5 | loop fusion | flops 18874368 | bytes 25362432 | tf_op jit(solution)/shard_map/convert_element_type | solution.py:21
  85.3 9.9 %all-reduce.4.cloned.1.call-done = bf16[48,2,4096]{2,0,1:T(8,128)(2,1)} async-done(((bf16[48,2,4096]{2,0,1:T(8,128)(2,1)}), bf16[48,2,4096]{2,0,1:T(8,128)(2,1)}) %all-reduce.4.cloned.1.call-update) | async-done | bytes 786448 | tf_op jit(solution)/shard_map/psum | solution.py:122
  95.3 1.4 convert_element_type.126
  96.6 6.8 %fusion.7 = bf16[48,2,1536]{2,0,1:T(8,128)(2,1)S(1)} fusion(bf16[2,2048,1536]{2,1,0:T(8,128)(2,1)} %fusion.2, f32[48,2,4096]{2,0,1:T(8,128)S(1)} %convert_element_type.126), kind=kOutput, calls=%fused_computation.14 | convolution fusion | flops 605306880 | bytes 14450688 | tf_op jit(solution)/shard_map/nef,efd->ned/dot_general | solution.py:127
  103.5 1.0 copy.80
  105.8 35.8 %all-reduce.6.cloned.1.call-done = bf16[48,2,1536]{2,1,0:T(2,128)(2,1)} async-done(((bf16[48,2,1536]{2,1,0:T(2,128)(2,1)}), bf16[48,2,1536]{2,1,0:T(2,128)(2,1)}) %all-reduce.6.cloned.1.call-update) | async-done | bytes 294928
  141.6 1.6 constant_dynamic-slice_fusion
  143.2 3.3 %all-to-all-start.2 = ((bf16[2,2,3,2,1536]{4,3,2,1,0:T(2,128)(2,1)}), bf16[2,2,3,2,1536]{4,3,2,1,0:T(2,128)(2,1)S(1)}, u32[]{:S(2)}, u32[]{:S(2)}) async-start(bf16[2,2,3,2,1536]{4,3,2,1,0:T(2,128)(2,1)} %bitcast.16), calls=%async_computation.2 | async-start | bytes 147456 | tf_op jit(solution)/shard_map/all_to_all | solution.py:136
  146.6 4.0 %all-to-all-done.2 = bf16[2,2,3,2,1536]{4,3,2,1,0:T(2,128)(2,1)S(1)} async-done(((bf16[2,2,3,2,1536]{4,3,2,1,0:T(2,128)(2,1)}), bf16[2,2,3,2,1536]{4,3,2,1,0:T(2,128)(2,1)S(1)}, u32[]{:S(2)}, u32[]{:S(2)}) %all-to-all-start.2) | async-done | bytes 73760 | tf_op jit(solution)/shard_map/all_to_all | solution.py:136
  150.7 3.8 %all_to_all.21 = bf16[2,2,3,2,1536]{4,3,2,0,1:T(2,128)(2,1)S(1)} all-to-all(bf16[2,2,3,2,1536]{4,3,2,0,1:T(2,128)(2,1)S(1)} %copy.81), channel_id=1, replica_groups=mesh['group'=2,'role'=2,'tp'=4,'sub'=2] {'sub'}, dimensions={1} | all-to-all | bytes 147456 | tf_op jit(solution)/shard_map/all_to_all | solution.py:135
  154.5 0.8 fusion.4
  (56 shorter events, 4.4 us)
Async XLA Ops:
  6.5 4.0 %copy-start = (bf16[4,128,1024]{2,1,0:T(8,128)(2,1)S(1)}, bf16[4,128,1024]{2,1,0:T(8,128)(2,1)}, u32[]{:S(2)}) copy-start(bf16[4,128,1024]{2,1,0:T(8,128)(2,1)} %param.20) | copy-start | bytes 3145732
  18.6 25.7 %all-to-all-start = ((bf16[2,2,3,2,1536]{4,3,2,1,0:T(2,128)(2,1)}), bf16[2,2,3,2,1536]{4,3,2,1,0:T(2,128)(2,1)S(1)}, u32[]{:S(2)}, u32[]{:S(2)}) async-start(bf16[2,2,3,2,1536]{4,3,2,1,0:T(2,128)(2,1)} %copy.74), calls=%async_computation | async-start | bytes 147456 | tf_op jit(solution)/shard_map/all_to_all | solution.py:109
  22.8 72.4 %all-reduce.4.cloned.1.call-start = ((), (), s32[]{:S(2)}) async-start(), calls=%async_computation.4 | async-start | bytes 1572864 | tf_op jit(solution)/shard_map/psum | solution.py:122
  24.8 13.4 %slice-start = ((s8[12582912]{0:T(1024)(128)(4,1)}), s8[4194304]{0:T(1024)(128)(4,1)S(1)}, s32[]{:S(2)}) async-start(s8[12582912]{0:T(1024)(128)(4,1)} %bitcast.83), calls=%async_computation.6 | async-start | bytes 8388608
  25.0 13.2 %slice-start.1 = ((s8[12582912]{0:T(1024)(128)(4,1)}), s8[4194304]{0:T(1024)(128)(4,1)S(1)}, s32[]{:S(2)}) async-start(s8[12582912]{0:T(1024)(128)(4,1)} %bitcast.83), calls=%async_computation.7 | async-start | bytes 8388608
  25.0 13.2 %slice-start.2 = ((s8[12582912]{0:T(1024)(128)(4,1)}), s8[4194304]{0:T(1024)(128)(4,1)S(1)}, s32[]{:S(2)}) async-start(s8[12582912]{0:T(1024)(128)(4,1)} %bitcast.83), calls=%async_computation.8 | async-start | bytes 8388608
  44.3 26.0 %copy-start.2 = (bf16[2,1536,2048]{2,1,0:T(8,128)(2,1)S(1)}, bf16[2,1536,2048]{2,1,0:T(8,128)(2,1)}, u32[]{:S(2)}) copy-start(bf16[2,1536,2048]{2,1,0:T(8,128)(2,1)} %fusion) | copy-start | bytes 37748740
  70.4 3.3 %copy-start.4 = (f32[2,16,12]{1,0,2:T(2,128)S(1)}, f32[2,16,12]{1,0,2:T(2,128)}, u32[]{:S(2)}) copy-start(f32[2,16,12]{1,0,2:T(2,128)} %param.31) | copy-start | bytes 4612
  73.7 67.9 %all-reduce.6.cloned.1.call-start = ((), (), s32[]{:S(2)}) async-start(), calls=%async_computation.5 | async-start | bytes 589824
  95.2 60.1 %copy-start.1 = (bf16[4,128,1024]{2,1,0:T(8,128)(2,1)S(1)}, bf16[4,128,1024]{2,1,0:T(8,128)(2,1)}, u32[]{:S(2)}) copy-start(bf16[4,128,1024]{2,1,0:T(8,128)(2,1)} %param.20) | copy-start | bytes 3145732
  96.6 7.9 %copy-start.5 = (u32[32]{0:T(128)S(1)}, u32[32]{0:T(128)}, u32[]{:S(2)}) copy-start(u32[32]{0:T(128)} %constant.34) | copy-start | bytes 388
  96.6 57.9 %copy-start.3 = (bf16[4,3072]{1,0:T(4,128)(2,1)S(1)}, bf16[4,3072]{1,0:T(4,128)(2,1)}, u32[]{:S(2)}) copy-start(bf16[4,3072]{1,0:T(4,128)(2,1)} %param.16) | copy-start | bytes 73732
  143.2 7.5 %all-to-all-start.2 = ((bf16[2,2,3,2,1536]{4,3,2,1,0:T(2,128)(2,1)}), bf16[2,2,3,2,1536]{4,3,2,1,0:T(2,128)(2,1)S(1)}, u32[]{:S(2)}, u32[]{:S(2)}) async-start(bf16[2,2,3,2,1536]{4,3,2,1,0:T(2,128)(2,1)} %bitcast.16), calls=%async_computation.2 | async-start | bytes 147456 | tf_op jit(solution)/shard_map/all_to_all | solution.py:136
Sparse Core Ops, SparseCore 0:
  73.8 21.4 all-reduce.3
  104.6 36.9 all-reduce.5
where the time goes:
time: 163 us; the launch traced here: 162 us
  waiting for transfers between devices  49.9 us (31%)
  other arithmetic  38.8 us (24%)
  blocking collectives  22.8 us (14%)
  matrix products  19.6 us (12%)
  between operations  14.3 us (9%)
  local copies, waits for them, and re-layouts  9.32 us (6%)
  starting transfers between devices  7.55 us (5%)
    unnamed x3, waiting for transfers between devices  35.9 us
    convert_element_type x3, other arithmetic, dequantize(): (blocked * widened[:, :, None, :]).reshape(experts, rows, columns)  30.6 us
    all_gather x1, blocking collectives, layer_rows(): row_piece = lax.all_gather(arrived, 'tp', axis=0, tiled=True)  14.8 us
    psum x1, waiting for transfers between devices, layer_rows(): lax.psum(partial_in.astype(jnp.bfloat16), 'sub').astype(jnp.float32)  9.94 us
    dot_general x1, matrix products, layer_rows(): jnp.einsum('ned,edf->nef', row_piece, w_gate, preferred_element_type=jnp....  6.87 us
    dot_general x1, matrix products, layer_rows(): jnp.einsum('nef,efd->ned', hidden, w_down, preferred_element_type=jnp.flo...  6.84 us
    all_to_all x1, blocking collectives, layer_rows(): lax.all_to_all(lax.all_to_all(outgoing, 'role', split_axis=0, concat_axis...  4.29 us
    all_to_all x1, starting transfers between devices, layer_rows(): lax.all_to_all(outgoing, 'role', split_axis=0, concat_axis=0, tiled=True)  4.2 us
  transfers between devices with their start and end apart: 4, of which 3 were waited for; matrix products, arithmetic and copies ran while one was open for 21% of the time, Pallas kernels for 0%

commit v1 on v0

v1 whole, which is shorter than its diff:
```python
import functools
import math

import jax
import jax.numpy as jnp
from jax import lax
from jax.experimental import pallas as pl
from jax.experimental.pallas import tpu as pltpu
from jax.sharding import PartitionSpec as P

D = 3072
HEADS = 24
KV_HEADS = 8
HEAD_DIM = 128
EXPERTS = 4
QBLOCK = 128
LANES = 128
GROUP = HEADS // KV_HEADS
SLOT = 16
VMEM_LIMIT = 16 << 20
COST = 48 << 20

VMEM = pl.BlockSpec(memory_space=pltpu.VMEM)
SMEM = pl.BlockSpec(memory_space=pltpu.SMEM)


def attend_kernel(
    residual_ref,
    query_ref,
    new_key_ref,
    new_value_ref,
    cache_key_ref,
    cache_value_ref,
    lengths_ref,
    gain_ref,
    ids_ref,
    levels_ref,
    own_ref,
    other_ref,
    stream_ref,
    q_scr,
    nk_scr,
    nv_scr,
    att_scr,
):
    rows, positions, _ = cache_key_ref.shape
    half = D // 2
    f32 = jnp.float32
    total = KV_HEADS * SLOT
    zeros = jnp.zeros((total, HEAD_DIM), f32)
    q_scr[...] = zeros
    nk_scr[...] = zeros
    nv_scr[...] = zeros
    for j in range(KV_HEADS):
        kv_cols = slice(j * HEAD_DIM, (j + 1) * HEAD_DIM)
        fresh_key = new_key_ref[:, kv_cols].astype(f32)
        fresh_value = new_value_ref[:, kv_cols].astype(f32)
        for g in range(GROUP):
            h = j * GROUP + g
            at = slice(j * SLOT + g * rows, j * SLOT + (g + 1) * rows)
            q_scr[at, :] = query_ref[:, h * HEAD_DIM : (h + 1) * HEAD_DIM].astype(f32)
            nk_scr[at, :] = fresh_key
            nv_scr[at, :] = fresh_value
    queries = q_scr[...]
    factor = 1.0 / math.sqrt(HEAD_DIM)
    fresh_score = jnp.sum(queries * nk_scr[...], axis=1, keepdims=True) * factor
    queries_bf = queries.astype(jnp.bfloat16)
    keys = cache_key_ref[...].reshape(rows * positions, KV_HEADS * HEAD_DIM)
    values = cache_value_ref[...].reshape(rows * positions, KV_HEADS * HEAD_DIM)
    scores = jnp.concatenate(
        [
            lax.dot_general(
                queries_bf[j * SLOT : (j + 1) * SLOT],
                keys[:, j * HEAD_DIM : (j + 1) * HEAD_DIM],
                (((1,), (1,)), ((), ())),
                preferred_element_type=f32,
            )
            for j in range(KV_HEADS)
        ],
        axis=0,
    )
    row_of = lax.broadcasted_iota(jnp.int32, (total, positions), 0) % rows
    position = lax.broadcasted_iota(jnp.int32, (total, positions), 1)
    valid = [
        jnp.logical_and(row_of == r, position < lengths_ref[r]) for r in range(rows)
    ]
    pieces = [
        jnp.where(valid[r], scores[:, r * positions : (r + 1) * positions] * factor, -1e30)
        for r in range(rows)
    ]
    peak = functools.reduce(jnp.maximum, pieces)
    peak = jnp.maximum(jnp.max(peak, axis=1, keepdims=True), fresh_score)
    exps = [jnp.where(valid[r], jnp.exp(pieces[r] - peak), 0.0) for r in range(rows)]
    fresh_exp = jnp.exp(fresh_score - peak)
    denominator = jnp.sum(sum(exps[1:], exps[0]), axis=1, keepdims=True) + fresh_exp
    inverse = 1.0 / denominator
    probabilities = jnp.concatenate([(e * inverse).astype(jnp.bfloat16) for e in exps], axis=1)
    fresh_prob = (fresh_exp * inverse).astype(jnp.bfloat16).astype(f32)
    attended = jnp.concatenate(
        [
            jnp.dot(
                probabilities[j * SLOT : (j + 1) * SLOT],
                values[:, j * HEAD_DIM : (j + 1) * HEAD_DIM],
                preferred_element_type=f32,
            )
            for j in range(KV_HEADS)
        ],
        axis=0,
    )
    att_scr[...] = attended + fresh_prob * nv_scr[...]
    squares = jnp.zeros((rows, HEAD_DIM), f32)
    for j in range(KV_HEADS):
        for g in range(GROUP):
            h = j * GROUP + g
            cols = slice(h * HEAD_DIM, (h + 1) * HEAD_DIM)
            at = slice(j * SLOT + g * rows, j * SLOT + (g + 1) * rows)
            piece = residual_ref[:, cols].astype(f32) + att_scr[at, :]
            stream_ref[:, cols] = piece
            squares = squares + piece * piece
    mean_square = jnp.sum(squares, axis=1, keepdims=True) * (1.0 / D)
    normed = stream_ref[...] * lax.rsqrt(mean_square + 1e-05) * gain_ref[...]
    first = lax.axis_index("sub") == 0
    low, high = normed[:, :half], normed[:, half:]
    lane = lax.broadcasted_iota(jnp.int32, (rows, LANES), 1)
    levels = levels_ref[...].astype(f32)
    ids = ids_ref[...]
    table = jnp.where(lane == ids[:, 0:1], levels[:, 0:1], 0.0) + jnp.where(
        lane == ids[:, 1:2], levels[:, 1:2], 0.0
    )
    own = jnp.concatenate([jnp.where(first, low, high), table], axis=1)
    other = jnp.concatenate([jnp.where(first, high, low), table], axis=1)
    for ref, value in ((own_ref, own), (other_ref, other)):
        ref[...] = jnp.concatenate(
            [jnp.where(first, value, 0.0), jnp.where(first, 0.0, value)], axis=0
        ).astype(jnp.bfloat16)


def scaled_product(left, weights_ref, scales_ref, expert, column, width):
    depth = weights_ref.shape[1]
    total = None
    for k in range(depth // QBLOCK):
        product = jnp.dot(
            left[:, k * QBLOCK : (k + 1) * QBLOCK],
            weights_ref[expert, k * QBLOCK : (k + 1) * QBLOCK, column : column + width],
            preferred_element_type=jnp.float32,
        )
        product = jnp.concatenate(
            [
                product[:, i * QBLOCK : (i + 1) * QBLOCK]
                * scales_ref[expert, k, column // QBLOCK + i]
                for i in range(width // QBLOCK)
            ],
            axis=1,
        )
        total = product if total is None else total + product
    return total


def gate_up_kernel(x_ref, gate_ref, up_ref, gate_s_ref, up_s_ref, out_ref, *, expert):
    _, depth, units = gate_ref.shape
    rows = x_ref.shape[0]
    block = min(rows, 64)
    width = 256
    for m in range(rows // block):
        at = slice(m * block, (m + 1) * block)
        left = x_ref[at, :depth]
        for column in range(0, units, width):
            out_ref[at, column : column + width] = scaled_product(
                left, gate_ref, gate_s_ref, expert, column, width
            ).astype(jnp.bfloat16)
            out_ref[at, units + column : units + column + width] = scaled_product(
                left, up_ref, up_s_ref, expert, column, width
            ).astype(jnp.bfloat16)


def down_kernel(x_ref, *refs, experts):
    parts = refs[: 2 * experts]
    down_ref, down_s_ref, out_ref = refs[2 * experts :]
    _, units, columns = down_ref.shape
    rows, extended = x_ref.shape
    block = min(rows, 64)
    width = 256
    f32 = jnp.float32
    base = lax.axis_index("role") * experts
    for m in range(rows // block):
        at = slice(m * block, (m + 1) * block)
        levels = x_ref[at, extended - LANES :].astype(f32)
        lane = lax.broadcasted_iota(jnp.int32, levels.shape, 1)
        shares = levels / jnp.sum(levels, axis=1, keepdims=True)
        hidden = []
        for e in range(experts):
            share = jnp.sum(jnp.where(lane == base + e, shares, 0.0), axis=1, keepdims=True)
            mine, theirs = parts[2 * e], parts[2 * e + 1]
            chunks = []
            for u in range(0, units, width):
                gate = mine[at, u : u + width].astype(f32) + theirs[at, u : u + width].astype(f32)
                v = slice(units + u, units + u + width)
                up = mine[at, v].astype(f32) + theirs[at, v].astype(f32)
                silu = gate / (1.0 + jnp.exp(-gate))
                chunks.append((silu * up * share).astype(jnp.bfloat16))
            hidden.append(jnp.concatenate(chunks, axis=1))
        for column in range(0, columns, width):
            total = None
            for e in range(experts):
                product = scaled_product(hidden[e], down_ref, down_s_ref, e, column, width)
                total = product if total is None else total + product
            out_ref[at, column : column + width] = total.astype(jnp.bfloat16)


def finish_kernel(stream_ref, own_ref, other_ref, out_ref):
    half = D // 2
    rows = stream_ref.shape[0]
    first = lax.axis_index("sub") == 0
    own, other = (
        jnp.where(first, pair[:rows], pair[rows:])
        for pair in (own_ref[...].astype(jnp.float32), other_ref[...].astype(jnp.float32))
    )
    out_ref[:, :half] = (stream_ref[:, :half] + jnp.where(first, own, other)).astype(jnp.bfloat16)
    out_ref[:, half:] = (stream_ref[:, half:] + jnp.where(first, other, own)).astype(jnp.bfloat16)


def swap(x, axis, bit):
    count = lax.axis_size(axis)
    return lax.ppermute(x, axis, [(i, i ^ bit) for i in range(count)])


def bits(axis):
    return [1 << b for b in range(lax.axis_size(axis).bit_length() - 1)]


def add_bf16(a, b):
    return (a.astype(jnp.float32) + b.astype(jnp.float32)).astype(jnp.bfloat16)


def per_device(
    residual,
    query,
    new_key,
    new_value,
    cache_key,
    cache_value,
    lengths,
    norm_gain,
    expert_ids,
    gate_levels,
    gate_codes,
    gate_scales,
    up_codes,
    up_scales,
    down_codes,
    down_scales,
):
    rows = residual.shape[0]
    half = D // 2
    extended = half + LANES
    params = pltpu.CompilerParams(vmem_limit_bytes=VMEM_LIMIT)
    cost = pl.CostEstimate(flops=0, bytes_accessed=COST, transcendentals=0)
    stacked = pltpu.VMEM((KV_HEADS * SLOT, HEAD_DIM), jnp.float32)
    own, other, stream = pl.pallas_call(
        attend_kernel,
        out_shape=(
            jax.ShapeDtypeStruct((2 * rows, extended), jnp.bfloat16),
            jax.ShapeDtypeStruct((2 * rows, extended), jnp.bfloat16),
            jax.ShapeDtypeStruct((rows, D), jnp.float32),
        ),
        in_specs=[VMEM] * 6 + [SMEM] + [VMEM] * 3,
        out_specs=(VMEM, VMEM, VMEM),
        scratch_shapes=[stacked] * 4,
        compiler_params=params,
        cost_estimate=cost,
        name="attend",
    )(
        residual,
        query,
        new_key,
        new_value,
        cache_key,
        cache_value,
        lengths,
        norm_gain.reshape(1, D),
        expert_ids,
        gate_levels,
    )
    gathered = own + swap(other, "sub", 1)
    steps = [("tp", bit) for bit in bits("tp")] + [("role", bit) for bit in bits("role")]
    for axis, bit in steps:
        gathered = jnp.concatenate([gathered, swap(gathered, axis, bit)], axis=0)
    total_rows = gathered.shape[0]
    experts, _, units = gate_codes.shape
    parts = []
    for e in range(experts):
        part = pl.pallas_call(
            functools.partial(gate_up_kernel, expert=e),
            out_shape=jax.ShapeDtypeStruct((total_rows, 2 * units), jnp.bfloat16),
            in_specs=[VMEM] * 3 + [SMEM] * 2,
            out_specs=VMEM,
            compiler_params=params,
            name="gate_up",
        )(gathered, gate_codes, up_codes, gate_scales, up_scales)
        parts += [part, swap(part, "sub", 1)]
    carried = pl.pallas_call(
        functools.partial(down_kernel, experts=experts),
        out_shape=jax.ShapeDtypeStruct((total_rows, half), jnp.bfloat16),
        in_specs=[VMEM] * (2 + 2 * experts) + [SMEM],
        out_specs=VMEM,
        compiler_params=params,
        name="down",
    )(gathered, *parts, down_codes, down_scales)
    for axis, bit in reversed(steps):
        kept = carried.shape[0] // 2
        carried = add_bf16(carried[:kept], swap(carried[kept:], axis, bit))
    return pl.pallas_call(
        finish_kernel,
        out_shape=jax.ShapeDtypeStruct((rows, D), jnp.bfloat16),
        in_specs=[VMEM] * 3,
        out_specs=VMEM,
        compiler_params=params,
        name="finish",
    )(stream, carried, swap(carried, "sub", 1))


def solution(mesh):
    row = ("group", "role", "tp", "sub")
    in_specs = (
        P(row, None),
        P(row, None),
        P(row, None),
        P(row, None),
        P(row, None, None),
        P(row, None, None),
        P(row),
        P(),
        P(row, None),
        P(row, None),
        P("role", "sub", "tp"),
        P("role", "sub", "tp"),
        P("role", "sub", "tp"),
        P("role", "sub", "tp"),
        P("role", "tp", "sub"),
        P("role", "tp", "sub"),
    )
    return jax.shard_map(
        per_device, mesh=mesh, in_specs=in_specs, out_specs=P(row, None), check_vma=False
    )
```

time: 163 us -> 68.3 us (0.42)
  other arithmetic: 38.8 us -> 0.1 us
  waiting for transfers between devices: 49.9 us -> 17.6 us
  blocking collectives: 22.8 us -> 0 us
  matrix products: 19.6 us -> 0 us
  local copies, waits for them, and re-layouts: 9.32 us -> 23.5 us
  between operations: 14.3 us -> 0.13 us
  Pallas kernels: 0 us -> 10.9 us
  starting transfers between devices: 7.55 us -> 15.4 us
    unnamed x3 -> x0, waiting for transfers between devices: 35.9 us -> none
    convert_element_type x8 -> x3, other arithmetic: 33.6 us -> 0.05 us  [add_bf16(): return (a.astype(jnp.float32) + b.astype(jnp.float32)).astype(jnp.bfloat16)]
    unnamed x23 -> x29, local copies, waits for them, and re-layouts: 3.15 us -> 23.4 us
    dot_general x8 -> x0, matrix products: 19.6 us -> none  [the longest x1 6.87 us: layer_rows(): jnp.einsum('ned,edf->nef', row_piece, w_gate, preferred_element_type=jnp....]
    ppermute x0 -> x10, waiting for transfers between devices: none -> 17.6 us  [swap(): return lax.ppermute(x, axis, [(i, i ^ bit) for i in range(count)])]
    ppermute x0 -> x10, starting transfers between devices: none -> 15.4 us  [swap(): return lax.ppermute(x, axis, [(i, i ^ bit) for i in range(count)])]
    all_gather x1 -> x0, blocking collectives: 14.8 us -> none  [layer_rows(): row_piece = lax.all_gather(arrived, 'tp', axis=0, tiled=True)]
    pallas_call x0 -> x5, Pallas kernels: none -> 10.9 us  [the longest x2 5.89 us: per_device(): pl.pallas_call(functools.partial(gate_up_kernel, expert=e), out_shape=jax...]
  transfers between devices with their start and end apart: 4 -> 10, of which waited for: 3 -> 10; matrix products, arithmetic and copies ran while one was open for 21% -> 2% of each run, Pallas kernels for 0% -> 0%
where the time goes in v1:
time: 68.3 us; the launch traced here: 67.6 us
  local copies, waits for them, and re-layouts  23.5 us (34%)
  waiting for transfers between devices  17.6 us (26%)
  starting transfers between devices  15.4 us (23%)
  Pallas kernels  10.9 us (16%)
    unnamed x29, local copies, waits for them, and re-layouts  23.4 us
    ppermute x10, waiting for transfers between devices, swap(): return lax.ppermute(x, axis, [(i, i ^ bit) for i in range(count)])  17.6 us
    ppermute x10, starting transfers between devices, swap(): return lax.ppermute(x, axis, [(i, i ^ bit) for i in range(count)])  15.4 us
    pallas_call x2, Pallas kernels, per_device(): pl.pallas_call(functools.partial(gate_up_kernel, expert=e), out_shape=jax...  5.89 us
    pallas_call x1, Pallas kernels, per_device(): pl.pallas_call(functools.partial(down_kernel, experts=experts), out_shape...  3 us
    pallas_call x1, Pallas kernels, per_device(): pl.pallas_call(attend_kernel, out_shape=(jax.ShapeDtypeStruct((2 * rows,...  1.37 us
  transfers between devices with their start and end apart: 10, of which 10 were waited for; matrix products, arithmetic and copies ran while one was open for 2% of the time, Pallas kernels for 0%

profile of v1, /device:TPU:0, one launch (start us, length us, event | category | flops | bytes accessed | tf_op | source)
XLA Modules:
  0.0 67.6 jit_solution(12564141678392053389)
XLA Ops:
  0.0 0.8 %copy.17.ids_ref = s32[4,2]{1,0:T(4,128)S(1)} copy(s32[4,2]{0,1:T(2,128)} %param.24) | data formatting | bytes 64 | tf_op args[8]
  0.8 0.8 %copy.18.levels_ref = s32[4,2]{1,0:T(4,128)S(1)} copy(s32[4,2]{0,1:T(2,128)} %param.25) | data formatting | bytes 64 | tf_op args[9]
  1.5 1.2 %copy-done.3 = bf16[4,128,1024]{2,1,0:T(8,128)(2,1)S(1)} copy-done((bf16[4,128,1024]{2,1,0:T(8,128)(2,1)S(1)}, bf16[4,128,1024]{2,1,0:T(8,128)(2,1)}, u32[]{:S(2)}) %copy-start.3) | copy-done | bytes 1048600
  2.8 1.2 %copy-done.4 = bf16[4,128,1024]{2,1,0:T(8,128)(2,1)S(1)} copy-done((bf16[4,128,1024]{2,1,0:T(8,128)(2,1)S(1)}, bf16[4,128,1024]{2,1,0:T(8,128)(2,1)}, u32[]{:S(2)}) %copy-start.4) | copy-done | bytes 1048600
  4.0 0.7 %copy-done.5 = bf16[4,3072]{1,0:T(4,128)(2,1)S(1)} copy-done((bf16[4,3072]{1,0:T(4,128)(2,1)S(1)}, bf16[4,3072]{1,0:T(4,128)(2,1)}, u32[]{:S(2)}) %copy-start.5) | copy-done | bytes 24600
  4.7 0.7 %copy-done.6 = bf16[4,3072]{1,0:T(4,128)(2,1)S(1)} copy-done((bf16[4,3072]{1,0:T(4,128)(2,1)S(1)}, bf16[4,3072]{1,0:T(4,128)(2,1)}, u32[]{:S(2)}) %copy-start.6) | copy-done | bytes 24600
  5.5 0.7 %copy-done.7 = f32[3072]{0:T(1024)S(1)} copy-done((f32[3072]{0:T(1024)S(1)}, f32[3072]{0:T(1024)}, u32[]{:S(2)}) %copy-start.7) | copy-done | bytes 12312
  8.2 1.4 %attend.1 = (bf16[8,1664]{1,0:T(8,128)(2,1)S(1)}, bf16[8,1664]{1,0:T(8,128)(2,1)S(1)}, f32[4,3072]{1,0:T(4,128)S(1)}) custom-call(bf16[4,3072]{1,0:T(4,128)(2,1)S(1)} %copy-done.5, bf16[4,3072]{1,0:T(4,128)(2,1)S(1)} %copy-done.6, bf16[4,1024]{1,0:T(4,128)(2,1)S(1)} %copy-done.8, bf16[4,1024]{1,0:T(4,128)(2,1)S(1)} %copy-done.9, ...), custom_call_target="tpu_custom_call" | custom-call | bytes 50331648 | tf_op jit(solution)/shard_map/attend/pallas_call | solution.py:259
  10.1 0.9 %collective-permute-done = bf16[8,1664]{1,0:T(8,128)(2,1)S(1)} collective-permute-done((bf16[8,1664]{1,0:T(8,128)(2,1)S(1)}, bf16[8,1664]{1,0:T(8,128)(2,1)S(1)}, u32[]{:S(2)}, u32[]{:S(2)}) %collective-permute-start) | collective-permute-done | bytes 26656 | tf_op jit(solution)/shard_map/ppermute | solution.py:224
  11.0 3.0 %collective-permute-start.1 = (bf16[8,1664]{1,0:T(8,128)(2,1)S(1)}, bf16[8,1664]{1,0:T(8,128)(2,1)S(1)}, u32[]{:S(2)}, u32[]{:S(2)}) collective-permute-start(bf16[8,1664]{1,0:T(8,128)(2,1)S(1)} %add.12), channel_id=1, source_target_pairs={{0,2},{2,0},{4,6},{6,4},{1,3},{3,1},{5,7},{7,5},{8,10},{10,8},{12,... | collective-permute-start | bytes 79880 | tf_op jit(solution)/shard_map/ppermute | solution.py:224
  14.0 1.8 %collective-permute-done.1 = bf16[8,1664]{1,0:T(8,128)(2,1)S(1)} collective-permute-done((bf16[8,1664]{1,0:T(8,128)(2,1)S(1)}, bf16[8,1664]{1,0:T(8,128)(2,1)S(1)}, u32[]{:S(2)}, u32[]{:S(2)}) %collective-permute-start.1) | collective-permute-done | bytes 26656 | tf_op jit(solution)/shard_map/ppermute | solution.py:224
  15.8 3.0 %collective-permute-start.2 = (bf16[16,1664]{1,0:T(8,128)(2,1)S(1)}, bf16[16,1664]{1,0:T(8,128)(2,1)S(1)}, u32[]{:S(2)}, u32[]{:S(2)}) collective-permute-start(bf16[16,1664]{1,0:T(8,128)(2,1)S(1)} %pad_maximum_fusion.2), channel_id=1, source_target_pairs={{0,4},{2,6},{4,0},{6,2},{1,5},{3,7},{5,1},{7,3},{8,12},{10,14},{12... | collective-permute-start | bytes 159752 | tf_op jit(solution)/shard_map/ppermute | solution.py:224
  18.8 2.1 %collective-permute-done.2 = bf16[16,1664]{1,0:T(8,128)(2,1)S(1)} collective-permute-done((bf16[16,1664]{1,0:T(8,128)(2,1)S(1)}, bf16[16,1664]{1,0:T(8,128)(2,1)S(1)}, u32[]{:S(2)}, u32[]{:S(2)}) %collective-permute-start.2) | collective-permute-done | bytes 53280 | tf_op jit(solution)/shard_map/ppermute | solution.py:224
  21.0 1.9 %collective-permute-start.3 = (bf16[32,1664]{1,0:T(8,128)(2,1)S(1)}, bf16[32,1664]{1,0:T(8,128)(2,1)S(1)}, u32[]{:S(2)}, u32[]{:S(2)}) collective-permute-start(bf16[32,1664]{1,0:T(8,128)(2,1)S(1)} %pad_maximum_fusion.1), channel_id=1, source_target_pairs={{0,8},{8,0},{1,9},{9,1},{2,10},{10,2},{3,11},{11,3},{4,12},{12,4},... | collective-permute-start | bytes 319496 | tf_op jit(solution)/shard_map/ppermute | solution.py:224
  22.8 0.7 %copy.19.gate_s_ref = f32[2,12,16]{2,1,0:T(8,128)S(1)} copy(f32[2,12,16]{2,0,1:T(2,128)} %param.27) | data formatting | bytes 3072 | tf_op args[11]
  23.6 0.7 %copy.20.up_s_ref = f32[2,12,16]{2,1,0:T(8,128)S(1)} copy(f32[2,12,16]{2,0,1:T(2,128)} %param.29) | data formatting | bytes 3072 | tf_op args[13]
  24.3 1.5 %collective-permute-done.3 = bf16[32,1664]{1,0:T(8,128)(2,1)S(1)} collective-permute-done((bf16[32,1664]{1,0:T(8,128)(2,1)S(1)}, bf16[32,1664]{1,0:T(8,128)(2,1)S(1)}, u32[]{:S(2)}, u32[]{:S(2)}) %collective-permute-start.3) | collective-permute-done | bytes 106528 | tf_op jit(solution)/shard_map/ppermute | solution.py:224
  25.8 4.6 %copy-done = bf16[2,1536,2048]{2,1,0:T(8,128)(2,1)S(1)} copy-done((bf16[2,1536,2048]{2,1,0:T(8,128)(2,1)S(1)}, bf16[2,1536,2048]{2,1,0:T(8,128)(2,1)}, u32[]{:S(2)}) %copy-start) | copy-done | bytes 12582936
  30.3 4.6 %copy-done.1 = bf16[2,1536,2048]{2,1,0:T(8,128)(2,1)S(1)} copy-done((bf16[2,1536,2048]{2,1,0:T(8,128)(2,1)S(1)}, bf16[2,1536,2048]{2,1,0:T(8,128)(2,1)}, u32[]{:S(2)}) %copy-start.1) | copy-done | bytes 12582936
  34.9 2.9 %gate_up.3.refs_2_ = bf16[64,4096]{1,0:T(8,128)(2,1)S(1)} custom-call(bf16[64,1664]{1,0:T(8,128)(2,1)S(1)} %pad_maximum_fusion.x_ref, bf16[2,1536,2048]{2,1,0:T(8,128)(2,1)S(1)} %copy-done, bf16[2,1536,2048]{2,1,0:T(8,128)(2,1)S(1)} %copy-done.1, f32[2,12,16]{2,1,0:T(8,128)S(1)} %copy.19.gate_s_ref, f32[2,12,16]{2,1,0:T(8,128)S(1)} %copy.20.up_s_ref), custom_call_target="tpu_custom_call" | custom-call | tf_op jit(solution)/shard_map/gate_up/pallas_call | solution.py:292
  37.9 2.9 %gate_up.2.refs_0_ = bf16[64,4096]{1,0:T(8,128)(2,1)S(1)} custom-call(bf16[64,1664]{1,0:T(8,128)(2,1)S(1)} %pad_maximum_fusion.x_ref, bf16[2,1536,2048]{2,1,0:T(8,128)(2,1)S(1)} %copy-done, bf16[2,1536,2048]{2,1,0:T(8,128)(2,1)S(1)} %copy-done.1, f32[2,12,16]{2,1,0:T(8,128)S(1)} %copy.19.gate_s_ref, f32[2,12,16]{2,1,0:T(8,128)S(1)} %copy.20.up_s_ref), custom_call_target="tpu_custom_call" | custom-call | tf_op jit(solution)/shard_map/gate_up/pallas_call | solution.py:292
  41.5 1.3 %collective-permute-done.4.refs_1_ = bf16[64,4096]{1,0:T(8,128)(2,1)S(1)} collective-permute-done((bf16[64,4096]{1,0:T(8,128)(2,1)S(1)}, bf16[64,4096]{1,0:T(8,128)(2,1)S(1)}, u32[]{:S(2)}, u32[]{:S(2)}) %collective-permute-start.4) | collective-permute-done | bytes 524320 | tf_op jit(solution)/shard_map/ppermute | solution.py:224
  42.8 0.7 %collective-permute-done.5.refs_3_ = bf16[64,4096]{1,0:T(8,128)(2,1)S(1)} collective-permute-done((bf16[64,4096]{1,0:T(8,128)(2,1)S(1)}, bf16[64,4096]{1,0:T(8,128)(2,1)S(1)}, u32[]{:S(2)}, u32[]{:S(2)}) %collective-permute-start.5) | collective-permute-done | bytes 524320 | tf_op jit(solution)/shard_map/ppermute | solution.py:224
  43.5 4.6 %copy-done.2 = bf16[2,2048,1536]{2,1,0:T(8,128)(2,1)S(1)} copy-done((bf16[2,2048,1536]{2,1,0:T(8,128)(2,1)S(1)}, bf16[2,2048,1536]{2,1,0:T(8,128)(2,1)}, u32[]{:S(2)}) %copy-start.2) | copy-done | bytes 12582936
  48.1 3.0 %down.1 = bf16[64,1536]{1,0:T(8,128)(2,1)S(1)} custom-call(bf16[64,1664]{1,0:T(8,128)(2,1)S(1)} %pad_maximum_fusion.x_ref, bf16[64,4096]{1,0:T(8,128)(2,1)S(1)} %gate_up.2.refs_0_, bf16[64,4096]{1,0:T(8,128)(2,1)S(1)} %collective-permute-done.4.refs_1_, bf16[64,4096]{1,0:T(8,128)(2,1)S(1)} %gate_up.3.refs_2_, ...), custom_call_target="tpu_custom_call" | custom-call | tf_op jit(solution)/shard_map/down/pallas_call | solution.py:301
  51.1 1.9 %collective-permute-start.6 = (bf16[32,1536]{1,0:T(8,128)(2,1)S(1)}, bf16[32,1536]{1,0:T(8,128)(2,1)S(1)}, u32[]{:S(2)}, u32[]{:S(2)}) collective-permute-start(bf16[32,1536]{1,0:T(8,128)(2,1)S(1)} %slice.25), channel_id=1, source_target_pairs={{0,8},{8,0},{1,9},{9,1},{2,10},{10,2},{3,11},{11,3},{4,12},{12,4},... | collective-permute-start | bytes 294920 | tf_op jit(solution)/shard_map/ppermute | solution.py:224
  53.0 3.1 %collective-permute-done.6 = bf16[32,1536]{1,0:T(8,128)(2,1)S(1)} collective-permute-done((bf16[32,1536]{1,0:T(8,128)(2,1)S(1)}, bf16[32,1536]{1,0:T(8,128)(2,1)S(1)}, u32[]{:S(2)}, u32[]{:S(2)}) %collective-permute-start.6) | collective-permute-done | bytes 98336 | tf_op jit(solution)/shard_map/ppermute | solution.py:224
  56.2 3.0 %collective-permute-start.7 = (bf16[16,1536]{1,0:T(8,128)(2,1)S(1)}, bf16[16,1536]{1,0:T(8,128)(2,1)S(1)}, u32[]{:S(2)}, u32[]{:S(2)}) collective-permute-start(bf16[16,1536]{1,0:T(8,128)(2,1)S(1)} %slice.27), channel_id=1, source_target_pairs={{0,4},{2,6},{4,0},{6,2},{1,5},{3,7},{5,1},{7,3},{8,12},{10,14},{12... | collective-permute-start | bytes 147464 | tf_op jit(solution)/shard_map/ppermute | solution.py:224
  59.1 2.6 %collective-permute-done.7 = bf16[16,1536]{1,0:T(8,128)(2,1)S(1)} collective-permute-done((bf16[16,1536]{1,0:T(8,128)(2,1)S(1)}, bf16[16,1536]{1,0:T(8,128)(2,1)S(1)}, u32[]{:S(2)}, u32[]{:S(2)}) %collective-permute-start.7) | collective-permute-done | bytes 49184 | tf_op jit(solution)/shard_map/ppermute | solution.py:224
  61.8 1.5 %collective-permute-start.8 = (bf16[8,1536]{1,0:T(8,128)(2,1)S(1)}, bf16[8,1536]{1,0:T(8,128)(2,1)S(1)}, u32[]{:S(2)}, u32[]{:S(2)}) collective-permute-start(bf16[8,1536]{1,0:T(8,128)(2,1)S(1)} %slice.29), channel_id=1, source_target_pairs={{0,2},{2,0},{4,6},{6,4},{1,3},{3,1},{5,7},{7,5},{8,10},{10,8},{12,... | collective-permute-start | bytes 73736 | tf_op jit(solution)/shard_map/ppermute | solution.py:224
  63.3 2.4 %collective-permute-done.8 = bf16[8,1536]{1,0:T(8,128)(2,1)S(1)} collective-permute-done((bf16[8,1536]{1,0:T(8,128)(2,1)S(1)}, bf16[8,1536]{1,0:T(8,128)(2,1)S(1)}, u32[]{:S(2)}, u32[]{:S(2)}) %collective-permute-start.8) | collective-permute-done | bytes 24608 | tf_op jit(solution)/shard_map/ppermute | solution.py:224
  65.8 1.2 %collective-permute-done.9.other_ref = bf16[8,1536]{1,0:T(8,128)(2,1)S(1)} collective-permute-done((bf16[8,1536]{1,0:T(8,128)(2,1)S(1)}, bf16[8,1536]{1,0:T(8,128)(2,1)S(1)}, u32[]{:S(2)}, u32[]{:S(2)}) %collective-permute-start.9) | collective-permute-done | bytes 24608 | tf_op jit(solution)/shard_map/ppermute | solution.py:224
  (32 shorter events, 4.1 us)
Async XLA Ops:
  1.5 1.2 %copy-start.3 = (bf16[4,128,1024]{2,1,0:T(8,128)(2,1)S(1)}, bf16[4,128,1024]{2,1,0:T(8,128)(2,1)}, u32[]{:S(2)}) copy-start(bf16[4,128,1024]{2,1,0:T(8,128)(2,1)} %cache_key_ref.1) | copy-start | bytes 3145732
  2.8 1.2 %copy-start.4 = (bf16[4,128,1024]{2,1,0:T(8,128)(2,1)S(1)}, bf16[4,128,1024]{2,1,0:T(8,128)(2,1)}, u32[]{:S(2)}) copy-start(bf16[4,128,1024]{2,1,0:T(8,128)(2,1)} %cache_value_ref.1) | copy-start | bytes 3145732
  4.0 0.7 %copy-start.5 = (bf16[4,3072]{1,0:T(4,128)(2,1)S(1)}, bf16[4,3072]{1,0:T(4,128)(2,1)}, u32[]{:S(2)}) copy-start(bf16[4,3072]{1,0:T(4,128)(2,1)} %residual_ref.1) | copy-start | bytes 73732
  4.7 0.7 %copy-start.6 = (bf16[4,3072]{1,0:T(4,128)(2,1)S(1)}, bf16[4,3072]{1,0:T(4,128)(2,1)}, u32[]{:S(2)}) copy-start(bf16[4,3072]{1,0:T(4,128)(2,1)} %query_ref.1) | copy-start | bytes 73732
  5.5 0.7 %copy-start.7 = (f32[3072]{0:T(1024)S(1)}, f32[3072]{0:T(1024)}, u32[]{:S(2)}) copy-start(f32[3072]{0:T(1024)} %param.23) | copy-start | bytes 36868
  6.2 0.7 %copy-start.8 = (bf16[4,1024]{1,0:T(4,128)(2,1)S(1)}, bf16[4,1024]{1,0:T(4,128)(2,1)}, u32[]{:S(2)}) copy-start(bf16[4,1024]{1,0:T(4,128)(2,1)} %new_key_ref.1) | copy-start | bytes 24580
  6.9 0.7 %copy-start.9 = (bf16[4,1024]{1,0:T(4,128)(2,1)S(1)}, bf16[4,1024]{1,0:T(4,128)(2,1)}, u32[]{:S(2)}) copy-start(bf16[4,1024]{1,0:T(4,128)(2,1)} %new_value_ref.1) | copy-start | bytes 24580
  7.6 0.7 copy-start.10
  9.6 1.4 %collective-permute-start = (bf16[8,1664]{1,0:T(8,128)(2,1)S(1)}, bf16[8,1664]{1,0:T(8,128)(2,1)S(1)}, u32[]{:S(2)}, u32[]{:S(2)}) collective-permute-start(bf16[8,1664]{1,0:T(8,128)(2,1)S(1)} %get-tuple-element.10), channel_id=1, source_target_pairs={{0,1},{1,0},{2,3},{3,2},{4,5},{5,4},{6,7},{7,6},{8,9},{9,8},{10,11... | collective-permute-start | bytes 79880 | tf_op jit(solution)/shard_map/ppermute | solution.py:224
  11.0 4.8 %collective-permute-start.1 = (bf16[8,1664]{1,0:T(8,128)(2,1)S(1)}, bf16[8,1664]{1,0:T(8,128)(2,1)S(1)}, u32[]{:S(2)}, u32[]{:S(2)}) collective-permute-start(bf16[8,1664]{1,0:T(8,128)(2,1)S(1)} %add.12), channel_id=1, source_target_pairs={{0,2},{2,0},{4,6},{6,4},{1,3},{3,1},{5,7},{7,5},{8,10},{10,8},{12,... | collective-permute-start | bytes 79880 | tf_op jit(solution)/shard_map/ppermute | solution.py:224
  15.8 5.1 %collective-permute-start.2 = (bf16[16,1664]{1,0:T(8,128)(2,1)S(1)}, bf16[16,1664]{1,0:T(8,128)(2,1)S(1)}, u32[]{:S(2)}, u32[]{:S(2)}) collective-permute-start(bf16[16,1664]{1,0:T(8,128)(2,1)S(1)} %pad_maximum_fusion.2), channel_id=1, source_target_pairs={{0,4},{2,6},{4,0},{6,2},{1,5},{3,7},{5,1},{7,3},{8,12},{10,14},{12... | collective-permute-start | bytes 159752 | tf_op jit(solution)/shard_map/ppermute | solution.py:224
  21.0 4.8 %collective-permute-start.3 = (bf16[32,1664]{1,0:T(8,128)(2,1)S(1)}, bf16[32,1664]{1,0:T(8,128)(2,1)S(1)}, u32[]{:S(2)}, u32[]{:S(2)}) collective-permute-start(bf16[32,1664]{1,0:T(8,128)(2,1)S(1)} %pad_maximum_fusion.1), channel_id=1, source_target_pairs={{0,8},{8,0},{1,9},{9,1},{2,10},{10,2},{3,11},{11,3},{4,12},{12,4},... | collective-permute-start | bytes 319496 | tf_op jit(solution)/shard_map/ppermute | solution.py:224
  25.7 4.6 %copy-start = (bf16[2,1536,2048]{2,1,0:T(8,128)(2,1)S(1)}, bf16[2,1536,2048]{2,1,0:T(8,128)(2,1)}, u32[]{:S(2)}) copy-start(bf16[2,1536,2048]{2,1,0:T(8,128)(2,1)} %gate_ref.3) | copy-start | bytes 37748740
  30.3 4.6 %copy-start.1 = (bf16[2,1536,2048]{2,1,0:T(8,128)(2,1)S(1)}, bf16[2,1536,2048]{2,1,0:T(8,128)(2,1)}, u32[]{:S(2)}) copy-start(bf16[2,1536,2048]{2,1,0:T(8,128)(2,1)} %up_ref.3) | copy-start | bytes 37748740
  37.9 3.5 %copy-start.11 = (f32[2,16,12]{1,0,2:T(2,128)S(1)}, f32[2,16,12]{1,0,2:T(2,128)}, u32[]{:S(2)}) copy-start(f32[2,16,12]{1,0,2:T(2,128)} %param.31) | copy-start | bytes 4612
  40.8 2.0 %collective-permute-start.4 = (bf16[64,4096]{1,0:T(8,128)(2,1)S(1)}, bf16[64,4096]{1,0:T(8,128)(2,1)S(1)}, u32[]{:S(2)}, u32[]{:S(2)}) collective-permute-start(bf16[64,4096]{1,0:T(8,128)(2,1)S(1)} %gate_up.2.refs_0_), channel_id=1, source_target_pairs={{0,1},{1,0},{2,3},{3,2},{4,5},{5,4},{6,7},{7,6},{8,9},{9,8},{10,11... | collective-permute-start | bytes 1572872 | tf_op jit(solution)/shard_map/ppermute | solution.py:224
  40.9 2.6 %collective-permute-start.5 = (bf16[64,4096]{1,0:T(8,128)(2,1)S(1)}, bf16[64,4096]{1,0:T(8,128)(2,1)S(1)}, u32[]{:S(2)}, u32[]{:S(2)}) collective-permute-start(bf16[64,4096]{1,0:T(8,128)(2,1)S(1)} %gate_up.3.refs_2_), channel_id=1, source_target_pairs={{0,1},{1,0},{2,3},{3,2},{4,5},{5,4},{6,7},{7,6},{8,9},{9,8},{10,11... | collective-permute-start | bytes 1572872 | tf_op jit(solution)/shard_map/ppermute | solution.py:224
  43.5 4.6 %copy-start.2 = (bf16[2,2048,1536]{2,1,0:T(8,128)(2,1)S(1)}, bf16[2,2048,1536]{2,1,0:T(8,128)(2,1)}, u32[]{:S(2)}) copy-start(bf16[2,2048,1536]{2,1,0:T(8,128)(2,1)} %refs_4_.1) | copy-start | bytes 37748740
  51.1 5.0 %collective-permute-start.6 = (bf16[32,1536]{1,0:T(8,128)(2,1)S(1)}, bf16[32,1536]{1,0:T(8,128)(2,1)S(1)}, u32[]{:S(2)}, u32[]{:S(2)}) collective-permute-start(bf16[32,1536]{1,0:T(8,128)(2,1)S(1)} %slice.25), channel_id=1, source_target_pairs={{0,8},{8,0},{1,9},{9,1},{2,10},{10,2},{3,11},{11,3},{4,12},{12,4},... | collective-permute-start | bytes 294920 | tf_op jit(solution)/shard_map/ppermute | solution.py:224
  56.2 5.6 %collective-permute-start.7 = (bf16[16,1536]{1,0:T(8,128)(2,1)S(1)}, bf16[16,1536]{1,0:T(8,128)(2,1)S(1)}, u32[]{:S(2)}, u32[]{:S(2)}) collective-permute-start(bf16[16,1536]{1,0:T(8,128)(2,1)S(1)} %slice.27), channel_id=1, source_target_pairs={{0,4},{2,6},{4,0},{6,2},{1,5},{3,7},{5,1},{7,3},{8,12},{10,14},{12... | collective-permute-start | bytes 147464 | tf_op jit(solution)/shard_map/ppermute | solution.py:224
  61.8 3.9 %collective-permute-start.8 = (bf16[8,1536]{1,0:T(8,128)(2,1)S(1)}, bf16[8,1536]{1,0:T(8,128)(2,1)S(1)}, u32[]{:S(2)}, u32[]{:S(2)}) collective-permute-start(bf16[8,1536]{1,0:T(8,128)(2,1)S(1)} %slice.29), channel_id=1, source_target_pairs={{0,2},{2,0},{4,6},{6,4},{1,3},{3,1},{5,7},{7,5},{8,10},{10,8},{12,... | collective-permute-start | bytes 73736 | tf_op jit(solution)/shard_map/ppermute | solution.py:224
  65.7 1.3 %collective-permute-start.9 = (bf16[8,1536]{1,0:T(8,128)(2,1)S(1)}, bf16[8,1536]{1,0:T(8,128)(2,1)S(1)}, u32[]{:S(2)}, u32[]{:S(2)}) collective-permute-start(bf16[8,1536]{1,0:T(8,128)(2,1)S(1)} %add_convert_fusion.2.own_ref), channel_id=1, source_target_pairs={{0,1},{1,0},{2,3},{3,2},{4,5},{5,4},{6,7},{7,6},{8,9},{9,8},{10,11... | collective-permute-start | bytes 73736 | tf_op jit(solution)/shard_map/ppermute | solution.py:224

commit v2 on v1

v2 whole, which is shorter than its diff:
```python
import functools
import math

import jax
import jax.numpy as jnp
from jax import lax
from jax.experimental import pallas as pl
from jax.experimental.pallas import tpu as pltpu
from jax.sharding import PartitionSpec as P

D = 3072
HEADS = 24
KV_HEADS = 8
HEAD_DIM = 128
EXPERTS = 4
QBLOCK = 128
LANES = 128
GROUP = HEADS // KV_HEADS
SLOT = 16
PIECES = 2
VMEM_LIMIT = 16 << 20

LOAD_ATTEND = 1
LOAD_STEP = (2, 2, 2)
LOAD_GATE_UP = 2
LOAD_DOWN = 1
WIDTH = 512

VMEM = pl.BlockSpec(memory_space=pltpu.VMEM)
ANY = pl.BlockSpec(memory_space=pltpu.HBM)


def segment(ref, expert, piece):
    depth = ref.shape[1] // PIECES
    return ref.at[expert, pl.ds(piece * depth, depth), :]


def start_loads(places, sources, targets, sems):
    copies = [
        pltpu.make_async_copy(segment(source, *place), target, sems.at[i])
        for i, (place, source, target) in enumerate(zip(places, sources, targets))
    ]
    for copy in copies:
        copy.start()
    return copies


def attend_kernel(*refs, places):
    count = len(places)
    inputs = refs[:10]
    sources = refs[10 : 10 + count]
    own_ref, other_ref, stream_ref = refs[10 + count : 13 + count]
    targets = refs[13 + count : 13 + 2 * count]
    scratch = refs[13 + 2 * count :]
    held = scratch[:10]
    q_scr, nk_scr, nv_scr, att_scr, in_sems, load_sems = scratch[10:]
    copies = [
        pltpu.make_async_copy(source, target, in_sems.at[i])
        for i, (source, target) in enumerate(zip(inputs, held))
    ]
    for copy in copies:
        copy.start()
    loads = start_loads(places, sources, targets, load_sems)
    (
        query_ref,
        new_key_ref,
        new_value_ref,
        lengths_ref,
        cache_key_ref,
        cache_value_ref,
        residual_ref,
        gain_ref,
        ids_ref,
        levels_ref,
    ) = held
    for copy in copies[:4]:
        copy.wait()
    rows, positions, _ = cache_key_ref.shape
    half = D // 2
    f32 = jnp.float32
    total = KV_HEADS * SLOT
    zeros = jnp.zeros((total, HEAD_DIM), f32)
    q_scr[...] = zeros
    nk_scr[...] = zeros
    nv_scr[...] = zeros
    for j in range(KV_HEADS):
        kv_cols = slice(j * HEAD_DIM, (j + 1) * HEAD_DIM)
        fresh_key = new_key_ref[:, kv_cols].astype(f32)
        fresh_value = new_value_ref[:, kv_cols].astype(f32)
        for g in range(GROUP):
            h = j * GROUP + g
            at = slice(j * SLOT + g * rows, j * SLOT + (g + 1) * rows)
            q_scr[at, :] = query_ref[:, h * HEAD_DIM : (h + 1) * HEAD_DIM].astype(f32)
            nk_scr[at, :] = fresh_key
            nv_scr[at, :] = fresh_value
    queries = q_scr[...]
    factor = 1.0 / math.sqrt(HEAD_DIM)
    fresh_score = jnp.sum(queries * nk_scr[...], axis=1, keepdims=True) * factor
    queries_bf = queries.astype(jnp.bfloat16)
    copies[4].wait()
    keys = cache_key_ref[...].reshape(rows * positions, KV_HEADS * HEAD_DIM)
    scores = jnp.concatenate(
        [
            lax.dot_general(
                queries_bf[j * SLOT : (j + 1) * SLOT],
                keys[:, j * HEAD_DIM : (j + 1) * HEAD_DIM],
                (((1,), (1,)), ((), ())),
                preferred_element_type=f32,
            )
            for j in range(KV_HEADS)
        ],
        axis=0,
    )
    row_of = lax.broadcasted_iota(jnp.int32, (total, positions), 0) % rows
    position = lax.broadcasted_iota(jnp.int32, (total, positions), 1)
    valid = [
        jnp.logical_and(row_of == r, position < lengths_ref[r]) for r in range(rows)
    ]
    pieces = [
        jnp.where(valid[r], scores[:, r * positions : (r + 1) * positions] * factor, -1e30)
        for r in range(rows)
    ]
    peak = functools.reduce(jnp.maximum, pieces)
    peak = jnp.maximum(jnp.max(peak, axis=1, keepdims=True), fresh_score)
    exps = [jnp.where(valid[r], jnp.exp(pieces[r] - peak), 0.0) for r in range(rows)]
    fresh_exp = jnp.exp(fresh_score - peak)
    denominator = jnp.sum(sum(exps[1:], exps[0]), axis=1, keepdims=True) + fresh_exp
    inverse = 1.0 / denominator
    probabilities = jnp.concatenate([(e * inverse).astype(jnp.bfloat16) for e in exps], axis=1)
    fresh_prob = (fresh_exp * inverse).astype(jnp.bfloat16).astype(f32)
    copies[5].wait()
    values = cache_value_ref[...].reshape(rows * positions, KV_HEADS * HEAD_DIM)
    attended = jnp.concatenate(
        [
            jnp.dot(
                probabilities[j * SLOT : (j + 1) * SLOT],
                values[:, j * HEAD_DIM : (j + 1) * HEAD_DIM],
                preferred_element_type=f32,
            )
            for j in range(KV_HEADS)
        ],
        axis=0,
    )
    att_scr[...] = attended + fresh_prob * nv_scr[...]
    for copy in copies[6:]:
        copy.wait()
    squares = jnp.zeros((rows, HEAD_DIM), f32)
    for j in range(KV_HEADS):
        for g in range(GROUP):
            h = j * GROUP + g
            cols = slice(h * HEAD_DIM, (h + 1) * HEAD_DIM)
            at = slice(j * SLOT + g * rows, j * SLOT + (g + 1) * rows)
            piece = residual_ref[:, cols].astype(f32) + att_scr[at, :]
            stream_ref[:, cols] = piece
            squares = squares + piece * piece
    mean_square = jnp.sum(squares, axis=1, keepdims=True) * (1.0 / D)
    normed = stream_ref[...] * lax.rsqrt(mean_square + 1e-05) * gain_ref[...]
    first = lax.axis_index("sub") == 0
    low, high = normed[:, :half], normed[:, half:]
    lane = lax.broadcasted_iota(jnp.int32, (rows, LANES), 1)
    row = lax.broadcasted_iota(jnp.int32, (rows, LANES), 0)
    table = jnp.zeros((rows, LANES), f32)
    for r in range(rows):
        for c in range(2):
            here = jnp.logical_and(row == r, lane == ids_ref[c, r])
            table = jnp.where(here, levels_ref[c, r].astype(f32), table)
    own = jnp.concatenate([jnp.where(first, low, high), table], axis=1)
    other = jnp.concatenate([jnp.where(first, high, low), table], axis=1)
    for ref, value in ((own_ref, own), (other_ref, other)):
        ref[...] = jnp.concatenate(
            [jnp.where(first, value, 0.0), jnp.where(first, 0.0, value)], axis=0
        ).astype(jnp.bfloat16)
    for load in loads:
        load.wait()


def spread(scales, columns, dimension):
    blocks = scales.shape[dimension]
    block = lax.broadcasted_iota(jnp.int32, (blocks, columns), 0)
    column = lax.broadcasted_iota(jnp.int32, (blocks, columns), 1)
    pick = (column // QBLOCK == block).astype(jnp.float32)
    return lax.dot_general(
        scales,
        pick,
        (((dimension,), (0,)), ((), ())),
        precision=lax.Precision.HIGHEST,
        preferred_element_type=jnp.float32,
    )


def load_kernel(*refs, places, spreading):
    count = len(places)
    after_ref, scales = refs[0], refs[1 : 1 + 3 * spreading]
    refs = refs[1 + 3 * spreading :]
    sources, refs = refs[:count], refs[count:]
    refs[0][...] = after_ref[...]
    refs = refs[1:]
    rows_refs, refs = refs[: 3 * spreading], refs[3 * spreading :]
    targets, refs = refs[:count], refs[count:]
    load_sems = refs[0]
    loads = start_loads(places, sources, targets, load_sems)
    if spreading:
        held, sems = refs[1:4], refs[4]
        copies = [
            pltpu.make_async_copy(source, target, sems.at[i])
            for i, (source, target) in enumerate(zip(scales, held))
        ]
        for copy in copies:
            copy.start()
        for i, (copy, target, out_ref) in enumerate(zip(copies, held, rows_refs)):
            copy.wait()
            experts, _, columns = out_ref.shape
            for e in range(experts):
                out_ref[e] = spread(target[:, e, :], columns, 1 if i < 2 else 0)
    for load in loads:
        load.wait()


def scaled_product(left, pieces, scales_ref, expert, column, width):
    depth = pieces[0].shape[0] // QBLOCK
    total = None
    for k in range(len(pieces) * depth):
        at = (k % depth) * QBLOCK
        product = jnp.dot(
            left[:, k * QBLOCK : (k + 1) * QBLOCK],
            pieces[k // depth][at : at + QBLOCK, column : column + width],
            preferred_element_type=jnp.float32,
        )
        product = product * scales_ref[expert, k : k + 1, column : column + width]
        total = product if total is None else total + product
    return total


def gate_up_kernel(*refs, expert, places):
    count = len(places)
    x_ref, gate_s_ref, up_s_ref = refs[:3]
    gate, up = refs[3 : 3 + PIECES], refs[3 + PIECES : 3 + 2 * PIECES]
    refs = refs[3 + 2 * PIECES :]
    sources, out_ref, targets = refs[:count], refs[count], refs[count + 1 : 2 * count + 1]
    loads = start_loads(places, sources, targets, refs[-1])
    units = gate[0].shape[1]
    depth = gate[0].shape[0] * PIECES
    rows = x_ref.shape[0]
    block = min(rows, 64)
    width = min(units, WIDTH)
    for m in range(rows // block):
        at = slice(m * block, (m + 1) * block)
        left = x_ref[at, :depth]
        for column in range(0, units, width):
            out_ref[at, column : column + width] = scaled_product(
                left, gate, gate_s_ref, expert, column, width
            ).astype(jnp.bfloat16)
            out_ref[at, units + column : units + column + width] = scaled_product(
                left, up, up_s_ref, expert, column, width
            ).astype(jnp.bfloat16)
    for load in loads:
        load.wait()


def down_kernel(*refs, expert, experts, places):
    count = len(places)
    x_ref, mine, theirs, down_s_ref = refs[:4]
    down, refs = refs[4 : 4 + PIECES], refs[4 + PIECES :]
    before = None
    if expert > 0:
        before, refs = refs[0], refs[1:]
    sources, out_ref, targets = refs[:count], refs[count], refs[count + 1 : 2 * count + 1]
    loads = start_loads(places, sources, targets, refs[-1])
    columns = down[0].shape[1]
    units = down[0].shape[0] * PIECES
    rows, extended = x_ref.shape
    block = min(rows, 64)
    width = 256
    f32 = jnp.float32
    wanted = lax.axis_index("role") * experts + expert
    for m in range(rows // block):
        at = slice(m * block, (m + 1) * block)
        levels = x_ref[at, extended - LANES :].astype(f32)
        lane = lax.broadcasted_iota(jnp.int32, levels.shape, 1)
        level = jnp.sum(jnp.where(lane == wanted, levels, 0.0), axis=1, keepdims=True)
        share = level / jnp.sum(levels, axis=1, keepdims=True)
        chunks = []
        for u in range(0, units, width):
            gate = mine[at, u : u + width].astype(f32) + theirs[at, u : u + width].astype(f32)
            v = slice(units + u, units + u + width)
            up = mine[at, v].astype(f32) + theirs[at, v].astype(f32)
            silu = gate / (1.0 + jnp.exp(-gate))
            chunks.append((silu * up * share).astype(jnp.bfloat16))
        hidden = jnp.concatenate(chunks, axis=1)
        for column in range(0, columns, width):
            total = scaled_product(hidden, down, down_s_ref, expert, column, width)
            if before is not None:
                total = total + before[at, column : column + width]
            out_ref[at, column : column + width] = total.astype(out_ref.dtype)
    for load in loads:
        load.wait()


def finish_kernel(stream_ref, own_ref, other_ref, out_ref):
    half = D // 2
    rows = stream_ref.shape[0]
    first = lax.axis_index("sub") == 0
    own, other = (
        jnp.where(first, pair[:rows], pair[rows:])
        for pair in (own_ref[...].astype(jnp.float32), other_ref[...].astype(jnp.float32))
    )
    out_ref[:, :half] = (stream_ref[:, :half] + jnp.where(first, own, other)).astype(jnp.bfloat16)
    out_ref[:, half:] = (stream_ref[:, half:] + jnp.where(first, other, own)).astype(jnp.bfloat16)


def swap(x, axis, bit):
    count = lax.axis_size(axis)
    return lax.ppermute(x, axis, [(i, i ^ bit) for i in range(count)])


def bits(axis):
    return [1 << b for b in range(lax.axis_size(axis).bit_length() - 1)]


def add_bf16(a, b):
    return (a.astype(jnp.float32) + b.astype(jnp.float32)).astype(jnp.bfloat16)


def swap(x, axis, bit):
    count = lax.axis_size(axis)
    return lax.ppermute(x, axis, [(i, i ^ bit) for i in range(count)])


def bits(axis):
    return [1 << b for b in range(lax.axis_size(axis).bit_length() - 1)]


def add_bf16(a, b):
    return (a.astype(jnp.float32) + b.astype(jnp.float32)).astype(jnp.bfloat16)


class Loader:
    def __init__(self, gate, up, down):
        self.experts = gate.shape[0]
        self.arrays = {"gate": gate, "up": up, "down": down}
        self.waiting = [
            (name, e, piece)
            for names in (("gate", "up"), ("down",))
            for e in range(self.experts)
            for name in names
            for piece in range(PIECES)
        ]
        self.loaded = {}

    def take(self, count):
        taken, self.waiting = self.waiting[:count], self.waiting[count:]
        return taken

    def missing(self, expert, names):
        return sum(1 for name, e, _ in self.waiting if e == expert and name in names)

    def call(self, kernel, taken, inputs, specs, outputs, scratch, name, cost, **static):
        sources = [self.arrays[segment_name] for segment_name, _, _ in taken]
        shapes = [
            pltpu.VMEM((a.shape[1] // PIECES, a.shape[2]), a.dtype) for a in sources
        ]
        moved = sum(2 * math.prod(shape.shape) for shape in shapes)
        inputs = [
            pltpu.with_memory_space_constraint(x, pltpu.HBM) if spec is ANY else x
            for x, spec in zip(inputs, specs)
        ]
        sources = [pltpu.with_memory_space_constraint(x, pltpu.HBM) for x in sources]
        results = pl.pallas_call(
            functools.partial(kernel, places=tuple((e, p) for _, e, p in taken), **static),
            out_shape=tuple(outputs) + tuple(shapes),
            in_specs=list(specs) + [ANY] * len(taken),
            out_specs=tuple([VMEM] * (len(outputs) + len(taken))),
            scratch_shapes=list(scratch(len(taken))),
            compiler_params=pltpu.CompilerParams(vmem_limit_bytes=VMEM_LIMIT),
            cost_estimate=pl.CostEstimate(
                flops=0, bytes_accessed=cost + moved, transcendentals=0
            ),
            name=name,
        )(*inputs, *sources)
        for at, array in zip(taken, results[len(outputs) :]):
            self.loaded[at] = array
        return results[: len(outputs)]

    def pieces(self, name, expert):
        return [self.loaded[(name, expert, piece)] for piece in range(PIECES)]


def semaphores(count):
    return pltpu.SemaphoreType.DMA((max(count, 1),))


def load_more(loader, taken, after, scales):
    outputs, scratch = [jax.ShapeDtypeStruct(after.shape, after.dtype)], []
    if scales:
        experts, depth, units = loader.arrays["gate"].shape
        columns = loader.arrays["down"].shape[2]
        outputs += [
            jax.ShapeDtypeStruct((experts, depth // QBLOCK, units), jnp.float32),
            jax.ShapeDtypeStruct((experts, depth // QBLOCK, units), jnp.float32),
            jax.ShapeDtypeStruct((experts, units // QBLOCK, columns), jnp.float32),
        ]
        scratch = [pltpu.VMEM(s.shape, s.dtype) for s in scales] + [semaphores(3)]
    return loader.call(
        load_kernel,
        taken,
        [after, *scales],
        [VMEM] + [ANY] * len(scales),
        outputs,
        lambda count: [semaphores(count)] + scratch,
        "load",
        0,
        spreading=1 if scales else 0,
    )


def per_device(
    residual,
    query,
    new_key,
    new_value,
    cache_key,
    cache_value,
    lengths,
    norm_gain,
    expert_ids,
    gate_levels,
    gate_codes,
    gate_scales,
    up_codes,
    up_scales,
    down_codes,
    down_scales,
):
    rows = residual.shape[0]
    half = D // 2
    extended = half + LANES
    experts, _, units = gate_codes.shape
    loader = Loader(gate_codes, up_codes, down_codes)
    inputs = [
        query,
        new_key,
        new_value,
        lengths,
        cache_key,
        cache_value,
        residual,
        norm_gain.reshape(1, D),
        expert_ids.T,
        gate_levels.T,
    ]
    stacked = pltpu.VMEM((KV_HEADS * SLOT, HEAD_DIM), jnp.float32)
    held = [
        (pltpu.SMEM if x.dtype == jnp.int32 else pltpu.VMEM)(x.shape, x.dtype) for x in inputs
    ]
    own, other, stream = loader.call(
        attend_kernel,
        loader.take(LOAD_ATTEND),
        inputs,
        [ANY] * len(inputs),
        [
            jax.ShapeDtypeStruct((2 * rows, extended), jnp.bfloat16),
            jax.ShapeDtypeStruct((2 * rows, extended), jnp.bfloat16),
            jax.ShapeDtypeStruct((rows, D), jnp.float32),
        ],
        lambda count: held + [stacked] * 4 + [semaphores(len(inputs)), semaphores(count)],
        "attend",
        4 << 20,
    )
    scales = [
        gate_scales.transpose(1, 0, 2),
        up_scales.transpose(1, 0, 2),
        down_scales.transpose(2, 0, 1),
    ]
    gathered = own + swap(other, "sub", 1)
    steps = [("tp", bit) for bit in bits("tp")] + [("role", bit) for bit in bits("role")]
    spread_scales = None
    for number, (axis, bit) in enumerate(steps):
        arriving = swap(gathered, axis, bit)
        taken = loader.take(LOAD_STEP[min(number, len(LOAD_STEP) - 1)])
        if spread_scales is None:
            gathered, *spread_scales = load_more(loader, taken, gathered, scales)
        elif taken:
            (gathered,) = load_more(loader, taken, gathered, [])
        gathered = jnp.concatenate([gathered, arriving], axis=0)
    gate_s, up_s, down_s = spread_scales
    total_rows = gathered.shape[0]
    parts = []
    x = gathered
    for e in range(experts):
        missing = loader.missing(e, ("gate", "up"))
        if missing:
            (x,) = load_more(loader, loader.take(missing), x, [])
        (part,) = loader.call(
            gate_up_kernel,
            loader.take(LOAD_GATE_UP),
            [x, gate_s, up_s, *loader.pieces("gate", e), *loader.pieces("up", e)],
            [VMEM] * (3 + 2 * PIECES),
            [jax.ShapeDtypeStruct((total_rows, 2 * units), jnp.bfloat16)],
            lambda count: [semaphores(count)],
            "gate_up",
            8 << 20,
            expert=e,
        )
        parts.append((part, swap(part, "sub", 1)))
        x, _ = lax.optimization_barrier((x, part))
    carried = None
    for e in range(experts):
        last = e == experts - 1
        missing = loader.missing(e, ("down",))
        if missing:
            load_more(loader, loader.take(missing), parts[-1][0], [])
        before = [] if carried is None else [carried]
        (carried,) = loader.call(
            down_kernel,
            loader.take(LOAD_DOWN),
            [gathered, *parts[e], down_s, *loader.pieces("down", e), *before],
            [VMEM] * (4 + PIECES + len(before)),
            [
                jax.ShapeDtypeStruct(
                    (total_rows, half), jnp.bfloat16 if last else jnp.float32
                )
            ],
            lambda count: [semaphores(count)],
            "down",
            4 << 20,
            expert=e,
            experts=experts,
        )
    for axis, bit in reversed(steps):
        kept = carried.shape[0] // 2
        carried = add_bf16(carried[:kept], swap(carried[kept:], axis, bit))
    return pl.pallas_call(
        finish_kernel,
        out_shape=jax.ShapeDtypeStruct((rows, D), jnp.bfloat16),
        in_specs=[VMEM] * 3,
        out_specs=VMEM,
        compiler_params=pltpu.CompilerParams(vmem_limit_bytes=VMEM_LIMIT),
        name="finish",
    )(stream, carried, swap(carried, "sub", 1))


def solution(mesh):
    row = ("group", "role", "tp", "sub")
    in_specs = (
        P(row, None),
        P(row, None),
        P(row, None),
        P(row, None),
        P(row, None, None),
        P(row, None, None),
        P(row),
        P(),
        P(row, None),
        P(row, None),
        P("role", "sub", "tp"),
        P("role", "sub", "tp"),
        P("role", "sub", "tp"),
        P("role", "sub", "tp"),
        P("role", "tp", "sub"),
        P("role", "tp", "sub"),
    )
    return jax.shard_map(
        per_device, mesh=mesh, in_specs=in_specs, out_specs=P(row, None), check_vma=False
    )
```

time: 68.3 us -> 46.6 us (0.68)
  local copies, waits for them, and re-layouts: 23.5 us -> 0.07 us
  Pallas kernels: 10.9 us -> 20.9 us
  waiting for transfers between devices: 17.6 us -> 12.8 us
  starting transfers between devices: 15.4 us -> 12.3 us
    unnamed x29 -> x3, local copies, waits for them, and re-layouts: 23.4 us -> 0.02 us
    pallas_call x4 -> x8, Pallas kernels: 10.3 us -> 20.3 us  [call(): pl.pallas_call(functools.partial(kernel, places=tuple(((e, p) for _, e, p...]
    ppermute x10, waiting for transfers between devices: 17.6 us -> 12.8 us  [swap(): return lax.ppermute(x, axis, [(i, i ^ bit) for i in range(count)])]
    ppermute x10, starting transfers between devices: 15.4 us -> 12.3 us  [swap(): return lax.ppermute(x, axis, [(i, i ^ bit) for i in range(count)])]
  transfers between devices with their start and end apart: 10 -> 10, of which waited for: 10 -> 7; matrix products, arithmetic and copies ran while one was open for 2% -> 0% of each run, Pallas kernels for 0% -> 29%
where the time goes in v2:
time: 46.6 us; the launch traced here: 46.3 us
  Pallas kernels  20.9 us (45%)
  waiting for transfers between devices  12.8 us (27%)
  starting transfers between devices  12.3 us (26%)
    pallas_call x8, Pallas kernels, call(): pl.pallas_call(functools.partial(kernel, places=tuple(((e, p) for _, e, p...  20.3 us
    ppermute x10, waiting for transfers between devices, swap(): return lax.ppermute(x, axis, [(i, i ^ bit) for i in range(count)])  12.8 us
    ppermute x10, starting transfers between devices, swap(): return lax.ppermute(x, axis, [(i, i ^ bit) for i in range(count)])  12.3 us
  transfers between devices with their start and end apart: 10, of which 7 were waited for; matrix products, arithmetic and copies ran while one was open for 0% of the time, Pallas kernels for 29%

profile of v2, /device:TPU:0, one launch (start us, length us, event | category | flops | bytes accessed | tf_op | source)
XLA Modules:
  0.0 46.3 jit_solution(9288669674134407483)
XLA Ops:
  0.0 2.7 %attend.1 = (bf16[8,1664]{1,0:T(8,128)(2,1)S(1)}, bf16[8,1664]{1,0:T(8,128)(2,1)S(1)}, f32[4,3072]{1,0:T(4,128)S(1)}, bf16[768,2048]{1,0:T(8,128)(2,1)S(1)}) custom-call(bf16[4,3072]{1,0:T(4,128)(2,1)} %refs_0_.1, bf16[4,1024]{1,0:T(4,128)(2,1)} %refs_1_.3, bf16[4,1024]{1,0:T(4,128)(2,1)} %refs_2_.3, s32[4]{0:T(128)} %refs_3_.1, ...), custom_call_target="tpu_custom_call" | custom-call | bytes 7340032 | tf_op jit(solution)/shard_map/attend/pallas_call | solution.py:368
  2.7 0.5 %collective-permute-start = (bf16[8,1664]{1,0:T(8,128)(2,1)S(1)}, bf16[8,1664]{1,0:T(8,128)(2,1)S(1)}, u32[]{:S(2)}, u32[]{:S(2)}) collective-permute-start(bf16[8,1664]{1,0:T(8,128)(2,1)S(1)} %get-tuple-element.32), channel_id=1, source_target_pairs={{0,1},{1,0},{2,3},{3,2},{4,5},{5,4},{6,7},{7,6},{8,9},{9,8},{10,11... | collective-permute-start | bytes 79880 | tf_op jit(solution)/shard_map/ppermute | solution.py:326
  3.2 0.9 %collective-permute-done = bf16[8,1664]{1,0:T(8,128)(2,1)S(1)} collective-permute-done((bf16[8,1664]{1,0:T(8,128)(2,1)S(1)}, bf16[8,1664]{1,0:T(8,128)(2,1)S(1)}, u32[]{:S(2)}, u32[]{:S(2)}) %collective-permute-start) | collective-permute-done | bytes 26656 | tf_op jit(solution)/shard_map/ppermute | solution.py:326
  4.1 3.0 %collective-permute-start.1 = (bf16[8,1664]{1,0:T(8,128)(2,1)S(1)}, bf16[8,1664]{1,0:T(8,128)(2,1)S(1)}, u32[]{:S(2)}, u32[]{:S(2)}) collective-permute-start(bf16[8,1664]{1,0:T(8,128)(2,1)S(1)} %add.12.refs_0_), channel_id=1, source_target_pairs={{0,2},{2,0},{4,6},{6,4},{1,3},{3,1},{5,7},{7,5},{8,10},{10,8},{12,... | collective-permute-start | bytes 79880 | tf_op jit(solution)/shard_map/ppermute | solution.py:326
  7.1 3.1 %load.3 = (bf16[8,1664]{1,0:T(8,128)(2,1)S(1)}, f32[2,12,2048]{2,1,0:T(8,128)S(1)}, f32[2,12,2048]{2,1,0:T(8,128)S(1)}, f32[2,16,1536]{2,1,0:T(8,128)S(1)}, bf16...) custom-call(bf16[8,1664]{1,0:T(8,128)(2,1)S(1)} %add.12.refs_0_, f32[12,2,16]{2,1,0:T(2,128)} %bitcast.7, ...), custom_call_target="tpu_custom_call" | custom-call | bytes 6291456 | tf_op jit(solution)/shard_map/load/pallas_call | solution.py:368
  10.2 0.0 collective-permute-done.1
  10.2 2.7 %collective-permute-start.2 = (bf16[16,1664]{1,0:T(8,128)(2,1)S(1)}, bf16[16,1664]{1,0:T(8,128)(2,1)S(1)}, u32[]{:S(2)}, u32[]{:S(2)}) collective-permute-start(bf16[16,1664]{1,0:T(8,128)(2,1)S(1)} %constant_dynamic-update-slice_fusion.refs_0_), channel_id=1, source_target_pairs={{0,4},{2,6},{4,0},{6,2},{1,5},{3,7},{5,1},{7,3},{8,12},{10,14},{12... | collective-permute-start | bytes 159752 | tf_op jit(solution)/shard_map/ppermute | solution.py:326
  12.9 2.9 %load.4 = (bf16[16,1664]{1,0:T(8,128)(2,1)S(1)}, bf16[768,2048]{1,0:T(8,128)(2,1)S(1)}, bf16[768,2048]{1,0:T(8,128)(2,1)S(1)}) custom-call(bf16[16,1664]{1,0:T(8,128)(2,1)S(1)} %constant_dynamic-update-slice_fusion.refs_0_, bf16[2,1536,2048]{2,1,0:T(8,128)(2,1)} %refs_7_.2, bf16[2,1536,2048]{2,1,0:T(8,128)(2,1)} %refs_1_.5), custom_call_target="tpu_custom_call" | custom-call | bytes 6291456 | tf_op jit(solution)/shard_map/load/pallas_call | solution.py:368
  15.8 0.1 collective-permute-done.2
  15.9 1.5 %collective-permute-start.3 = (bf16[32,1664]{1,0:T(8,128)(2,1)S(1)}, bf16[32,1664]{1,0:T(8,128)(2,1)S(1)}, u32[]{:S(2)}, u32[]{:S(2)}) collective-permute-start(bf16[32,1664]{1,0:T(8,128)(2,1)S(1)} %constant_dynamic-update-slice_fusion.2.refs_0_), channel_id=1, source_target_pairs={{0,8},{8,0},{1,9},{9,1},{2,10},{10,2},{3,11},{11,3},{4,12},{12,4},... | collective-permute-start | bytes 319496 | tf_op jit(solution)/shard_map/ppermute | solution.py:326
  17.4 2.9 %load.5 = (bf16[32,1664]{1,0:T(8,128)(2,1)S(1)}, bf16[768,2048]{1,0:T(8,128)(2,1)S(1)}, bf16[768,2048]{1,0:T(8,128)(2,1)S(1)}) custom-call(bf16[32,1664]{1,0:T(8,128)(2,1)S(1)} %constant_dynamic-update-slice_fusion.2.refs_0_, bf16[2,1536,2048]{2,1,0:T(8,128)(2,1)} %refs_1_.5, bf16[2,1536,2048]{2,1,0:T(8,128)(2,1)} %refs_7_.2), custom_call_target="tpu_custom_call" | custom-call | bytes 6291456 | tf_op jit(solution)/shard_map/load/pallas_call | solution.py:368
  20.3 0.3 collective-permute-done.3
  20.6 2.9 %gate_up.2 = (bf16[64,4096]{1,0:T(8,128)(2,1)S(1)}, bf16[768,2048]{1,0:T(8,128)(2,1)S(1)}, bf16[1024,1536]{1,0:T(8,128)(2,1)S(1)}) custom-call(bf16[64,1664]{1,0:T(8,128)(2,1)S(1)} %constant_dynamic-update-slice_fusion.4.refs_0_, f32[2,12,2048]{2,1,0:T(8,128)S(1)} %get-tuple-element.36.refs_1_, f32[2,12,2048]{2,1,0:T(8,128)S(1)} %get-tuple-element.37.refs_2_, ...), custom_call_target="tpu_custom_call" | custom-call | bytes 14680064 | tf_op jit(solution)/shard_map/gate_up/pallas_call | solution.py:368
  23.5 0.1 collective-permute-start.5
  23.6 2.9 %gate_up.3 = (bf16[64,4096]{1,0:T(8,128)(2,1)S(1)}, bf16[1024,1536]{1,0:T(8,128)(2,1)S(1)}, bf16[1024,1536]{1,0:T(8,128)(2,1)S(1)}) custom-call(bf16[64,1664]{1,0:T(8,128)(2,1)S(1)} %constant_dynamic-update-slice_fusion.4.refs_0_, f32[2,12,2048]{2,1,0:T(8,128)S(1)} %get-tuple-element.36.refs_1_, f32[2,12,2048]{2,1,0:T(8,128)S(1)} %get-tuple-element.37.refs_2_, ...), custom_call_target="tpu_custom_call" | custom-call | bytes 14680064 | tf_op jit(solution)/shard_map/gate_up/pallas_call | solution.py:368
  26.5 0.6 %collective-permute-start.4 = (bf16[64,4096]{1,0:T(8,128)(2,1)S(1)}, bf16[64,4096]{1,0:T(8,128)(2,1)S(1)}, u32[]{:S(2)}, u32[]{:S(2)}) collective-permute-start(bf16[64,4096]{1,0:T(8,128)(2,1)S(1)} %get-tuple-element.48.refs_1_), channel_id=1, source_target_pairs={{0,1},{1,0},{2,3},{3,2},{4,5},{5,4},{6,7},{7,6},{8,9},{9,8},{10,11... | collective-permute-start | bytes 1572872 | tf_op jit(solution)/shard_map/ppermute | solution.py:326
  27.0 0.0 collective-permute-done.5.refs_2_
  27.0 1.9 %down.2 = (f32[64,1536]{1,0:T(8,128)S(1)}, bf16[1024,1536]{1,0:T(8,128)(2,1)S(1)}) custom-call(bf16[64,1664]{1,0:T(8,128)(2,1)S(1)} %constant_dynamic-update-slice_fusion.4.refs_0_, bf16[64,4096]{1,0:T(8,128)(2,1)S(1)} %get-tuple-element.42.refs_1_, bf16[64,4096]{1,0:T(8,128)(2,1)S(1)} %collective-permute-done.5.refs_2_, ...), custom_call_target="tpu_custom_call" | custom-call | bytes 7340032 | tf_op jit(solution)/shard_map/down/pallas_call | solution.py:368
  28.9 0.0 collective-permute-done.4.refs_2_
  28.9 1.1 %down.3 = bf16[64,1536]{1,0:T(8,128)(2,1)S(1)} custom-call(bf16[64,1664]{1,0:T(8,128)(2,1)S(1)} %constant_dynamic-update-slice_fusion.4.refs_0_, bf16[64,4096]{1,0:T(8,128)(2,1)S(1)} %get-tuple-element.48.refs_1_, bf16[64,4096]{1,0:T(8,128)(2,1)S(1)} %collective-permute-done.4.refs_2_, f32[2,16,1536]{2,1,0:T(8,128)S(1)} %get-tuple-element.49.refs_3_, ...), custom_call_target="tpu_custom_call" | custom-call | bytes 4194304 | tf_op jit(solution)/shard_map/down/pallas_call | solution.py:368
  30.1 1.6 %collective-permute-start.6 = (bf16[32,1536]{1,0:T(8,128)(2,1)S(1)}, bf16[32,1536]{1,0:T(8,128)(2,1)S(1)}, u32[]{:S(2)}, u32[]{:S(2)}) collective-permute-start(bf16[32,1536]{1,0:T(8,128)(2,1)S(1)} %slice.25), channel_id=1, source_target_pairs={{0,8},{8,0},{1,9},{9,1},{2,10},{10,2},{3,11},{11,3},{4,12},{12,4},... | collective-permute-start | bytes 294920 | tf_op jit(solution)/shard_map/ppermute | solution.py:326
  31.7 3.2 %collective-permute-done.6 = bf16[32,1536]{1,0:T(8,128)(2,1)S(1)} collective-permute-done((bf16[32,1536]{1,0:T(8,128)(2,1)S(1)}, bf16[32,1536]{1,0:T(8,128)(2,1)S(1)}, u32[]{:S(2)}, u32[]{:S(2)}) %collective-permute-start.6) | collective-permute-done | bytes 98336 | tf_op jit(solution)/shard_map/ppermute | solution.py:326
  34.9 2.1 %collective-permute-start.7 = (bf16[16,1536]{1,0:T(8,128)(2,1)S(1)}, bf16[16,1536]{1,0:T(8,128)(2,1)S(1)}, u32[]{:S(2)}, u32[]{:S(2)}) collective-permute-start(bf16[16,1536]{1,0:T(8,128)(2,1)S(1)} %slice.27), channel_id=1, source_target_pairs={{0,4},{2,6},{4,0},{6,2},{1,5},{3,7},{5,1},{7,3},{8,12},{10,14},{12... | collective-permute-start | bytes 147464 | tf_op jit(solution)/shard_map/ppermute | solution.py:326
  37.1 3.4 %collective-permute-done.7 = bf16[16,1536]{1,0:T(8,128)(2,1)S(1)} collective-permute-done((bf16[16,1536]{1,0:T(8,128)(2,1)S(1)}, bf16[16,1536]{1,0:T(8,128)(2,1)S(1)}, u32[]{:S(2)}, u32[]{:S(2)}) %collective-permute-start.7) | collective-permute-done | bytes 49184 | tf_op jit(solution)/shard_map/ppermute | solution.py:326
  40.5 0.2 collective-permute-start.8
  40.8 3.7 %collective-permute-done.8 = bf16[8,1536]{1,0:T(8,128)(2,1)S(1)} collective-permute-done((bf16[8,1536]{1,0:T(8,128)(2,1)S(1)}, bf16[8,1536]{1,0:T(8,128)(2,1)S(1)}, u32[]{:S(2)}, u32[]{:S(2)}) %collective-permute-start.8) | collective-permute-done | bytes 24608 | tf_op jit(solution)/shard_map/ppermute | solution.py:326
  44.5 0.1 collective-permute-start.9
  44.5 1.2 %collective-permute-done.9.other_ref = bf16[8,1536]{1,0:T(8,128)(2,1)S(1)} collective-permute-done((bf16[8,1536]{1,0:T(8,128)(2,1)S(1)}, bf16[8,1536]{1,0:T(8,128)(2,1)S(1)}, u32[]{:S(2)}, u32[]{:S(2)}) %collective-permute-start.9) | collective-permute-done | bytes 24608 | tf_op jit(solution)/shard_map/ppermute | solution.py:326
  45.7 0.6 %finish.1 = bf16[4,3072]{1,0:T(4,128)(2,1)} custom-call(f32[4,3072]{1,0:T(4,128)S(1)} %get-tuple-element.30.stream_ref, bf16[8,1536]{1,0:T(8,128)(2,1)S(1)} %add_convert_fusion.2.own_ref, bf16[8,1536]{1,0:T(8,128)(2,1)S(1)} %collective-permute-done.9.other_ref), custom_call_target="tpu_custom_call" | custom-call | tf_op jit(solution)/shard_map/finish/pallas_call | solution.py:532
  (13 shorter events, 0.1 us)
Async XLA Ops:
  2.7 1.4 %collective-permute-start = (bf16[8,1664]{1,0:T(8,128)(2,1)S(1)}, bf16[8,1664]{1,0:T(8,128)(2,1)S(1)}, u32[]{:S(2)}, u32[]{:S(2)}) collective-permute-start(bf16[8,1664]{1,0:T(8,128)(2,1)S(1)} %get-tuple-element.32), channel_id=1, source_target_pairs={{0,1},{1,0},{2,3},{3,2},{4,5},{5,4},{6,7},{7,6},{8,9},{9,8},{10,11... | collective-permute-start | bytes 79880 | tf_op jit(solution)/shard_map/ppermute | solution.py:326
  4.1 6.1 %collective-permute-start.1 = (bf16[8,1664]{1,0:T(8,128)(2,1)S(1)}, bf16[8,1664]{1,0:T(8,128)(2,1)S(1)}, u32[]{:S(2)}, u32[]{:S(2)}) collective-permute-start(bf16[8,1664]{1,0:T(8,128)(2,1)S(1)} %add.12.refs_0_), channel_id=1, source_target_pairs={{0,2},{2,0},{4,6},{6,4},{1,3},{3,1},{5,7},{7,5},{8,10},{10,8},{12,... | collective-permute-start | bytes 79880 | tf_op jit(solution)/shard_map/ppermute | solution.py:326
  10.2 5.7 %collective-permute-start.2 = (bf16[16,1664]{1,0:T(8,128)(2,1)S(1)}, bf16[16,1664]{1,0:T(8,128)(2,1)S(1)}, u32[]{:S(2)}, u32[]{:S(2)}) collective-permute-start(bf16[16,1664]{1,0:T(8,128)(2,1)S(1)} %constant_dynamic-update-slice_fusion.refs_0_), channel_id=1, source_target_pairs={{0,4},{2,6},{4,0},{6,2},{1,5},{3,7},{5,1},{7,3},{8,12},{10,14},{12... | collective-permute-start | bytes 159752 | tf_op jit(solution)/shard_map/ppermute | solution.py:326
  15.9 4.7 %collective-permute-start.3 = (bf16[32,1664]{1,0:T(8,128)(2,1)S(1)}, bf16[32,1664]{1,0:T(8,128)(2,1)S(1)}, u32[]{:S(2)}, u32[]{:S(2)}) collective-permute-start(bf16[32,1664]{1,0:T(8,128)(2,1)S(1)} %constant_dynamic-update-slice_fusion.2.refs_0_), channel_id=1, source_target_pairs={{0,8},{8,0},{1,9},{9,1},{2,10},{10,2},{3,11},{11,3},{4,12},{12,4},... | collective-permute-start | bytes 319496 | tf_op jit(solution)/shard_map/ppermute | solution.py:326
  23.5 3.5 %collective-permute-start.5 = (bf16[64,4096]{1,0:T(8,128)(2,1)S(1)}, bf16[64,4096]{1,0:T(8,128)(2,1)S(1)}, u32[]{:S(2)}, u32[]{:S(2)}) collective-permute-start(bf16[64,4096]{1,0:T(8,128)(2,1)S(1)} %get-tuple-element.42.refs_1_), channel_id=1, source_target_pairs={{0,1},{1,0},{2,3},{3,2},{4,5},{5,4},{6,7},{7,6},{8,9},{9,8},{10,11... | collective-permute-start | bytes 1572872 | tf_op jit(solution)/shard_map/ppermute | solution.py:326
  26.5 2.5 %collective-permute-start.4 = (bf16[64,4096]{1,0:T(8,128)(2,1)S(1)}, bf16[64,4096]{1,0:T(8,128)(2,1)S(1)}, u32[]{:S(2)}, u32[]{:S(2)}) collective-permute-start(bf16[64,4096]{1,0:T(8,128)(2,1)S(1)} %get-tuple-element.48.refs_1_), channel_id=1, source_target_pairs={{0,1},{1,0},{2,3},{3,2},{4,5},{5,4},{6,7},{7,6},{8,9},{9,8},{10,11... | collective-permute-start | bytes 1572872 | tf_op jit(solution)/shard_map/ppermute | solution.py:326
  30.1 4.8 %collective-permute-start.6 = (bf16[32,1536]{1,0:T(8,128)(2,1)S(1)}, bf16[32,1536]{1,0:T(8,128)(2,1)S(1)}, u32[]{:S(2)}, u32[]{:S(2)}) collective-permute-start(bf16[32,1536]{1,0:T(8,128)(2,1)S(1)} %slice.25), channel_id=1, source_target_pairs={{0,8},{8,0},{1,9},{9,1},{2,10},{10,2},{3,11},{11,3},{4,12},{12,4},... | collective-permute-start | bytes 294920 | tf_op jit(solution)/shard_map/ppermute | solution.py:326
  34.9 5.6 %collective-permute-start.7 = (bf16[16,1536]{1,0:T(8,128)(2,1)S(1)}, bf16[16,1536]{1,0:T(8,128)(2,1)S(1)}, u32[]{:S(2)}, u32[]{:S(2)}) collective-permute-start(bf16[16,1536]{1,0:T(8,128)(2,1)S(1)} %slice.27), channel_id=1, source_target_pairs={{0,4},{2,6},{4,0},{6,2},{1,5},{3,7},{5,1},{7,3},{8,12},{10,14},{12... | collective-permute-start | bytes 147464 | tf_op jit(solution)/shard_map/ppermute | solution.py:326
  40.5 3.9 %collective-permute-start.8 = (bf16[8,1536]{1,0:T(8,128)(2,1)S(1)}, bf16[8,1536]{1,0:T(8,128)(2,1)S(1)}, u32[]{:S(2)}, u32[]{:S(2)}) collective-permute-start(bf16[8,1536]{1,0:T(8,128)(2,1)S(1)} %slice.29), channel_id=1, source_target_pairs={{0,2},{2,0},{4,6},{6,4},{1,3},{3,1},{5,7},{7,5},{8,10},{10,8},{12,... | collective-permute-start | bytes 73736 | tf_op jit(solution)/shard_map/ppermute | solution.py:326
  44.5 1.3 %collective-permute-start.9 = (bf16[8,1536]{1,0:T(8,128)(2,1)S(1)}, bf16[8,1536]{1,0:T(8,128)(2,1)S(1)}, u32[]{:S(2)}, u32[]{:S(2)}) collective-permute-start(bf16[8,1536]{1,0:T(8,128)(2,1)S(1)} %add_convert_fusion.2.own_ref), channel_id=1, source_target_pairs={{0,1},{1,0},{2,3},{3,2},{4,5},{5,4},{6,7},{7,6},{8,9},{9,8},{10,11... | collective-permute-start | bytes 73736 | tf_op jit(solution)/shard_map/ppermute | solution.py:326

commit v3 on v2

--- a/solution.py
+++ b/solution.py
@@ -21,7 +21,7 @@
 VMEM_LIMIT = 16 << 20
 
 LOAD_ATTEND = 1
-LOAD_STEP = (2, 2, 2)
+LOAD_STEP = (2, 1, 0)
 LOAD_GATE_UP = 2
 LOAD_DOWN = 1
 WIDTH = 512
@@ -234,8 +234,8 @@
 def gate_up_kernel(*refs, expert, places):
     count = len(places)
     x_ref, gate_s_ref, up_s_ref = refs[:3]
-    gate, up = refs[3 : 3 + PIECES], refs[3 + PIECES : 3 + 2 * PIECES]
-    refs = refs[3 + 2 * PIECES :]
+    gate, up = refs[3 : 3 + PIECES], [refs[3 + PIECES].at[expert]]
+    refs = refs[4 + PIECES :]
     sources, out_ref, targets = refs[:count], refs[count], refs[count + 1 : 2 * count + 1]
     loads = start_loads(places, sources, targets, refs[-1])
     units = gate[0].shape[1]
@@ -260,14 +260,14 @@
 def down_kernel(*refs, expert, experts, places):
     count = len(places)
     x_ref, mine, theirs, down_s_ref = refs[:4]
-    down, refs = refs[4 : 4 + PIECES], refs[4 + PIECES :]
+    down, refs = [refs[4].at[expert]], refs[5:]
     before = None
     if expert > 0:
         before, refs = refs[0], refs[1:]
     sources, out_ref, targets = refs[:count], refs[count], refs[count + 1 : 2 * count + 1]
     loads = start_loads(places, sources, targets, refs[-1])
     columns = down[0].shape[1]
-    units = down[0].shape[0] * PIECES
+    units = down[0].shape[0]
     rows, extended = x_ref.shape
     block = min(rows, 64)
     width = 256
@@ -340,7 +340,7 @@
         self.arrays = {"gate": gate, "up": up, "down": down}
         self.waiting = [
             (name, e, piece)
-            for names in (("gate", "up"), ("down",))
+            for names in (("gate",),)
             for e in range(self.experts)
             for name in names
             for piece in range(PIECES)
@@ -408,7 +408,7 @@
         outputs,
         lambda count: [semaphores(count)] + scratch,
         "load",
-        0,
+        1 << 20,
         spreading=1 if scales else 0,
     )
 
@@ -493,12 +493,12 @@
         (part,) = loader.call(
             gate_up_kernel,
             loader.take(LOAD_GATE_UP),
-            [x, gate_s, up_s, *loader.pieces("gate", e), *loader.pieces("up", e)],
-            [VMEM] * (3 + 2 * PIECES),
+            [x, gate_s, up_s, *loader.pieces("gate", e), up_codes],
+            [VMEM] * (4 + PIECES),
             [jax.ShapeDtypeStruct((total_rows, 2 * units), jnp.bfloat16)],
             lambda count: [semaphores(count)],
             "gate_up",
-            8 << 20,
+            2 << 20,
             expert=e,
         )
         parts.append((part, swap(part, "sub", 1)))
@@ -506,15 +506,12 @@
     carried = None
     for e in range(experts):
         last = e == experts - 1
-        missing = loader.missing(e, ("down",))
-        if missing:
-            load_more(loader, loader.take(missing), parts[-1][0], [])
         before = [] if carried is None else [carried]
         (carried,) = loader.call(
             down_kernel,
             loader.take(LOAD_DOWN),
-            [gathered, *parts[e], down_s, *loader.pieces("down", e), *before],
-            [VMEM] * (4 + PIECES + len(before)),
+            [gathered, *parts[e], down_s, down_codes, *before],
+            [VMEM] * (5 + len(before)),
             [
                 jax.ShapeDtypeStruct(
                     (total_rows, half), jnp.bfloat16 if last else jnp.float32

time: 46.6 us -> 44.3 us (0.951)
  Pallas kernels: 20.9 us -> 14.5 us
  waiting for transfers between devices: 12.8 us -> 16.4 us
  local copies, waits for them, and re-layouts: 0.07 us -> 0.58 us
    pallas_call x8 -> x7, Pallas kernels: 20.3 us -> 13.8 us  [call(): pl.pallas_call(functools.partial(kernel, places=tuple(((e, p) for _, e, p...]
    ppermute x10, waiting for transfers between devices: 12.8 us -> 16.4 us  [swap(): return lax.ppermute(x, axis, [(i, i ^ bit) for i in range(count)])]
    unnamed x3 -> x15, local copies, waits for them, and re-layouts: 0.02 us -> 0.54 us
  transfers between devices with their start and end apart: 10 -> 10, of which waited for: 7 -> 7; matrix products, arithmetic and copies ran while one was open for 0% -> 0% of each run, Pallas kernels for 29% -> 18%
where the time goes in v3:
time: 44.3 us; the launch traced here: 44.1 us
  waiting for transfers between devices  16.4 us (37%)
  Pallas kernels  14.5 us (33%)
  starting transfers between devices  12.4 us (28%)
  local copies, waits for them, and re-layouts  0.58 us (1%)
    ppermute x10, waiting for transfers between devices, swap(): return lax.ppermute(x, axis, [(i, i ^ bit) for i in range(count)])  16.4 us
    pallas_call x7, Pallas kernels, call(): pl.pallas_call(functools.partial(kernel, places=tuple(((e, p) for _, e, p...  13.8 us
    ppermute x10, starting transfers between devices, swap(): return lax.ppermute(x, axis, [(i, i ^ bit) for i in range(count)])  12.4 us
  transfers between devices with their start and end apart: 10, of which 7 were waited for; matrix products, arithmetic and copies ran while one was open for 0% of the time, Pallas kernels for 18%

profile of v3, /device:TPU:0, one launch (start us, length us, event | category | flops | bytes accessed | tf_op | source)
XLA Modules:
  0.0 44.1 jit_solution(6669246731005910668)
XLA Ops:
  0.0 2.7 %attend.1 = (bf16[8,1664]{1,0:T(8,128)(2,1)S(1)}, bf16[8,1664]{1,0:T(8,128)(2,1)S(1)}, f32[4,3072]{1,0:T(4,128)S(1)}, bf16[768,2048]{1,0:T(8,128)(2,1)S(1)}) custom-call(bf16[4,3072]{1,0:T(4,128)(2,1)} %refs_0_.1, bf16[4,1024]{1,0:T(4,128)(2,1)} %refs_1_.2, bf16[4,1024]{1,0:T(4,128)(2,1)} %refs_2_.1, s32[4]{0:T(128)} %refs_3_.1, ...), custom_call_target="tpu_custom_call" | custom-call | bytes 7340032 | tf_op jit(solution)/shard_map/attend/pallas_call | solution.py:368
  2.7 0.5 %collective-permute-start = (bf16[8,1664]{1,0:T(8,128)(2,1)S(1)}, bf16[8,1664]{1,0:T(8,128)(2,1)S(1)}, u32[]{:S(2)}, u32[]{:S(2)}) collective-permute-start(bf16[8,1664]{1,0:T(8,128)(2,1)S(1)} %get-tuple-element.20), channel_id=1, source_target_pairs={{0,1},{1,0},{2,3},{3,2},{4,5},{5,4},{6,7},{7,6},{8,9},{9,8},{10,11... | collective-permute-start | bytes 79880 | tf_op jit(solution)/shard_map/ppermute | solution.py:326
  3.2 0.9 %collective-permute-done = bf16[8,1664]{1,0:T(8,128)(2,1)S(1)} collective-permute-done((bf16[8,1664]{1,0:T(8,128)(2,1)S(1)}, bf16[8,1664]{1,0:T(8,128)(2,1)S(1)}, u32[]{:S(2)}, u32[]{:S(2)}) %collective-permute-start) | collective-permute-done | bytes 26656 | tf_op jit(solution)/shard_map/ppermute | solution.py:326
  4.1 3.0 %collective-permute-start.1 = (bf16[8,1664]{1,0:T(8,128)(2,1)S(1)}, bf16[8,1664]{1,0:T(8,128)(2,1)S(1)}, u32[]{:S(2)}, u32[]{:S(2)}) collective-permute-start(bf16[8,1664]{1,0:T(8,128)(2,1)S(1)} %add.12.refs_0_), channel_id=1, source_target_pairs={{0,2},{2,0},{4,6},{6,4},{1,3},{3,1},{5,7},{7,5},{8,10},{10,8},{12,... | collective-permute-start | bytes 79880 | tf_op jit(solution)/shard_map/ppermute | solution.py:326
  7.1 3.3 %load.2 = (bf16[8,1664]{1,0:T(8,128)(2,1)S(1)}, f32[2,12,2048]{2,1,0:T(8,128)S(1)}, f32[2,12,2048]{2,1,0:T(8,128)S(1)}, f32[2,16,1536]{2,1,0:T(8,128)S(1)}, bf16...) custom-call(bf16[8,1664]{1,0:T(8,128)(2,1)S(1)} %add.12.refs_0_, f32[12,2,16]{2,1,0:T(2,128)} %bitcast.11, ...), custom_call_target="tpu_custom_call" | custom-call | bytes 7340032 | tf_op jit(solution)/shard_map/load/pallas_call | solution.py:368
  10.4 0.0 collective-permute-done.1
  10.4 0.0 slice-start.5
  10.4 2.7 %collective-permute-start.2 = (bf16[16,1664]{1,0:T(8,128)(2,1)S(1)}, bf16[16,1664]{1,0:T(8,128)(2,1)S(1)}, u32[]{:S(2)}, u32[]{:S(2)}) collective-permute-start(bf16[16,1664]{1,0:T(8,128)(2,1)S(1)} %constant_dynamic-update-slice_fusion.refs_0_), channel_id=1, source_target_pairs={{0,4},{2,6},{4,0},{6,2},{1,5},{3,7},{5,1},{7,3},{8,12},{10,14},{12... | collective-permute-start | bytes 159752 | tf_op jit(solution)/shard_map/ppermute | solution.py:326
  13.0 1.9 %load.3 = (bf16[16,1664]{1,0:T(8,128)(2,1)S(1)}, bf16[768,2048]{1,0:T(8,128)(2,1)S(1)}) custom-call(bf16[16,1664]{1,0:T(8,128)(2,1)S(1)} %constant_dynamic-update-slice_fusion.refs_0_, bf16[2,1536,2048]{2,1,0:T(8,128)(2,1)} %refs_1_.3), custom_call_target="tpu_custom_call" | custom-call | bytes 4194304 | tf_op jit(solution)/shard_map/load/pallas_call | solution.py:368
  15.0 1.0 %collective-permute-done.2 = bf16[16,1664]{1,0:T(8,128)(2,1)S(1)} collective-permute-done((bf16[16,1664]{1,0:T(8,128)(2,1)S(1)}, bf16[16,1664]{1,0:T(8,128)(2,1)S(1)}, u32[]{:S(2)}, u32[]{:S(2)}) %collective-permute-start.2) | collective-permute-done | bytes 53280 | tf_op jit(solution)/shard_map/ppermute | solution.py:326
  16.0 1.6 %collective-permute-start.3 = (bf16[32,1664]{1,0:T(8,128)(2,1)S(1)}, bf16[32,1664]{1,0:T(8,128)(2,1)S(1)}, u32[]{:S(2)}, u32[]{:S(2)}) collective-permute-start(bf16[32,1664]{1,0:T(8,128)(2,1)S(1)} %pad_maximum_fusion), channel_id=1, source_target_pairs={{0,8},{8,0},{1,9},{9,1},{2,10},{10,2},{3,11},{11,3},{4,12},{12,4},... | collective-permute-start | bytes 319496 | tf_op jit(solution)/shard_map/ppermute | solution.py:326
  17.6 3.2 %collective-permute-done.3 = bf16[32,1664]{1,0:T(8,128)(2,1)S(1)} collective-permute-done((bf16[32,1664]{1,0:T(8,128)(2,1)S(1)}, bf16[32,1664]{1,0:T(8,128)(2,1)S(1)}, u32[]{:S(2)}, u32[]{:S(2)}) %collective-permute-start.3) | collective-permute-done | bytes 106528 | tf_op jit(solution)/shard_map/ppermute | solution.py:326
  20.8 0.0 slice-start
  20.8 0.0 slice-start.1
  20.8 1.9 %gate_up.2.refs_1_ = bf16[64,4096]{1,0:T(8,128)(2,1)S(1)} custom-call(bf16[64,1664]{1,0:T(8,128)(2,1)S(1)} %constant_dynamic-update-slice_fusion.2.refs_0_, f32[2,12,2048]{2,1,0:T(8,128)S(1)} %get-tuple-element.23.refs_1_, f32[2,12,2048]{2,1,0:T(8,128)S(1)} %get-tuple-element.24.refs_2_, bf16[768,2048]{1,0:T(8,128)(2,1)S(1)} %get-tuple-element.25.refs_3_, ...), custom_call_target="tpu_custom_call" | custom-call | bytes 2097152 | tf_op jit(solution)/shard_map/gate_up/pallas_call | solution.py:368
  22.7 0.1 collective-permute-start.5
  22.8 0.0 slice-start.2
  22.8 1.8 %gate_up.3.refs_1_ = bf16[64,4096]{1,0:T(8,128)(2,1)S(1)} custom-call(bf16[64,1664]{1,0:T(8,128)(2,1)S(1)} %constant_dynamic-update-slice_fusion.2.refs_0_, f32[2,12,2048]{2,1,0:T(8,128)S(1)} %get-tuple-element.23.refs_1_, f32[2,12,2048]{2,1,0:T(8,128)S(1)} %get-tuple-element.24.refs_2_, bf16[768,2048]{1,0:T(8,128)(2,1)S(1)} %get-tuple-element.28.refs_3_, ...), custom_call_target="tpu_custom_call" | custom-call | bytes 2097152 | tf_op jit(solution)/shard_map/gate_up/pallas_call | solution.py:368
  24.6 0.5 %collective-permute-start.4 = (bf16[64,4096]{1,0:T(8,128)(2,1)S(1)}, bf16[64,4096]{1,0:T(8,128)(2,1)S(1)}, u32[]{:S(2)}, u32[]{:S(2)}) collective-permute-start(bf16[64,4096]{1,0:T(8,128)(2,1)S(1)} %gate_up.3.refs_1_), channel_id=1, source_target_pairs={{0,1},{1,0},{2,3},{3,2},{4,5},{5,4},{6,7},{7,6},{8,9},{9,8},{10,11... | collective-permute-start | bytes 1572872 | tf_op jit(solution)/shard_map/ppermute | solution.py:326
  25.2 0.0 collective-permute-done.5.refs_2_
  25.2 0.5 %slice-done.2 = s8[4194304]{0:T(1024)(128)(4,1)S(1)} async-done(((s8[12582912]{0:T(1024)(128)(4,1)}), s8[4194304]{0:T(1024)(128)(4,1)S(1)}, s32[]{:S(2)}) %slice-start.2) | async-done | bytes 4194328
  25.7 1.1 %down.2.refs_5_ = f32[64,1536]{1,0:T(8,128)S(1)} custom-call(bf16[64,1664]{1,0:T(8,128)(2,1)S(1)} %constant_dynamic-update-slice_fusion.2.refs_0_, bf16[64,4096]{1,0:T(8,128)(2,1)S(1)} %gate_up.2.refs_1_, bf16[64,4096]{1,0:T(8,128)(2,1)S(1)} %collective-permute-done.5.refs_2_, f32[2,16,1536]{2,1,0:T(8,128)S(1)} %get-tuple-element.30.refs_3_, ...), custom_call_target="tpu_custom_call" | custom-call | bytes 4194304 | tf_op jit(solution)/shard_map/down/pallas_call | solution.py:368
  26.8 1.1 %down.3 = bf16[64,1536]{1,0:T(8,128)(2,1)S(1)} custom-call(bf16[64,1664]{1,0:T(8,128)(2,1)S(1)} %constant_dynamic-update-slice_fusion.2.refs_0_, bf16[64,4096]{1,0:T(8,128)(2,1)S(1)} %gate_up.3.refs_1_, bf16[64,4096]{1,0:T(8,128)(2,1)S(1)} %collective-permute-done.4.refs_2_, f32[2,16,1536]{2,1,0:T(8,128)S(1)} %get-tuple-element.30.refs_3_, ...), custom_call_target="tpu_custom_call" | custom-call | bytes 4194304 | tf_op jit(solution)/shard_map/down/pallas_call | solution.py:368
  28.0 1.6 %collective-permute-start.6 = (bf16[32,1536]{1,0:T(8,128)(2,1)S(1)}, bf16[32,1536]{1,0:T(8,128)(2,1)S(1)}, u32[]{:S(2)}, u32[]{:S(2)}) collective-permute-start(bf16[32,1536]{1,0:T(8,128)(2,1)S(1)} %slice.25), channel_id=1, source_target_pairs={{0,8},{8,0},{1,9},{9,1},{2,10},{10,2},{3,11},{11,3},{4,12},{12,4},... | collective-permute-start | bytes 294920 | tf_op jit(solution)/shard_map/ppermute | solution.py:326
  29.6 3.4 %collective-permute-done.6 = bf16[32,1536]{1,0:T(8,128)(2,1)S(1)} collective-permute-done((bf16[32,1536]{1,0:T(8,128)(2,1)S(1)}, bf16[32,1536]{1,0:T(8,128)(2,1)S(1)}, u32[]{:S(2)}, u32[]{:S(2)}) %collective-permute-start.6) | collective-permute-done | bytes 98336 | tf_op jit(solution)/shard_map/ppermute | solution.py:326
  33.1 2.2 %collective-permute-start.7 = (bf16[16,1536]{1,0:T(8,128)(2,1)S(1)}, bf16[16,1536]{1,0:T(8,128)(2,1)S(1)}, u32[]{:S(2)}, u32[]{:S(2)}) collective-permute-start(bf16[16,1536]{1,0:T(8,128)(2,1)S(1)} %slice.27), channel_id=1, source_target_pairs={{0,4},{2,6},{4,0},{6,2},{1,5},{3,7},{5,1},{7,3},{8,12},{10,14},{12... | collective-permute-start | bytes 147464 | tf_op jit(solution)/shard_map/ppermute | solution.py:326
  35.3 2.9 %collective-permute-done.7 = bf16[16,1536]{1,0:T(8,128)(2,1)S(1)} collective-permute-done((bf16[16,1536]{1,0:T(8,128)(2,1)S(1)}, bf16[16,1536]{1,0:T(8,128)(2,1)S(1)}, u32[]{:S(2)}, u32[]{:S(2)}) %collective-permute-start.7) | collective-permute-done | bytes 49184 | tf_op jit(solution)/shard_map/ppermute | solution.py:326
  38.3 0.1 collective-permute-start.8
  38.4 3.8 %collective-permute-done.8 = bf16[8,1536]{1,0:T(8,128)(2,1)S(1)} collective-permute-done((bf16[8,1536]{1,0:T(8,128)(2,1)S(1)}, bf16[8,1536]{1,0:T(8,128)(2,1)S(1)}, u32[]{:S(2)}, u32[]{:S(2)}) %collective-permute-start.8) | collective-permute-done | bytes 24608 | tf_op jit(solution)/shard_map/ppermute | solution.py:326
  42.2 0.1 collective-permute-start.9
  42.2 1.2 %collective-permute-done.9.other_ref = bf16[8,1536]{1,0:T(8,128)(2,1)S(1)} collective-permute-done((bf16[8,1536]{1,0:T(8,128)(2,1)S(1)}, bf16[8,1536]{1,0:T(8,128)(2,1)S(1)}, u32[]{:S(2)}, u32[]{:S(2)}) %collective-permute-start.9) | collective-permute-done | bytes 24608 | tf_op jit(solution)/shard_map/ppermute | solution.py:326
  43.4 0.6 %finish.1 = bf16[4,3072]{1,0:T(4,128)(2,1)} custom-call(f32[4,3072]{1,0:T(4,128)S(1)} %get-tuple-element.18.stream_ref, bf16[8,1536]{1,0:T(8,128)(2,1)S(1)} %add_convert_fusion.2.own_ref, bf16[8,1536]{1,0:T(8,128)(2,1)S(1)} %collective-permute-done.9.other_ref), custom_call_target="tpu_custom_call" | custom-call | tf_op jit(solution)/shard_map/finish/pallas_call | solution.py:529
  (23 shorter events, 0.2 us)
Async XLA Ops:
  2.7 1.4 %collective-permute-start = (bf16[8,1664]{1,0:T(8,128)(2,1)S(1)}, bf16[8,1664]{1,0:T(8,128)(2,1)S(1)}, u32[]{:S(2)}, u32[]{:S(2)}) collective-permute-start(bf16[8,1664]{1,0:T(8,128)(2,1)S(1)} %get-tuple-element.20), channel_id=1, source_target_pairs={{0,1},{1,0},{2,3},{3,2},{4,5},{5,4},{6,7},{7,6},{8,9},{9,8},{10,11... | collective-permute-start | bytes 79880 | tf_op jit(solution)/shard_map/ppermute | solution.py:326
  4.1 6.3 %collective-permute-start.1 = (bf16[8,1664]{1,0:T(8,128)(2,1)S(1)}, bf16[8,1664]{1,0:T(8,128)(2,1)S(1)}, u32[]{:S(2)}, u32[]{:S(2)}) collective-permute-start(bf16[8,1664]{1,0:T(8,128)(2,1)S(1)} %add.12.refs_0_), channel_id=1, source_target_pairs={{0,2},{2,0},{4,6},{6,4},{1,3},{3,1},{5,7},{7,5},{8,10},{10,8},{12,... | collective-permute-start | bytes 79880 | tf_op jit(solution)/shard_map/ppermute | solution.py:326
  7.1 13.7 %slice-start.3 = ((s8[12582912]{0:T(1024)(128)(4,1)}), s8[4194304]{0:T(1024)(128)(4,1)S(1)}, s32[]{:S(2)}) async-start(s8[12582912]{0:T(1024)(128)(4,1)} %bitcast.8), calls=%async_computation.3 | async-start | bytes 8388608
  7.1 13.7 %slice-start.4 = ((s8[12582912]{0:T(1024)(128)(4,1)}), s8[4194304]{0:T(1024)(128)(4,1)S(1)}, s32[]{:S(2)}) async-start(s8[12582912]{0:T(1024)(128)(4,1)} %bitcast.8), calls=%async_computation.4 | async-start | bytes 8388608
  10.4 10.4 %slice-start.5 = ((s8[12582912]{0:T(1024)(128)(4,1)}), s8[4194304]{0:T(1024)(128)(4,1)S(1)}, s32[]{:S(2)}) async-start(s8[12582912]{0:T(1024)(128)(4,1)} %bitcast.8), calls=%async_computation.5 | async-start | bytes 8388608
  10.4 5.6 %collective-permute-start.2 = (bf16[16,1664]{1,0:T(8,128)(2,1)S(1)}, bf16[16,1664]{1,0:T(8,128)(2,1)S(1)}, u32[]{:S(2)}, u32[]{:S(2)}) collective-permute-start(bf16[16,1664]{1,0:T(8,128)(2,1)S(1)} %constant_dynamic-update-slice_fusion.refs_0_), channel_id=1, source_target_pairs={{0,4},{2,6},{4,0},{6,2},{1,5},{3,7},{5,1},{7,3},{8,12},{10,14},{12... | collective-permute-start | bytes 159752 | tf_op jit(solution)/shard_map/ppermute | solution.py:326
  16.0 4.8 %collective-permute-start.3 = (bf16[32,1664]{1,0:T(8,128)(2,1)S(1)}, bf16[32,1664]{1,0:T(8,128)(2,1)S(1)}, u32[]{:S(2)}, u32[]{:S(2)}) collective-permute-start(bf16[32,1664]{1,0:T(8,128)(2,1)S(1)} %pad_maximum_fusion), channel_id=1, source_target_pairs={{0,8},{8,0},{1,9},{9,1},{2,10},{10,2},{3,11},{11,3},{4,12},{12,4},... | collective-permute-start | bytes 319496 | tf_op jit(solution)/shard_map/ppermute | solution.py:326
  20.8 4.4 %slice-start = ((s8[12582912]{0:T(1024)(128)(4,1)}), s8[4194304]{0:T(1024)(128)(4,1)S(1)}, s32[]{:S(2)}) async-start(s8[12582912]{0:T(1024)(128)(4,1)} %bitcast.6), calls=%async_computation | async-start | bytes 8388608
  20.8 4.4 %slice-start.1 = ((s8[12582912]{0:T(1024)(128)(4,1)}), s8[4194304]{0:T(1024)(128)(4,1)S(1)}, s32[]{:S(2)}) async-start(s8[12582912]{0:T(1024)(128)(4,1)} %bitcast.6), calls=%async_computation.1 | async-start | bytes 8388608
  22.7 2.5 %collective-permute-start.5 = (bf16[64,4096]{1,0:T(8,128)(2,1)S(1)}, bf16[64,4096]{1,0:T(8,128)(2,1)S(1)}, u32[]{:S(2)}, u32[]{:S(2)}) collective-permute-start(bf16[64,4096]{1,0:T(8,128)(2,1)S(1)} %gate_up.2.refs_1_), channel_id=1, source_target_pairs={{0,1},{1,0},{2,3},{3,2},{4,5},{5,4},{6,7},{7,6},{8,9},{9,8},{10,11... | collective-permute-start | bytes 1572872 | tf_op jit(solution)/shard_map/ppermute | solution.py:326
  22.8 2.9 %slice-start.2 = ((s8[12582912]{0:T(1024)(128)(4,1)}), s8[4194304]{0:T(1024)(128)(4,1)S(1)}, s32[]{:S(2)}) async-start(s8[12582912]{0:T(1024)(128)(4,1)} %bitcast.6), calls=%async_computation.2 | async-start | bytes 8388608
  24.6 2.2 %collective-permute-start.4 = (bf16[64,4096]{1,0:T(8,128)(2,1)S(1)}, bf16[64,4096]{1,0:T(8,128)(2,1)S(1)}, u32[]{:S(2)}, u32[]{:S(2)}) collective-permute-start(bf16[64,4096]{1,0:T(8,128)(2,1)S(1)} %gate_up.3.refs_1_), channel_id=1, source_target_pairs={{0,1},{1,0},{2,3},{3,2},{4,5},{5,4},{6,7},{7,6},{8,9},{9,8},{10,11... | collective-permute-start | bytes 1572872 | tf_op jit(solution)/shard_map/ppermute | solution.py:326
  28.0 5.0 %collective-permute-start.6 = (bf16[32,1536]{1,0:T(8,128)(2,1)S(1)}, bf16[32,1536]{1,0:T(8,128)(2,1)S(1)}, u32[]{:S(2)}, u32[]{:S(2)}) collective-permute-start(bf16[32,1536]{1,0:T(8,128)(2,1)S(1)} %slice.25), channel_id=1, source_target_pairs={{0,8},{8,0},{1,9},{9,1},{2,10},{10,2},{3,11},{11,3},{4,12},{12,4},... | collective-permute-start | bytes 294920 | tf_op jit(solution)/shard_map/ppermute | solution.py:326
  33.1 5.2 %collective-permute-start.7 = (bf16[16,1536]{1,0:T(8,128)(2,1)S(1)}, bf16[16,1536]{1,0:T(8,128)(2,1)S(1)}, u32[]{:S(2)}, u32[]{:S(2)}) collective-permute-start(bf16[16,1536]{1,0:T(8,128)(2,1)S(1)} %slice.27), channel_id=1, source_target_pairs={{0,4},{2,6},{4,0},{6,2},{1,5},{3,7},{5,1},{7,3},{8,12},{10,14},{12... | collective-permute-start | bytes 147464 | tf_op jit(solution)/shard_map/ppermute | solution.py:326
  38.3 3.9 %collective-permute-start.8 = (bf16[8,1536]{1,0:T(8,128)(2,1)S(1)}, bf16[8,1536]{1,0:T(8,128)(2,1)S(1)}, u32[]{:S(2)}, u32[]{:S(2)}) collective-permute-start(bf16[8,1536]{1,0:T(8,128)(2,1)S(1)} %slice.29), channel_id=1, source_target_pairs={{0,2},{2,0},{4,6},{6,4},{1,3},{3,1},{5,7},{7,5},{8,10},{10,8},{12,... | collective-permute-start | bytes 73736 | tf_op jit(solution)/shard_map/ppermute | solution.py:326
  42.2 1.3 %collective-permute-start.9 = (bf16[8,1536]{1,0:T(8,128)(2,1)S(1)}, bf16[8,1536]{1,0:T(8,128)(2,1)S(1)}, u32[]{:S(2)}, u32[]{:S(2)}) collective-permute-start(bf16[8,1536]{1,0:T(8,128)(2,1)S(1)} %add_convert_fusion.2.own_ref), channel_id=1, source_target_pairs={{0,1},{1,0},{2,3},{3,2},{4,5},{5,4},{6,7},{7,6},{8,9},{9,8},{10,11... | collective-permute-start | bytes 73736 | tf_op jit(solution)/shard_map/ppermute | solution.py:326

commit v4 on v3

--- a/solution.py
+++ b/solution.py
@@ -21,7 +21,7 @@
 VMEM_LIMIT = 16 << 20
 
 LOAD_ATTEND = 1
-LOAD_STEP = (2, 1, 0)
+LOAD_STEP = (1, 1, 1)
 LOAD_GATE_UP = 2
 LOAD_DOWN = 1
 WIDTH = 512
@@ -49,9 +49,9 @@
     count = len(places)
     inputs = refs[:10]
     sources = refs[10 : 10 + count]
-    own_ref, other_ref, stream_ref = refs[10 + count : 13 + count]
-    targets = refs[13 + count : 13 + 2 * count]
-    scratch = refs[13 + 2 * count :]
+    x_ref, stream_ref = refs[10 + count : 12 + count]
+    targets = refs[12 + count : 12 + 2 * count]
+    scratch = refs[12 + 2 * count :]
     held = scratch[:10]
     q_scr, nk_scr, nv_scr, att_scr, in_sems, load_sems = scratch[10:]
     copies = [
@@ -76,7 +76,6 @@
     for copy in copies[:4]:
         copy.wait()
     rows, positions, _ = cache_key_ref.shape
-    half = D // 2
     f32 = jnp.float32
     total = KV_HEADS * SLOT
     zeros = jnp.zeros((total, HEAD_DIM), f32)
@@ -155,8 +154,6 @@
             squares = squares + piece * piece
     mean_square = jnp.sum(squares, axis=1, keepdims=True) * (1.0 / D)
     normed = stream_ref[...] * lax.rsqrt(mean_square + 1e-05) * gain_ref[...]
-    first = lax.axis_index("sub") == 0
-    low, high = normed[:, :half], normed[:, half:]
     lane = lax.broadcasted_iota(jnp.int32, (rows, LANES), 1)
     row = lax.broadcasted_iota(jnp.int32, (rows, LANES), 0)
     table = jnp.zeros((rows, LANES), f32)
@@ -164,12 +161,7 @@
         for c in range(2):
             here = jnp.logical_and(row == r, lane == ids_ref[c, r])
             table = jnp.where(here, levels_ref[c, r].astype(f32), table)
-    own = jnp.concatenate([jnp.where(first, low, high), table], axis=1)
-    other = jnp.concatenate([jnp.where(first, high, low), table], axis=1)
-    for ref, value in ((own_ref, own), (other_ref, other)):
-        ref[...] = jnp.concatenate(
-            [jnp.where(first, value, 0.0), jnp.where(first, 0.0, value)], axis=0
-        ).astype(jnp.bfloat16)
+    x_ref[...] = jnp.concatenate([normed, table], axis=1).astype(jnp.bfloat16)
     for load in loads:
         load.wait()
 
@@ -231,21 +223,48 @@
     return total
 
 
+def split_kernel(near_ref, far_ref, kept_ref, sent_ref):
+    half = D // 2
+    first = lax.axis_index("sub") == 0
+    count = near_ref.shape[0]
+    for i, ref in enumerate((near_ref, far_ref)):
+        at = slice(i * count, (i + 1) * count)
+        low, high, table = ref[:, :half], ref[:, half:D], ref[:, D:]
+        kept_ref[at, :half] = jnp.where(first, low, high)
+        sent_ref[at, :half] = jnp.where(first, high, low)
+        kept_ref[at, half:] = table
+        sent_ref[at, half:] = table
+
+
+def chip_rows(kept_ref, other_ref, start, block, columns):
+    first = lax.axis_index("sub") == 0
+    count = kept_ref.shape[0]
+    parts = []
+    while block > 0:
+        core, row = start // count, start % count
+        size = min(block, count - row)
+        at = slice(row, row + size)
+        pair = kept_ref[at, columns], other_ref[at, columns]
+        parts.append(jnp.where(first, pair[core], pair[1 - core]))
+        start, block = start + size, block - size
+    return parts[0] if len(parts) == 1 else jnp.concatenate(parts, axis=0)
+
+
 def gate_up_kernel(*refs, expert, places):
     count = len(places)
-    x_ref, gate_s_ref, up_s_ref = refs[:3]
-    gate, up = refs[3 : 3 + PIECES], [refs[3 + PIECES].at[expert]]
-    refs = refs[4 + PIECES :]
+    kept_ref, other_ref, gate_s_ref, up_s_ref = refs[:4]
+    gate, up = refs[4 : 4 + PIECES], [refs[4 + PIECES].at[expert]]
+    refs = refs[5 + PIECES :]
     sources, out_ref, targets = refs[:count], refs[count], refs[count + 1 : 2 * count + 1]
     loads = start_loads(places, sources, targets, refs[-1])
     units = gate[0].shape[1]
     depth = gate[0].shape[0] * PIECES
-    rows = x_ref.shape[0]
+    rows = 2 * kept_ref.shape[0]
     block = min(rows, 64)
     width = min(units, WIDTH)
     for m in range(rows // block):
         at = slice(m * block, (m + 1) * block)
-        left = x_ref[at, :depth]
+        left = chip_rows(kept_ref, other_ref, m * block, block, slice(0, depth))
         for column in range(0, units, width):
             out_ref[at, column : column + width] = scaled_product(
                 left, gate, gate_s_ref, expert, column, width
@@ -259,23 +278,28 @@
 
 def down_kernel(*refs, expert, experts, places):
     count = len(places)
-    x_ref, mine, theirs, down_s_ref = refs[:4]
-    down, refs = [refs[4].at[expert]], refs[5:]
+    last = expert == experts - 1
+    kept_ref, other_ref, mine, theirs, down_s_ref = refs[:5]
+    down, refs = [refs[5].at[expert]], refs[6:]
     before = None
     if expert > 0:
         before, refs = refs[0], refs[1:]
-    sources, out_ref, targets = refs[:count], refs[count], refs[count + 1 : 2 * count + 1]
-    loads = start_loads(places, sources, targets, refs[-1])
+    sources, refs = refs[:count], refs[count:]
+    outputs, refs = refs[: 1 + last], refs[1 + last :]
+    loads = start_loads(places, sources, refs[:count], refs[count])
+    out_ref = refs[count + 1] if last else outputs[0]
     columns = down[0].shape[1]
     units = down[0].shape[0]
-    rows, extended = x_ref.shape
+    rows, extended = 2 * kept_ref.shape[0], kept_ref.shape[1]
     block = min(rows, 64)
     width = 256
     f32 = jnp.float32
     wanted = lax.axis_index("role") * experts + expert
     for m in range(rows // block):
         at = slice(m * block, (m + 1) * block)
-        levels = x_ref[at, extended - LANES :].astype(f32)
+        levels = chip_rows(
+            kept_ref, other_ref, m * block, block, slice(extended - LANES, extended)
+        ).astype(f32)
         lane = lax.broadcasted_iota(jnp.int32, levels.shape, 1)
         level = jnp.sum(jnp.where(lane == wanted, levels, 0.0), axis=1, keepdims=True)
         share = level / jnp.sum(levels, axis=1, keepdims=True)
@@ -291,43 +315,52 @@
             total = scaled_product(hidden, down, down_s_ref, expert, column, width)
             if before is not None:
                 total = total + before[at, column : column + width]
-            out_ref[at, column : column + width] = total.astype(out_ref.dtype)
+            out_ref[at, column : column + width] = total
+    if last:
+        first = lax.axis_index("sub") == 0
+        low, high = out_ref[: rows // 2, :], out_ref[rows // 2 :, :]
+        outputs[0][...] = jnp.where(first, low, high).astype(jnp.bfloat16)
+        outputs[1][...] = jnp.where(first, high, low).astype(jnp.bfloat16)
     for load in loads:
         load.wait()
 
 
-def finish_kernel(stream_ref, own_ref, other_ref, out_ref):
+def join_kernel(kept_ref, other_ref, near_ref, far_ref):
     half = D // 2
-    rows = stream_ref.shape[0]
     first = lax.axis_index("sub") == 0
-    own, other = (
-        jnp.where(first, pair[:rows], pair[rows:])
-        for pair in (own_ref[...].astype(jnp.float32), other_ref[...].astype(jnp.float32))
-    )
-    out_ref[:, :half] = (stream_ref[:, :half] + jnp.where(first, own, other)).astype(jnp.bfloat16)
-    out_ref[:, half:] = (stream_ref[:, half:] + jnp.where(first, other, own)).astype(jnp.bfloat16)
+    count = near_ref.shape[0]
+    for ref, at in ((near_ref, slice(0, count)), (far_ref, slice(count, 2 * count))):
+        kept, other = kept_ref[at, :], other_ref[at, :]
+        ref[:, :half] = jnp.where(first, kept, other)
+        ref[:, half:] = jnp.where(first, other, kept)
+
+
+def finish_kernel(stream_ref, kept_ref, other_ref, out_ref):
+    f32 = jnp.float32
+    total = stream_ref[...] + (kept_ref[...].astype(f32) + other_ref[...].astype(f32))
+    out_ref[...] = total.astype(jnp.bfloat16)
 
 
 def swap(x, axis, bit):
-    count = lax.axis_size(axis)
-    return lax.ppermute(x, axis, [(i, i ^ bit) for i in range(count)])
+    if axis is None:
+        return lax.ppermute(x, "sub", [(0, 1), (1, 0)])
+    count = 2 * lax.axis_size(axis)
+    return lax.ppermute(x, (axis, "sub"), [(i, i ^ (2 * bit + 1)) for i in range(count)])
 
 
 def bits(axis):
-    return [1 << b for b in range(lax.axis_size(axis).bit_length() - 1)]
-
-
-def add_bf16(a, b):
-    return (a.astype(jnp.float32) + b.astype(jnp.float32)).astype(jnp.bfloat16)
-
-
-def swap(x, axis, bit):
-    count = lax.axis_size(axis)
-    return lax.ppermute(x, axis, [(i, i ^ bit) for i in range(count)])
-
-
-def bits(axis):
-    return [1 << b for b in range(lax.axis_size(axis).bit_length() - 1)]
+    return [1 << b for b in reversed(range(lax.axis_size(axis).bit_length() - 1))]
+
+
+def local_call(kernel, outputs, inputs, name):
+    return pl.pallas_call(
+        kernel,
+        out_shape=outputs,
+        in_specs=[VMEM] * len(inputs),
+        out_specs=jax.tree.map(lambda _: VMEM, outputs),
+        compiler_params=pltpu.CompilerParams(vmem_limit_bytes=VMEM_LIMIT),
+        name=name,
+    )(*inputs)
 
 
 def add_bf16(a, b):
@@ -452,14 +485,13 @@
     held = [
         (pltpu.SMEM if x.dtype == jnp.int32 else pltpu.VMEM)(x.shape, x.dtype) for x in inputs
     ]
-    own, other, stream = loader.call(
+    x, stream = loader.call(
         attend_kernel,
         loader.take(LOAD_ATTEND),
         inputs,
         [ANY] * len(inputs),
         [
-            jax.ShapeDtypeStruct((2 * rows, extended), jnp.bfloat16),
-            jax.ShapeDtypeStruct((2 * rows, extended), jnp.bfloat16),
+            jax.ShapeDtypeStruct((rows, D + LANES), jnp.bfloat16),
             jax.ShapeDtypeStruct((rows, D), jnp.float32),
         ],
         lambda count: held + [stacked] * 4 + [semaphores(len(inputs)), semaphores(count)],
@@ -471,69 +503,68 @@
         up_scales.transpose(1, 0, 2),
         down_scales.transpose(2, 0, 1),
     ]
-    gathered = own + swap(other, "sub", 1)
     steps = [("tp", bit) for bit in bits("tp")] + [("role", bit) for bit in bits("role")]
     spread_scales = None
+    near, far = x, None
     for number, (axis, bit) in enumerate(steps):
-        arriving = swap(gathered, axis, bit)
+        if far is not None:
+            near = jnp.concatenate([near, far], axis=0)
+        far = swap(near, axis, bit)
         taken = loader.take(LOAD_STEP[min(number, len(LOAD_STEP) - 1)])
         if spread_scales is None:
-            gathered, *spread_scales = load_more(loader, taken, gathered, scales)
+            near, *spread_scales = load_more(loader, taken, near, scales)
         elif taken:
-            (gathered,) = load_more(loader, taken, gathered, [])
-        gathered = jnp.concatenate([gathered, arriving], axis=0)
+            (near,) = load_more(loader, taken, near, [])
     gate_s, up_s, down_s = spread_scales
-    total_rows = gathered.shape[0]
+    count = 2 * near.shape[0]
+    piece = jax.ShapeDtypeStruct((count, extended), jnp.bfloat16)
+    kept, sent = local_call(split_kernel, (piece, piece), (near, far), "split")
+    other = swap(sent, None, 0)
     parts = []
-    x = gathered
+    before = other
     for e in range(experts):
-        missing = loader.missing(e, ("gate", "up"))
+        missing = loader.missing(e, ("gate",))
         if missing:
-            (x,) = load_more(loader, loader.take(missing), x, [])
+            (before,) = load_more(loader, loader.take(missing), before, [])
         (part,) = loader.call(
             gate_up_kernel,
             loader.take(LOAD_GATE_UP),
-            [x, gate_s, up_s, *loader.pieces("gate", e), up_codes],
-            [VMEM] * (4 + PIECES),
-            [jax.ShapeDtypeStruct((total_rows, 2 * units), jnp.bfloat16)],
-            lambda count: [semaphores(count)],
+            [kept, before, gate_s, up_s, *loader.pieces("gate", e), up_codes],
+            [VMEM] * (5 + PIECES),
+            [jax.ShapeDtypeStruct((2 * count, 2 * units), jnp.bfloat16)],
+            lambda loads: [semaphores(loads)],
             "gate_up",
             2 << 20,
             expert=e,
         )
-        parts.append((part, swap(part, "sub", 1)))
-        x, _ = lax.optimization_barrier((x, part))
-    carried = None
+        parts.append((part, swap(part, None, 0)))
+        before, _ = lax.optimization_barrier((before, part))
+    carried = []
     for e in range(experts):
         last = e == experts - 1
-        before = [] if carried is None else [carried]
-        (carried,) = loader.call(
+        sums = jax.ShapeDtypeStruct((2 * count, half), jnp.float32)
+        returned = jax.ShapeDtypeStruct((count, half), jnp.bfloat16)
+        carried = loader.call(
             down_kernel,
             loader.take(LOAD_DOWN),
-            [gathered, *parts[e], down_s, down_codes, *before],
-            [VMEM] * (5 + len(before)),
-            [
-                jax.ShapeDtypeStruct(
-                    (total_rows, half), jnp.bfloat16 if last else jnp.float32
-                )
-            ],
-            lambda count: [semaphores(count)],
+            [kept, other, *parts[e], down_s, down_codes, *carried],
+            [VMEM] * (6 + len(carried)),
+            [returned, returned] if last else [sums],
+            lambda loads: [semaphores(loads)] + ([pltpu.VMEM(sums.shape, sums.dtype)] if last else []),
             "down",
             4 << 20,
             expert=e,
             experts=experts,
         )
-    for axis, bit in reversed(steps):
-        kept = carried.shape[0] // 2
-        carried = add_bf16(carried[:kept], swap(carried[kept:], axis, bit))
-    return pl.pallas_call(
-        finish_kernel,
-        out_shape=jax.ShapeDtypeStruct((rows, D), jnp.bfloat16),
-        in_specs=[VMEM] * 3,
-        out_specs=VMEM,
-        compiler_params=pltpu.CompilerParams(vmem_limit_bytes=VMEM_LIMIT),
-        name="finish",
-    )(stream, carried, swap(carried, "sub", 1))
+    kept, sent = carried
+    piece = jax.ShapeDtypeStruct((count // 2, D), jnp.bfloat16)
+    near, far = local_call(join_kernel, (piece, piece), (kept, swap(sent, None, 0)), "join")
+    for axis, bit in reversed(steps[1:]):
+        carried = add_bf16(near, swap(far, axis, bit))
+        middle = carried.shape[0] // 2
+        near, far = carried[:middle], carried[middle:]
+    out = jax.ShapeDtypeStruct((rows, D), jnp.bfloat16)
+    return local_call(finish_kernel, out, (stream, near, swap(far, *steps[0])), "finish")
 
 
 def solution(mesh):

time: 44.3 us -> 41.1 us (0.928)
  waiting for transfers between devices: 16.4 us -> 10.2 us
  Pallas kernels: 14.5 us -> 16.4 us
  starting transfers between devices: 12.4 us -> 13.6 us
    ppermute x10, waiting for transfers between devices: 16.4 us -> 10.2 us  [the longest x6 8.08 us: swap(): lax.ppermute(x, (axis, 'sub'), [(i, i ^ 2 * bit + 1) for i in range(count)])]
    pallas_call x7 -> x8, Pallas kernels: 13.8 us -> 15.7 us  [call(): pl.pallas_call(functools.partial(kernel, places=tuple(((e, p) for _, e, p...]
    ppermute x10, starting transfers between devices: 12.4 us -> 13.6 us  [the longest x6 12.3 us: swap(): lax.ppermute(x, (axis, 'sub'), [(i, i ^ 2 * bit + 1) for i in range(count)])]
  transfers between devices with their start and end apart: 10 -> 10, of which waited for: 7 -> 7; matrix products, arithmetic and copies ran while one was open for 0% -> 0% of each run, Pallas kernels for 18% -> 24%
where the time goes in v4:
time: 41.1 us; the launch traced here: 40.9 us
  Pallas kernels  16.4 us (40%)
  starting transfers between devices  13.6 us (33%)
  waiting for transfers between devices  10.2 us (25%)
    pallas_call x8, Pallas kernels, call(): pl.pallas_call(functools.partial(kernel, places=tuple(((e, p) for _, e, p...  15.7 us
    ppermute x6, starting transfers between devices, swap(): lax.ppermute(x, (axis, 'sub'), [(i, i ^ 2 * bit + 1) for i in range(count)])  12.3 us
    ppermute x6, waiting for transfers between devices, swap(): lax.ppermute(x, (axis, 'sub'), [(i, i ^ 2 * bit + 1) for i in range(count)])  8.08 us
    ppermute x4, waiting for transfers between devices, swap(): return lax.ppermute(x, 'sub', [(0, 1), (1, 0)])  2.15 us
    ppermute x4, starting transfers between devices, swap(): return lax.ppermute(x, 'sub', [(0, 1), (1, 0)])  1.32 us
  transfers between devices with their start and end apart: 10, of which 7 were waited for; matrix products, arithmetic and copies ran while one was open for 0% of the time, Pallas kernels for 24%

profile of v4, /device:TPU:0, one launch (start us, length us, event | category | flops | bytes accessed | tf_op | source)
XLA Modules:
  0.0 40.9 jit_solution(15334609260440878089)
XLA Ops:
  0.0 2.7 %attend.1 = (bf16[4,3200]{1,0:T(4,128)(2,1)S(1)}, f32[4,3072]{1,0:T(4,128)S(1)}, bf16[768,2048]{1,0:T(8,128)(2,1)S(1)}) custom-call(bf16[4,3072]{1,0:T(4,128)(2,1)} %refs_0_.1, bf16[4,1024]{1,0:T(4,128)(2,1)} %refs_1_.3, bf16[4,1024]{1,0:T(4,128)(2,1)} %refs_2_.1, s32[4]{0:T(128)} %refs_3_.1, bf16[4,128,1024]{2,1,0:T(8,128)(2,1)} %refs_4_.2, ...), custom_call_target="tpu_custom_call" | custom-call | bytes 7340032 | tf_op jit(solution)/shard_map/attend/pallas_call | solution.py:401
  2.7 3.5 %collective-permute-start = (bf16[4,3200]{1,0:T(4,128)(2,1)S(1)}, bf16[4,3200]{1,0:T(4,128)(2,1)S(1)}, u32[]{:S(2)}, u32[]{:S(2)}) collective-permute-start(bf16[4,3200]{1,0:T(4,128)(2,1)S(1)} %get-tuple-element.25.refs_0_), channel_id=1, source_target_pairs={{0,5},{1,4},{2,7},{3,6},{4,1},{5,0},{6,3},{7,2},{8,13},{9,12},{10,... | collective-permute-start | bytes 76808 | tf_op jit(solution)/shard_map/ppermute | solution.py:348
  6.2 2.2 %load.3 = (bf16[4,3200]{1,0:T(4,128)(2,1)S(1)}, f32[2,12,2048]{2,1,0:T(8,128)S(1)}, f32[2,12,2048]{2,1,0:T(8,128)S(1)}, f32[2,16,1536]{2,1,0:T(8,128)S(1)}, bf16[768,2048]{1,0:T(8,128)(2,1)S(1)}) custom-call(bf16[4,3200]{1,0:T(4,128)(2,1)S(1)} %get-tuple-element.25.refs_0_, f32[12,2,16]{2,1,0:T(2,128)} %bitcast.11, f32[12,2,16]{2,1,0:T(2,128)} %bitcast.12, ...), custom_call_target="tpu_custom_call" | custom-call | bytes 4194304 | tf_op jit(solution)/shard_map/load/pallas_call | solution.py:401
  8.5 0.0 collective-permute-done
  8.5 1.9 %collective-permute-start.1 = (bf16[8,3200]{1,0:T(8,128)(2,1)S(1)}, bf16[8,3200]{1,0:T(8,128)(2,1)S(1)}, u32[]{:S(2)}, u32[]{:S(2)}) collective-permute-start(bf16[8,3200]{1,0:T(8,128)(2,1)S(1)} %pad_maximum_fusion.refs_0_), channel_id=1, source_target_pairs={{0,3},{1,2},{2,1},{3,0},{4,7},{5,6},{6,5},{7,4},{8,11},{9,10},{10,... | collective-permute-start | bytes 153608 | tf_op jit(solution)/shard_map/ppermute | solution.py:348
  10.4 2.0 %load.4 = (bf16[8,3200]{1,0:T(8,128)(2,1)S(1)}, bf16[768,2048]{1,0:T(8,128)(2,1)S(1)}) custom-call(bf16[8,3200]{1,0:T(8,128)(2,1)S(1)} %pad_maximum_fusion.refs_0_, bf16[2,1536,2048]{2,1,0:T(8,128)(2,1)} %refs_1_.5), custom_call_target="tpu_custom_call" | custom-call | bytes 4194304 | tf_op jit(solution)/shard_map/load/pallas_call | solution.py:401
  12.5 0.0 collective-permute-done.1
  12.5 0.0 slice-start.5
  12.5 1.4 %collective-permute-start.2 = (bf16[16,3200]{1,0:T(8,128)(2,1)S(1)}, bf16[16,3200]{1,0:T(8,128)(2,1)S(1)}, u32[]{:S(2)}, u32[]{:S(2)}) collective-permute-start(bf16[16,3200]{1,0:T(8,128)(2,1)S(1)} %constant_dynamic-update-slice_fusion.refs_0_), channel_id=1, source_target_pairs={{0,9},{1,8},{8,1},{9,0},{2,11},{3,10},{10,3},{11,2},{4,13},{5,12},... | collective-permute-start | bytes 307208 | tf_op jit(solution)/shard_map/ppermute | solution.py:348
  14.0 2.7 %load.5 = (bf16[16,3200]{1,0:T(8,128)(2,1)S(1)}, bf16[768,2048]{1,0:T(8,128)(2,1)S(1)}) custom-call(bf16[16,3200]{1,0:T(8,128)(2,1)S(1)} %constant_dynamic-update-slice_fusion.refs_0_, bf16[2,1536,2048]{2,1,0:T(8,128)(2,1)} %refs_1_.5), custom_call_target="tpu_custom_call" | custom-call | bytes 4194304 | tf_op jit(solution)/shard_map/load/pallas_call | solution.py:401
  16.6 0.8 %collective-permute-done.2.far_ref = bf16[16,3200]{1,0:T(8,128)(2,1)S(1)} collective-permute-done((bf16[16,3200]{1,0:T(8,128)(2,1)S(1)}, bf16[16,3200]{1,0:T(8,128)(2,1)S(1)}, u32[]{:S(2)}, u32[]{:S(2)}) %collective-permute-start.2) | collective-permute-done | bytes 102432 | tf_op jit(solution)/shard_map/ppermute | solution.py:348
  17.5 0.2 collective-permute-start.3
  17.7 1.1 %collective-permute-done.3.refs_1_ = bf16[32,1664]{1,0:T(8,128)(2,1)S(1)} collective-permute-done((bf16[32,1664]{1,0:T(8,128)(2,1)S(1)}, bf16[32,1664]{1,0:T(8,128)(2,1)S(1)}, u32[]{:S(2)}, u32[]{:S(2)}) %collective-permute-start.3) | collective-permute-done | bytes 106528 | tf_op jit(solution)/shard_map/ppermute | solution.py:346
  18.9 0.0 slice-start
  18.9 0.0 slice-start.1
  18.9 1.9 %gate_up.2.refs_2_ = bf16[64,4096]{1,0:T(8,128)(2,1)S(1)} custom-call(bf16[32,1664]{1,0:T(8,128)(2,1)S(1)} %get-tuple-element.29.refs_0_, bf16[32,1664]{1,0:T(8,128)(2,1)S(1)} %collective-permute-done.3.refs_1_, f32[2,12,2048]{2,1,0:T(8,128)S(1)} %get-tuple-element.31.refs_2_, f32[2,12,2048]{2,1,0:T(8,128)S(1)} %get-tuple-element.32.refs_3_, ...), custom_call_target="tpu_custom_call" | custom-call | bytes 2097152 | tf_op jit(solution)/shard_map/gate_up/pallas_call | solution.py:401
  20.8 0.2 collective-permute-start.5
  21.0 1.9 %gate_up.3.refs_2_ = bf16[64,4096]{1,0:T(8,128)(2,1)S(1)} custom-call(bf16[32,1664]{1,0:T(8,128)(2,1)S(1)} %get-tuple-element.29.refs_0_, bf16[32,1664]{1,0:T(8,128)(2,1)S(1)} %collective-permute-done.3.refs_1_, f32[2,12,2048]{2,1,0:T(8,128)S(1)} %get-tuple-element.31.refs_2_, f32[2,12,2048]{2,1,0:T(8,128)S(1)} %get-tuple-element.32.refs_3_, ...), custom_call_target="tpu_custom_call" | custom-call | bytes 2097152 | tf_op jit(solution)/shard_map/gate_up/pallas_call | solution.py:401
  23.0 0.4 %collective-permute-start.4 = (bf16[64,4096]{1,0:T(8,128)(2,1)S(1)}, bf16[64,4096]{1,0:T(8,128)(2,1)S(1)}, u32[]{:S(2)}, u32[]{:S(2)}) collective-permute-start(bf16[64,4096]{1,0:T(8,128)(2,1)S(1)} %gate_up.3.refs_2_), channel_id=1, source_target_pairs={{0,1},{1,0},{2,3},{3,2},{4,5},{5,4},{6,7},{7,6},{8,9},{9,8},{10,11... | collective-permute-start | bytes 1572872 | tf_op jit(solution)/shard_map/ppermute | solution.py:346
  23.4 0.3 slice-done.2
  23.7 1.1 %down.2.refs_6_ = f32[64,1536]{1,0:T(8,128)S(1)} custom-call(bf16[32,1664]{1,0:T(8,128)(2,1)S(1)} %get-tuple-element.29.refs_0_, bf16[32,1664]{1,0:T(8,128)(2,1)S(1)} %collective-permute-done.3.refs_1_, bf16[64,4096]{1,0:T(8,128)(2,1)S(1)} %gate_up.2.refs_2_, bf16[64,4096]{1,0:T(8,128)(2,1)S(1)} %collective-permute-done.5.refs_3_, ...), custom_call_target="tpu_custom_call" | custom-call | bytes 4194304 | tf_op jit(solution)/shard_map/down/pallas_call | solution.py:401
  24.9 0.1 collective-permute-done.4.refs_3_
  24.9 1.1 %down.3 = (bf16[32,1536]{1,0:T(8,128)(2,1)S(1)}, bf16[32,1536]{1,0:T(8,128)(2,1)S(1)}) custom-call(bf16[32,1664]{1,0:T(8,128)(2,1)S(1)} %get-tuple-element.29.refs_0_, bf16[32,1664]{1,0:T(8,128)(2,1)S(1)} %collective-permute-done.3.refs_1_, bf16[64,4096]{1,0:T(8,128)(2,1)S(1)} %gate_up.3.refs_2_, bf16[64,4096]{1,0:T(8,128)(2,1)S(1)} %collective-permute-done.4.refs_3_, ...), custom_call_target="tpu_custom_call" | custom-call | bytes 4194304 | tf_op jit(solution)/shard_map/down/pallas_call | solution.py:401
  26.1 0.4 %collective-permute-start.6 = (bf16[32,1536]{1,0:T(8,128)(2,1)S(1)}, bf16[32,1536]{1,0:T(8,128)(2,1)S(1)}, u32[]{:S(2)}, u32[]{:S(2)}) collective-permute-start(bf16[32,1536]{1,0:T(8,128)(2,1)S(1)} %get-tuple-element.40), channel_id=1, source_target_pairs={{0,1},{1,0},{2,3},{3,2},{4,5},{5,4},{6,7},{7,6},{8,9},{9,8},{10,11... | collective-permute-start | bytes 294920 | tf_op jit(solution)/shard_map/ppermute | solution.py:346
  26.5 0.9 %collective-permute-done.6.other_ref = bf16[32,1536]{1,0:T(8,128)(2,1)S(1)} collective-permute-done((bf16[32,1536]{1,0:T(8,128)(2,1)S(1)}, bf16[32,1536]{1,0:T(8,128)(2,1)S(1)}, u32[]{:S(2)}, u32[]{:S(2)}) %collective-permute-start.6) | collective-permute-done | bytes 98336 | tf_op jit(solution)/shard_map/ppermute | solution.py:346
  27.5 1.5 %collective-permute-start.7 = (bf16[16,3072]{1,0:T(8,128)(2,1)S(1)}, bf16[16,3072]{1,0:T(8,128)(2,1)S(1)}, u32[]{:S(2)}, u32[]{:S(2)}) collective-permute-start(bf16[16,3072]{1,0:T(8,128)(2,1)S(1)} %get-tuple-element.42), channel_id=1, source_target_pairs={{0,9},{1,8},{8,1},{9,0},{2,11},{3,10},{10,3},{11,2},{4,13},{5,12},... | collective-permute-start | bytes 294920 | tf_op jit(solution)/shard_map/ppermute | solution.py:348
  29.0 3.2 %collective-permute-done.7 = bf16[16,3072]{1,0:T(8,128)(2,1)S(1)} collective-permute-done((bf16[16,3072]{1,0:T(8,128)(2,1)S(1)}, bf16[16,3072]{1,0:T(8,128)(2,1)S(1)}, u32[]{:S(2)}, u32[]{:S(2)}) %collective-permute-start.7) | collective-permute-done | bytes 98336 | tf_op jit(solution)/shard_map/ppermute | solution.py:348
  32.2 1.2 %collective-permute-start.8 = (bf16[8,3072]{1,0:T(8,128)(2,1)S(1)}, bf16[8,3072]{1,0:T(8,128)(2,1)S(1)}, u32[]{:S(2)}, u32[]{:S(2)}) collective-permute-start(bf16[8,3072]{1,0:T(8,128)(2,1)S(1)} %slice.17), channel_id=1, source_target_pairs={{0,3},{1,2},{2,1},{3,0},{4,7},{5,6},{6,5},{7,4},{8,11},{9,10},{10,... | collective-permute-start | bytes 147464 | tf_op jit(solution)/shard_map/ppermute | solution.py:348
  33.4 2.6 %collective-permute-done.8 = bf16[8,3072]{1,0:T(8,128)(2,1)S(1)} collective-permute-done((bf16[8,3072]{1,0:T(8,128)(2,1)S(1)}, bf16[8,3072]{1,0:T(8,128)(2,1)S(1)}, u32[]{:S(2)}, u32[]{:S(2)}) %collective-permute-start.8) | collective-permute-done | bytes 49184 | tf_op jit(solution)/shard_map/ppermute | solution.py:348
  36.0 2.7 %collective-permute-start.9 = (bf16[4,3072]{1,0:T(4,128)(2,1)S(1)}, bf16[4,3072]{1,0:T(4,128)(2,1)S(1)}, u32[]{:S(2)}, u32[]{:S(2)}) collective-permute-start(bf16[4,3072]{1,0:T(4,128)(2,1)S(1)} %get-tuple-element.43), channel_id=1, source_target_pairs={{0,5},{1,4},{2,7},{3,6},{4,1},{5,0},{6,3},{7,2},{8,13},{9,12},{10,... | collective-permute-start | bytes 73736 | tf_op jit(solution)/shard_map/ppermute | solution.py:348
  38.7 1.5 %collective-permute-done.9.other_ref = bf16[4,3072]{1,0:T(4,128)(2,1)S(1)} collective-permute-done((bf16[4,3072]{1,0:T(4,128)(2,1)S(1)}, bf16[4,3072]{1,0:T(4,128)(2,1)S(1)}, u32[]{:S(2)}, u32[]{:S(2)}) %collective-permute-start.9) | collective-permute-done | bytes 24608 | tf_op jit(solution)/shard_map/ppermute | solution.py:348
  40.2 0.6 %finish.1 = bf16[4,3072]{1,0:T(4,128)(2,1)} custom-call(f32[4,3072]{1,0:T(4,128)S(1)} %get-tuple-element.24.stream_ref, bf16[4,3072]{1,0:T(4,128)(2,1)S(1)} %get-tuple-element.44.kept_ref, bf16[4,3072]{1,0:T(4,128)(2,1)S(1)} %collective-permute-done.9.other_ref), custom_call_target="tpu_custom_call" | custom-call | tf_op jit(solution)/shard_map/finish/pallas_call | solution.py:356
  (20 shorter events, 0.2 us)
Async XLA Ops:
  2.7 5.7 %collective-permute-start = (bf16[4,3200]{1,0:T(4,128)(2,1)S(1)}, bf16[4,3200]{1,0:T(4,128)(2,1)S(1)}, u32[]{:S(2)}, u32[]{:S(2)}) collective-permute-start(bf16[4,3200]{1,0:T(4,128)(2,1)S(1)} %get-tuple-element.25.refs_0_), channel_id=1, source_target_pairs={{0,5},{1,4},{2,7},{3,6},{4,1},{5,0},{6,3},{7,2},{8,13},{9,12},{10,... | collective-permute-start | bytes 76808 | tf_op jit(solution)/shard_map/ppermute | solution.py:348
  8.5 4.0 %collective-permute-start.1 = (bf16[8,3200]{1,0:T(8,128)(2,1)S(1)}, bf16[8,3200]{1,0:T(8,128)(2,1)S(1)}, u32[]{:S(2)}, u32[]{:S(2)}) collective-permute-start(bf16[8,3200]{1,0:T(8,128)(2,1)S(1)} %pad_maximum_fusion.refs_0_), channel_id=1, source_target_pairs={{0,3},{1,2},{2,1},{3,0},{4,7},{5,6},{6,5},{7,4},{8,11},{9,10},{10,... | collective-permute-start | bytes 153608 | tf_op jit(solution)/shard_map/ppermute | solution.py:348
  10.4 8.4 %slice-start.3 = ((s8[12582912]{0:T(1024)(128)(4,1)}), s8[4194304]{0:T(1024)(128)(4,1)S(1)}, s32[]{:S(2)}) async-start(s8[12582912]{0:T(1024)(128)(4,1)} %bitcast.8), calls=%async_computation.3 | async-start | bytes 8388608
  10.4 8.4 %slice-start.4 = ((s8[12582912]{0:T(1024)(128)(4,1)}), s8[4194304]{0:T(1024)(128)(4,1)S(1)}, s32[]{:S(2)}) async-start(s8[12582912]{0:T(1024)(128)(4,1)} %bitcast.8), calls=%async_computation.4 | async-start | bytes 8388608
  12.5 6.3 %slice-start.5 = ((s8[12582912]{0:T(1024)(128)(4,1)}), s8[4194304]{0:T(1024)(128)(4,1)S(1)}, s32[]{:S(2)}) async-start(s8[12582912]{0:T(1024)(128)(4,1)} %bitcast.8), calls=%async_computation.5 | async-start | bytes 8388608
  12.5 4.9 %collective-permute-start.2 = (bf16[16,3200]{1,0:T(8,128)(2,1)S(1)}, bf16[16,3200]{1,0:T(8,128)(2,1)S(1)}, u32[]{:S(2)}, u32[]{:S(2)}) collective-permute-start(bf16[16,3200]{1,0:T(8,128)(2,1)S(1)} %constant_dynamic-update-slice_fusion.refs_0_), channel_id=1, source_target_pairs={{0,9},{1,8},{8,1},{9,0},{2,11},{3,10},{10,3},{11,2},{4,13},{5,12},... | collective-permute-start | bytes 307208 | tf_op jit(solution)/shard_map/ppermute | solution.py:348
  17.5 1.4 %collective-permute-start.3 = (bf16[32,1664]{1,0:T(8,128)(2,1)S(1)}, bf16[32,1664]{1,0:T(8,128)(2,1)S(1)}, u32[]{:S(2)}, u32[]{:S(2)}) collective-permute-start(bf16[32,1664]{1,0:T(8,128)(2,1)S(1)} %get-tuple-element.30), channel_id=1, source_target_pairs={{0,1},{1,0},{2,3},{3,2},{4,5},{5,4},{6,7},{7,6},{8,9},{9,8},{10,11... | collective-permute-start | bytes 319496 | tf_op jit(solution)/shard_map/ppermute | solution.py:346
  18.9 4.5 %slice-start = ((s8[12582912]{0:T(1024)(128)(4,1)}), s8[4194304]{0:T(1024)(128)(4,1)S(1)}, s32[]{:S(2)}) async-start(s8[12582912]{0:T(1024)(128)(4,1)} %bitcast.6), calls=%async_computation | async-start | bytes 8388608
  18.9 4.5 %slice-start.1 = ((s8[12582912]{0:T(1024)(128)(4,1)}), s8[4194304]{0:T(1024)(128)(4,1)S(1)}, s32[]{:S(2)}) async-start(s8[12582912]{0:T(1024)(128)(4,1)} %bitcast.6), calls=%async_computation.1 | async-start | bytes 8388608
  20.8 2.6 %collective-permute-start.5 = (bf16[64,4096]{1,0:T(8,128)(2,1)S(1)}, bf16[64,4096]{1,0:T(8,128)(2,1)S(1)}, u32[]{:S(2)}, u32[]{:S(2)}) collective-permute-start(bf16[64,4096]{1,0:T(8,128)(2,1)S(1)} %gate_up.2.refs_2_), channel_id=1, source_target_pairs={{0,1},{1,0},{2,3},{3,2},{4,5},{5,4},{6,7},{7,6},{8,9},{9,8},{10,11... | collective-permute-start | bytes 1572872 | tf_op jit(solution)/shard_map/ppermute | solution.py:346
  21.0 2.7 %slice-start.2 = ((s8[12582912]{0:T(1024)(128)(4,1)}), s8[4194304]{0:T(1024)(128)(4,1)S(1)}, s32[]{:S(2)}) async-start(s8[12582912]{0:T(1024)(128)(4,1)} %bitcast.6), calls=%async_computation.2 | async-start | bytes 8388608
  23.0 2.0 %collective-permute-start.4 = (bf16[64,4096]{1,0:T(8,128)(2,1)S(1)}, bf16[64,4096]{1,0:T(8,128)(2,1)S(1)}, u32[]{:S(2)}, u32[]{:S(2)}) collective-permute-start(bf16[64,4096]{1,0:T(8,128)(2,1)S(1)} %gate_up.3.refs_2_), channel_id=1, source_target_pairs={{0,1},{1,0},{2,3},{3,2},{4,5},{5,4},{6,7},{7,6},{8,9},{9,8},{10,11... | collective-permute-start | bytes 1572872 | tf_op jit(solution)/shard_map/ppermute | solution.py:346
  26.1 1.4 %collective-permute-start.6 = (bf16[32,1536]{1,0:T(8,128)(2,1)S(1)}, bf16[32,1536]{1,0:T(8,128)(2,1)S(1)}, u32[]{:S(2)}, u32[]{:S(2)}) collective-permute-start(bf16[32,1536]{1,0:T(8,128)(2,1)S(1)} %get-tuple-element.40), channel_id=1, source_target_pairs={{0,1},{1,0},{2,3},{3,2},{4,5},{5,4},{6,7},{7,6},{8,9},{9,8},{10,11... | collective-permute-start | bytes 294920 | tf_op jit(solution)/shard_map/ppermute | solution.py:346
  27.5 4.7 %collective-permute-start.7 = (bf16[16,3072]{1,0:T(8,128)(2,1)S(1)}, bf16[16,3072]{1,0:T(8,128)(2,1)S(1)}, u32[]{:S(2)}, u32[]{:S(2)}) collective-permute-start(bf16[16,3072]{1,0:T(8,128)(2,1)S(1)} %get-tuple-element.42), channel_id=1, source_target_pairs={{0,9},{1,8},{8,1},{9,0},{2,11},{3,10},{10,3},{11,2},{4,13},{5,12},... | collective-permute-start | bytes 294920 | tf_op jit(solution)/shard_map/ppermute | solution.py:348
  32.2 3.7 %collective-permute-start.8 = (bf16[8,3072]{1,0:T(8,128)(2,1)S(1)}, bf16[8,3072]{1,0:T(8,128)(2,1)S(1)}, u32[]{:S(2)}, u32[]{:S(2)}) collective-permute-start(bf16[8,3072]{1,0:T(8,128)(2,1)S(1)} %slice.17), channel_id=1, source_target_pairs={{0,3},{1,2},{2,1},{3,0},{4,7},{5,6},{6,5},{7,4},{8,11},{9,10},{10,... | collective-permute-start | bytes 147464 | tf_op jit(solution)/shard_map/ppermute | solution.py:348
  36.0 4.3 %collective-permute-start.9 = (bf16[4,3072]{1,0:T(4,128)(2,1)S(1)}, bf16[4,3072]{1,0:T(4,128)(2,1)S(1)}, u32[]{:S(2)}, u32[]{:S(2)}) collective-permute-start(bf16[4,3072]{1,0:T(4,128)(2,1)S(1)} %get-tuple-element.43), channel_id=1, source_target_pairs={{0,5},{1,4},{2,7},{3,6},{4,1},{5,0},{6,3},{7,2},{8,13},{9,12},{10,... | collective-permute-start | bytes 73736 | tf_op jit(solution)/shard_map/ppermute | solution.py:348

commit v5 on v4

--- a/solution.py
+++ b/solution.py
@@ -21,7 +21,8 @@
 VMEM_LIMIT = 16 << 20
 
 LOAD_ATTEND = 1
-LOAD_STEP = (1, 1, 1)
+LOAD_STEP = (1, 2)
+ORDER = (2, 1, 3)
 LOAD_GATE_UP = 2
 LOAD_DOWN = 1
 WIDTH = 512
@@ -47,16 +48,17 @@
 
 def attend_kernel(*refs, places):
     count = len(places)
-    inputs = refs[:10]
-    sources = refs[10 : 10 + count]
-    x_ref, stream_ref = refs[10 + count : 12 + count]
-    targets = refs[12 + count : 12 + 2 * count]
-    scratch = refs[12 + 2 * count :]
+    inputs = refs[:13]
+    sources = refs[13 : 13 + count]
+    x_ref, stream_ref = refs[13 + count : 15 + count]
+    scales = refs[15 + count : 18 + count]
+    targets = refs[18 + count : 18 + 2 * count]
+    scratch = refs[18 + 2 * count :]
     held = scratch[:10]
     q_scr, nk_scr, nv_scr, att_scr, in_sems, load_sems = scratch[10:]
     copies = [
         pltpu.make_async_copy(source, target, in_sems.at[i])
-        for i, (source, target) in enumerate(zip(inputs, held))
+        for i, (source, target) in enumerate(zip(inputs, (*held, *scales)))
     ]
     for copy in copies:
         copy.start()
@@ -141,7 +143,7 @@
         axis=0,
     )
     att_scr[...] = attended + fresh_prob * nv_scr[...]
-    for copy in copies[6:]:
+    for copy in copies[6:10]:
         copy.wait()
     squares = jnp.zeros((rows, HEAD_DIM), f32)
     for j in range(KV_HEADS):
@@ -162,8 +164,8 @@
             here = jnp.logical_and(row == r, lane == ids_ref[c, r])
             table = jnp.where(here, levels_ref[c, r].astype(f32), table)
     x_ref[...] = jnp.concatenate([normed, table], axis=1).astype(jnp.bfloat16)
-    for load in loads:
-        load.wait()
+    for copy in (*copies[10:], *loads):
+        copy.wait()
 
 
 def spread(scales, columns, dimension):
@@ -191,19 +193,17 @@
     targets, refs = refs[:count], refs[count:]
     load_sems = refs[0]
     loads = start_loads(places, sources, targets, load_sems)
-    if spreading:
-        held, sems = refs[1:4], refs[4]
-        copies = [
-            pltpu.make_async_copy(source, target, sems.at[i])
-            for i, (source, target) in enumerate(zip(scales, held))
-        ]
-        for copy in copies:
-            copy.start()
-        for i, (copy, target, out_ref) in enumerate(zip(copies, held, rows_refs)):
-            copy.wait()
-            experts, _, columns = out_ref.shape
-            for e in range(experts):
-                out_ref[e] = spread(target[:, e, :], columns, 1 if i < 2 else 0)
+    for i, (source, out_ref) in enumerate(zip(scales, rows_refs)):
+        experts, _, columns = out_ref.shape
+        for e in range(experts):
+            table = source[:, e, :]
+            if i == 2:
+                out_ref[e] = spread(table, columns, 0)
+                continue
+            for block in range(columns // QBLOCK):
+                at = slice(block * QBLOCK, (block + 1) * QBLOCK)
+                wide = (table.shape[0], QBLOCK)
+                out_ref[e, :, at] = jnp.broadcast_to(table[:, block : block + 1], wide)
     for load in loads:
         load.wait()
 
@@ -223,11 +223,12 @@
     return total
 
 
-def split_kernel(near_ref, far_ref, kept_ref, sent_ref):
+def split_kernel(*refs):
+    *pieces, kept_ref, sent_ref = refs
     half = D // 2
     first = lax.axis_index("sub") == 0
-    count = near_ref.shape[0]
-    for i, ref in enumerate((near_ref, far_ref)):
+    count = pieces[0].shape[0]
+    for i, ref in enumerate(pieces):
         at = slice(i * count, (i + 1) * count)
         low, high, table = ref[:, :half], ref[:, half:D], ref[:, D:]
         kept_ref[at, :half] = jnp.where(first, low, high)
@@ -325,19 +326,22 @@
         load.wait()
 
 
-def join_kernel(kept_ref, other_ref, near_ref, far_ref):
+def join_kernel(kept_ref, other_ref, *refs):
     half = D // 2
     first = lax.axis_index("sub") == 0
-    count = near_ref.shape[0]
-    for ref, at in ((near_ref, slice(0, count)), (far_ref, slice(count, 2 * count))):
+    count = refs[0].shape[0]
+    for i, ref in enumerate(refs):
+        at = slice(i * count, (i + 1) * count)
         kept, other = kept_ref[at, :], other_ref[at, :]
         ref[:, :half] = jnp.where(first, kept, other)
         ref[:, half:] = jnp.where(first, other, kept)
 
 
-def finish_kernel(stream_ref, kept_ref, other_ref, out_ref):
-    f32 = jnp.float32
-    total = stream_ref[...] + (kept_ref[...].astype(f32) + other_ref[...].astype(f32))
+def finish_kernel(stream_ref, *refs):
+    *pieces, out_ref = refs
+    total = stream_ref[...]
+    for piece in pieces:
+        total = total + piece[...].astype(jnp.float32)
     out_ref[...] = total.astype(jnp.bfloat16)
 
 
@@ -348,8 +352,19 @@
     return lax.ppermute(x, (axis, "sub"), [(i, i ^ (2 * bit + 1)) for i in range(count)])
 
 
-def bits(axis):
-    return [1 << b for b in reversed(range(lax.axis_size(axis).bit_length() - 1))]
+def digits(axis, base):
+    size, unit, rounds = lax.axis_size(axis), 1, []
+    while unit < size:
+        span = min(base, size // unit)
+        order = ORDER if span == 4 else (1,)
+        rounds.append((axis, tuple(unit * i for i in order)))
+        unit *= span
+    return rounds
+
+
+def returned_pieces(pieces, axis, offsets):
+    near, *far = pieces
+    return [near, *[swap(piece, axis, offset) for piece, offset in zip(far, offsets)]]
 
 
 def local_call(kernel, outputs, inputs, name):
@@ -363,8 +378,9 @@
     )(*inputs)
 
 
-def add_bf16(a, b):
-    return (a.astype(jnp.float32) + b.astype(jnp.float32)).astype(jnp.bfloat16)
+def add_bf16(pieces):
+    total = sum((piece.astype(jnp.float32) for piece in pieces[1:]), pieces[0].astype(jnp.float32))
+    return total.astype(jnp.bfloat16)
 
 
 class Loader:
@@ -423,7 +439,7 @@
 
 
 def load_more(loader, taken, after, scales):
-    outputs, scratch = [jax.ShapeDtypeStruct(after.shape, after.dtype)], []
+    outputs = [jax.ShapeDtypeStruct(after.shape, after.dtype)]
     if scales:
         experts, depth, units = loader.arrays["gate"].shape
         columns = loader.arrays["down"].shape[2]
@@ -432,14 +448,13 @@
             jax.ShapeDtypeStruct((experts, depth // QBLOCK, units), jnp.float32),
             jax.ShapeDtypeStruct((experts, units // QBLOCK, columns), jnp.float32),
         ]
-        scratch = [pltpu.VMEM(s.shape, s.dtype) for s in scales] + [semaphores(3)]
     return loader.call(
         load_kernel,
         taken,
         [after, *scales],
-        [VMEM] + [ANY] * len(scales),
+        [VMEM] * (1 + len(scales)),
         outputs,
-        lambda count: [semaphores(count)] + scratch,
+        lambda count: [semaphores(count)],
         "load",
         1 << 20,
         spreading=1 if scales else 0,
@@ -481,44 +496,45 @@
         expert_ids.T,
         gate_levels.T,
     ]
-    stacked = pltpu.VMEM((KV_HEADS * SLOT, HEAD_DIM), jnp.float32)
-    held = [
-        (pltpu.SMEM if x.dtype == jnp.int32 else pltpu.VMEM)(x.shape, x.dtype) for x in inputs
-    ]
-    x, stream = loader.call(
-        attend_kernel,
-        loader.take(LOAD_ATTEND),
-        inputs,
-        [ANY] * len(inputs),
-        [
-            jax.ShapeDtypeStruct((rows, D + LANES), jnp.bfloat16),
-            jax.ShapeDtypeStruct((rows, D), jnp.float32),
-        ],
-        lambda count: held + [stacked] * 4 + [semaphores(len(inputs)), semaphores(count)],
-        "attend",
-        4 << 20,
-    )
     scales = [
         gate_scales.transpose(1, 0, 2),
         up_scales.transpose(1, 0, 2),
         down_scales.transpose(2, 0, 1),
     ]
-    steps = [("tp", bit) for bit in bits("tp")] + [("role", bit) for bit in bits("role")]
+    stacked = pltpu.VMEM((KV_HEADS * SLOT, HEAD_DIM), jnp.float32)
+    held = [
+        (pltpu.SMEM if x.dtype == jnp.int32 else pltpu.VMEM)(x.shape, x.dtype) for x in inputs
+    ]
+    x, stream, *scales = loader.call(
+        attend_kernel,
+        loader.take(LOAD_ATTEND),
+        inputs + scales,
+        [ANY] * (len(inputs) + len(scales)),
+        [
+            jax.ShapeDtypeStruct((rows, D + LANES), jnp.bfloat16),
+            jax.ShapeDtypeStruct((rows, D), jnp.float32),
+            *[jax.ShapeDtypeStruct(table.shape, table.dtype) for table in scales],
+        ],
+        lambda count: held + [stacked] * 4 + [semaphores(13), semaphores(count)],
+        "attend",
+        4 << 20,
+    )
+    steps = digits("role", 2) + digits("tp", 4)
     spread_scales = None
-    near, far = x, None
-    for number, (axis, bit) in enumerate(steps):
-        if far is not None:
-            near = jnp.concatenate([near, far], axis=0)
-        far = swap(near, axis, bit)
+    near, far = x, []
+    for number, (axis, offsets) in enumerate(steps):
+        if far:
+            near = jnp.concatenate([near, *far], axis=0)
+        far = [swap(near, axis, offset) for offset in offsets]
         taken = loader.take(LOAD_STEP[min(number, len(LOAD_STEP) - 1)])
         if spread_scales is None:
             near, *spread_scales = load_more(loader, taken, near, scales)
         elif taken:
             (near,) = load_more(loader, taken, near, [])
     gate_s, up_s, down_s = spread_scales
-    count = 2 * near.shape[0]
+    count = (1 + len(far)) * near.shape[0]
     piece = jax.ShapeDtypeStruct((count, extended), jnp.bfloat16)
-    kept, sent = local_call(split_kernel, (piece, piece), (near, far), "split")
+    kept, sent = local_call(split_kernel, (piece, piece), (near, *far), "split")
     other = swap(sent, None, 0)
     parts = []
     before = other
@@ -557,14 +573,16 @@
             experts=experts,
         )
     kept, sent = carried
-    piece = jax.ShapeDtypeStruct((count // 2, D), jnp.bfloat16)
-    near, far = local_call(join_kernel, (piece, piece), (kept, swap(sent, None, 0)), "join")
-    for axis, bit in reversed(steps[1:]):
-        carried = add_bf16(near, swap(far, axis, bit))
-        middle = carried.shape[0] // 2
-        near, far = carried[:middle], carried[middle:]
+    axis, offsets = steps[-1]
+    parts = 1 + len(offsets)
+    piece = jax.ShapeDtypeStruct((count // parts, D), jnp.bfloat16)
+    pieces = local_call(join_kernel, (piece,) * parts, (kept, swap(sent, None, 0)), "join")
+    for following, _ in zip(reversed(steps[:-1]), steps[1:]):
+        carried = add_bf16(returned_pieces(pieces, axis, offsets))
+        axis, offsets = following
+        pieces = jnp.split(carried, 1 + len(offsets))
     out = jax.ShapeDtypeStruct((rows, D), jnp.bfloat16)
-    return local_call(finish_kernel, out, (stream, near, swap(far, *steps[0])), "finish")
+    return local_call(finish_kernel, out, (stream, *returned_pieces(pieces, axis, offsets)), "finish")
 
 
 def solution(mesh):

time: 41.1 us -> 38.6 us (0.939)
  Pallas kernels: 16.4 us -> 14.2 us
  waiting for transfers between devices: 10.2 us -> 9.37 us
  starting transfers between devices: 13.6 us -> 14.1 us
    pallas_call x8 -> x7, Pallas kernels: 15.7 us -> 13.6 us  [call(): pl.pallas_call(functools.partial(kernel, places=tuple(((e, p) for _, e, p...]
    ppermute x6 -> x8, waiting for transfers between devices: 8.08 us -> 7.12 us  [swap(): lax.ppermute(x, (axis, 'sub'), [(i, i ^ 2 * bit + 1) for i in range(count)])]
    ppermute x6 -> x8, starting transfers between devices: 12.3 us -> 12.6 us  [swap(): lax.ppermute(x, (axis, 'sub'), [(i, i ^ 2 * bit + 1) for i in range(count)])]
  transfers between devices with their start and end apart: 10 -> 12, of which waited for: 7 -> 8; matrix products, arithmetic and copies ran while one was open for 0% -> 0% of each run, Pallas kernels for 24% -> 20%
where the time goes in v5:
time: 38.6 us; the launch traced here: 38.4 us
  Pallas kernels  14.2 us (37%)
  starting transfers between devices  14.1 us (37%)
  waiting for transfers between devices  9.37 us (24%)
  local copies, waits for them, and re-layouts  0.5 us (1%)
    pallas_call x7, Pallas kernels, call(): pl.pallas_call(functools.partial(kernel, places=tuple(((e, p) for _, e, p...  13.6 us
    ppermute x8, starting transfers between devices, swap(): lax.ppermute(x, (axis, 'sub'), [(i, i ^ 2 * bit + 1) for i in range(count)])  12.6 us
    ppermute x8, waiting for transfers between devices, swap(): lax.ppermute(x, (axis, 'sub'), [(i, i ^ 2 * bit + 1) for i in range(count)])  7.12 us
    ppermute x4, waiting for transfers between devices, swap(): return lax.ppermute(x, 'sub', [(0, 1), (1, 0)])  2.25 us
    ppermute x4, starting transfers between devices, swap(): return lax.ppermute(x, 'sub', [(0, 1), (1, 0)])  1.47 us
  transfers between devices with their start and end apart: 12, of which 8 were waited for; matrix products, arithmetic and copies ran while one was open for 0% of the time, Pallas kernels for 20%

profile of v5, /device:TPU:0, one launch (start us, length us, event | category | flops | bytes accessed | tf_op | source)
XLA Modules:
  0.0 38.4 jit_solution(16910613488918889023)
XLA Ops:
  0.0 2.8 %attend.1 = (bf16[4,3200]{1,0:T(4,128)(2,1)S(1)}, f32[4,3072]{1,0:T(4,128)S(1)}, f32[12,2,16]{2,1,0:T(2,128)S(1)}, f32[12,2,16]{2,1,0:T(2,128)S(1)}, f32[12,2,16...) custom-call(bf16[4,3072]{1,0:T(4,128)(2,1)} %refs_0_.1, bf16[4,1024]{1,0:T(4,128)(2,1)} %refs_1_.2, bf16[4,1024]{1,0:T(4,128)(2,1)} %refs_2_.2, ...), custom_call_target="tpu_custom_call" | custom-call | bytes 7340032 | tf_op jit(solution)/shard_map/attend/pallas_call | solution.py:417
  2.8 2.4 %collective-permute-start = (bf16[4,3200]{1,0:T(4,128)(2,1)S(1)}, bf16[4,3200]{1,0:T(4,128)(2,1)S(1)}, u32[]{:S(2)}, u32[]{:S(2)}) collective-permute-start(bf16[4,3200]{1,0:T(4,128)(2,1)S(1)} %get-tuple-element.29.refs_0_), channel_id=1, source_target_pairs={{0,9},{1,8},{8,1},{9,0},{2,11},{3,10},{10,3},{11,2},{4,13},{5,12},... | collective-permute-start | bytes 76808 | tf_op jit(solution)/shard_map/ppermute | solution.py:352
  5.2 1.9 %load.2 = (bf16[4,3200]{1,0:T(4,128)(2,1)S(1)}, f32[2,12,2048]{2,1,0:T(8,128)S(1)}, f32[2,12,2048]{2,1,0:T(8,128)S(1)}, f32[2,16,1536]{2,1,0:T(8,128)S(1)}, bf16[768,2048]{1,0:T(8,128)(2,1)S(1)}) custom-call(bf16[4,3200]{1,0:T(4,128)(2,1)S(1)} %get-tuple-element.29.refs_0_, f32[12,2,16]{2,1,0:T(2,128)S(1)} %get-tuple-element.30.refs_1_, ...), custom_call_target="tpu_custom_call" | custom-call | bytes 4194304 | tf_op jit(solution)/shard_map/load/pallas_call | solution.py:417
  7.1 0.0 slice-start.3
  7.2 0.0 slice-start.4
  7.2 4.0 %collective-permute-start.3 = (bf16[8,3200]{1,0:T(8,128)(2,1)S(1)}, bf16[8,3200]{1,0:T(8,128)(2,1)S(1)}, u32[]{:S(2)}, u32[]{:S(2)}) collective-permute-start(bf16[8,3200]{1,0:T(8,128)(2,1)S(1)} %pad_maximum_fusion.refs_0_), channel_id=1, source_target_pairs={{0,7},{1,6},{2,5},{3,4},{4,3},{5,2},{6,1},{7,0},{8,15},{9,14},{10,... | collective-permute-start | bytes 153608 | tf_op jit(solution)/shard_map/ppermute | solution.py:352
  11.2 0.7 %collective-permute-start.1 = (bf16[8,3200]{1,0:T(8,128)(2,1)S(1)}, bf16[8,3200]{1,0:T(8,128)(2,1)S(1)}, u32[]{:S(2)}, u32[]{:S(2)}) collective-permute-start(bf16[8,3200]{1,0:T(8,128)(2,1)S(1)} %pad_maximum_fusion.refs_0_), channel_id=1, source_target_pairs={{0,5},{1,4},{2,7},{3,6},{4,1},{5,0},{6,3},{7,2},{8,13},{9,12},{10,... | collective-permute-start | bytes 153608 | tf_op jit(solution)/shard_map/ppermute | solution.py:352
  11.9 2.9 %load.3 = (bf16[8,3200]{1,0:T(8,128)(2,1)S(1)}, bf16[768,2048]{1,0:T(8,128)(2,1)S(1)}, bf16[768,2048]{1,0:T(8,128)(2,1)S(1)}) custom-call(bf16[8,3200]{1,0:T(8,128)(2,1)S(1)} %pad_maximum_fusion.refs_0_, bf16[2,1536,2048]{2,1,0:T(8,128)(2,1)} %refs_2_.3, bf16[2,1536,2048]{2,1,0:T(8,128)(2,1)} %refs_2_.3), custom_call_target="tpu_custom_call" | custom-call | bytes 7340032 | tf_op jit(solution)/shard_map/load/pallas_call | solution.py:417
  14.8 1.0 %collective-permute-done.1.refs_1_ = bf16[8,3200]{1,0:T(8,128)(2,1)S(1)} collective-permute-done((bf16[8,3200]{1,0:T(8,128)(2,1)S(1)}, bf16[8,3200]{1,0:T(8,128)(2,1)S(1)}, u32[]{:S(2)}, u32[]{:S(2)}) %collective-permute-start.1) | collective-permute-done | bytes 51232 | tf_op jit(solution)/shard_map/ppermute | solution.py:352
  15.8 0.6 %collective-permute-start.4 = (bf16[32,1664]{1,0:T(8,128)(2,1)S(1)}, bf16[32,1664]{1,0:T(8,128)(2,1)S(1)}, u32[]{:S(2)}, u32[]{:S(2)}) collective-permute-start(bf16[32,1664]{1,0:T(8,128)(2,1)S(1)} %get-tuple-element.36), channel_id=1, source_target_pairs={{0,1},{1,0},{2,3},{3,2},{4,5},{5,4},{6,7},{7,6},{8,9},{9,8},{10,11... | collective-permute-start | bytes 319496 | tf_op jit(solution)/shard_map/ppermute | solution.py:350
  16.4 1.0 %collective-permute-done.4.refs_1_ = bf16[32,1664]{1,0:T(8,128)(2,1)S(1)} collective-permute-done((bf16[32,1664]{1,0:T(8,128)(2,1)S(1)}, bf16[32,1664]{1,0:T(8,128)(2,1)S(1)}, u32[]{:S(2)}, u32[]{:S(2)}) %collective-permute-start.4) | collective-permute-done | bytes 106528 | tf_op jit(solution)/shard_map/ppermute | solution.py:350
  17.3 0.0 slice-start
  17.4 0.0 slice-start.1
  17.4 1.9 %gate_up.2.refs_2_ = bf16[64,4096]{1,0:T(8,128)(2,1)S(1)} custom-call(bf16[32,1664]{1,0:T(8,128)(2,1)S(1)} %get-tuple-element.35.refs_0_, bf16[32,1664]{1,0:T(8,128)(2,1)S(1)} %collective-permute-done.4.refs_1_, f32[2,12,2048]{2,1,0:T(8,128)S(1)} %get-tuple-element.37.refs_2_, f32[2,12,2048]{2,1,0:T(8,128)S(1)} %get-tuple-element.38.refs_3_, ...), custom_call_target="tpu_custom_call" | custom-call | bytes 2097152 | tf_op jit(solution)/shard_map/gate_up/pallas_call | solution.py:417
  19.3 0.4 %collective-permute-start.6 = (bf16[64,4096]{1,0:T(8,128)(2,1)S(1)}, bf16[64,4096]{1,0:T(8,128)(2,1)S(1)}, u32[]{:S(2)}, u32[]{:S(2)}) collective-permute-start(bf16[64,4096]{1,0:T(8,128)(2,1)S(1)} %gate_up.2.refs_2_), channel_id=1, source_target_pairs={{0,1},{1,0},{2,3},{3,2},{4,5},{5,4},{6,7},{7,6},{8,9},{9,8},{10,11... | collective-permute-start | bytes 1572872 | tf_op jit(solution)/shard_map/ppermute | solution.py:350
  19.7 1.9 %gate_up.3.refs_2_ = bf16[64,4096]{1,0:T(8,128)(2,1)S(1)} custom-call(bf16[32,1664]{1,0:T(8,128)(2,1)S(1)} %get-tuple-element.35.refs_0_, bf16[32,1664]{1,0:T(8,128)(2,1)S(1)} %collective-permute-done.4.refs_1_, f32[2,12,2048]{2,1,0:T(8,128)S(1)} %get-tuple-element.37.refs_2_, f32[2,12,2048]{2,1,0:T(8,128)S(1)} %get-tuple-element.38.refs_3_, ...), custom_call_target="tpu_custom_call" | custom-call | bytes 2097152 | tf_op jit(solution)/shard_map/gate_up/pallas_call | solution.py:417
  21.6 0.2 collective-permute-start.5
  21.8 0.4 %slice-done.2 = s8[4194304]{0:T(1024)(128)(4,1)S(1)} async-done(((s8[12582912]{0:T(1024)(128)(4,1)}), s8[4194304]{0:T(1024)(128)(4,1)S(1)}, s32[]{:S(2)}) %slice-start.2) | async-done | bytes 4194328
  22.2 1.1 %down.2.refs_6_ = f32[64,1536]{1,0:T(8,128)S(1)} custom-call(bf16[32,1664]{1,0:T(8,128)(2,1)S(1)} %get-tuple-element.35.refs_0_, bf16[32,1664]{1,0:T(8,128)(2,1)S(1)} %collective-permute-done.4.refs_1_, bf16[64,4096]{1,0:T(8,128)(2,1)S(1)} %gate_up.2.refs_2_, bf16[64,4096]{1,0:T(8,128)(2,1)S(1)} %collective-permute-done.6.refs_3_, ...), custom_call_target="tpu_custom_call" | custom-call | bytes 4194304 | tf_op jit(solution)/shard_map/down/pallas_call | solution.py:417
  23.4 0.2 collective-permute-done.5.refs_3_
  23.6 1.1 %down.3 = (bf16[32,1536]{1,0:T(8,128)(2,1)S(1)}, bf16[32,1536]{1,0:T(8,128)(2,1)S(1)}) custom-call(bf16[32,1664]{1,0:T(8,128)(2,1)S(1)} %get-tuple-element.35.refs_0_, bf16[32,1664]{1,0:T(8,128)(2,1)S(1)} %collective-permute-done.4.refs_1_, bf16[64,4096]{1,0:T(8,128)(2,1)S(1)} %gate_up.3.refs_2_, bf16[64,4096]{1,0:T(8,128)(2,1)S(1)} %collective-permute-done.5.refs_3_, ...), custom_call_target="tpu_custom_call" | custom-call | bytes 4194304 | tf_op jit(solution)/shard_map/down/pallas_call | solution.py:417
  24.7 0.2 collective-permute-start.7
  24.9 1.1 %collective-permute-done.7.other_ref = bf16[32,1536]{1,0:T(8,128)(2,1)S(1)} collective-permute-done((bf16[32,1536]{1,0:T(8,128)(2,1)S(1)}, bf16[32,1536]{1,0:T(8,128)(2,1)S(1)}, u32[]{:S(2)}, u32[]{:S(2)}) %collective-permute-start.7) | collective-permute-done | bytes 98336 | tf_op jit(solution)/shard_map/ppermute | solution.py:350
  26.1 2.3 %collective-permute-start.8 = (bf16[8,3072]{1,0:T(8,128)(2,1)S(1)}, bf16[8,3072]{1,0:T(8,128)(2,1)S(1)}, u32[]{:S(2)}, u32[]{:S(2)}) collective-permute-start(bf16[8,3072]{1,0:T(8,128)(2,1)S(1)} %get-tuple-element.48), channel_id=1, source_target_pairs={{0,5},{1,4},{2,7},{3,6},{4,1},{5,0},{6,3},{7,2},{8,13},{9,12},{10,... | collective-permute-start | bytes 147464 | tf_op jit(solution)/shard_map/ppermute | solution.py:352
  28.4 0.6 %collective-permute-start.9 = (bf16[8,3072]{1,0:T(8,128)(2,1)S(1)}, bf16[8,3072]{1,0:T(8,128)(2,1)S(1)}, u32[]{:S(2)}, u32[]{:S(2)}) collective-permute-start(bf16[8,3072]{1,0:T(8,128)(2,1)S(1)} %get-tuple-element.49), channel_id=1, source_target_pairs={{0,3},{1,2},{2,1},{3,0},{4,7},{5,6},{6,5},{7,4},{8,11},{9,10},{10,... | collective-permute-start | bytes 147464 | tf_op jit(solution)/shard_map/ppermute | solution.py:352
  29.0 1.2 %collective-permute-start.10 = (bf16[8,3072]{1,0:T(8,128)(2,1)S(1)}, bf16[8,3072]{1,0:T(8,128)(2,1)S(1)}, u32[]{:S(2)}, u32[]{:S(2)}) collective-permute-start(bf16[8,3072]{1,0:T(8,128)(2,1)S(1)} %get-tuple-element.50), channel_id=1, source_target_pairs={{0,7},{1,6},{2,5},{3,4},{4,3},{5,2},{6,1},{7,0},{8,15},{9,14},{10,... | collective-permute-start | bytes 147464 | tf_op jit(solution)/shard_map/ppermute | solution.py:352
  30.1 0.7 %collective-permute-done.8 = bf16[8,3072]{1,0:T(8,128)(2,1)S(1)} collective-permute-done((bf16[8,3072]{1,0:T(8,128)(2,1)S(1)}, bf16[8,3072]{1,0:T(8,128)(2,1)S(1)}, u32[]{:S(2)}, u32[]{:S(2)}) %collective-permute-start.8) | collective-permute-done | bytes 49184 | tf_op jit(solution)/shard_map/ppermute | solution.py:352
  30.8 1.2 %collective-permute-done.9 = bf16[8,3072]{1,0:T(8,128)(2,1)S(1)} collective-permute-done((bf16[8,3072]{1,0:T(8,128)(2,1)S(1)}, bf16[8,3072]{1,0:T(8,128)(2,1)S(1)}, u32[]{:S(2)}, u32[]{:S(2)}) %collective-permute-start.9) | collective-permute-done | bytes 49184 | tf_op jit(solution)/shard_map/ppermute | solution.py:352
  32.1 2.3 %collective-permute-done.10 = bf16[8,3072]{1,0:T(8,128)(2,1)S(1)} collective-permute-done((bf16[8,3072]{1,0:T(8,128)(2,1)S(1)}, bf16[8,3072]{1,0:T(8,128)(2,1)S(1)}, u32[]{:S(2)}, u32[]{:S(2)}) %collective-permute-start.10) | collective-permute-done | bytes 49184 | tf_op jit(solution)/shard_map/ppermute | solution.py:352
  34.5 1.5 %collective-permute-start.11 = (bf16[4,3072]{1,0:T(4,128)(2,1)S(1)}, bf16[4,3072]{1,0:T(4,128)(2,1)S(1)}, u32[]{:S(2)}, u32[]{:S(2)}) collective-permute-start(bf16[4,3072]{1,0:T(4,128)(2,1)S(1)} %get-tuple-element.51), channel_id=1, source_target_pairs={{0,9},{1,8},{8,1},{9,0},{2,11},{3,10},{10,3},{11,2},{4,13},{5,12},... | collective-permute-start | bytes 73736 | tf_op jit(solution)/shard_map/ppermute | solution.py:352
  35.9 1.9 %collective-permute-done.11.refs_1_ = bf16[4,3072]{1,0:T(4,128)(2,1)S(1)} collective-permute-done((bf16[4,3072]{1,0:T(4,128)(2,1)S(1)}, bf16[4,3072]{1,0:T(4,128)(2,1)S(1)}, u32[]{:S(2)}, u32[]{:S(2)}) %collective-permute-start.11) | collective-permute-done | bytes 24608 | tf_op jit(solution)/shard_map/ppermute | solution.py:352
  37.8 0.6 %finish.1 = bf16[4,3072]{1,0:T(4,128)(2,1)} custom-call(f32[4,3072]{1,0:T(4,128)S(1)} %get-tuple-element.28.stream_ref, bf16[4,3072]{1,0:T(4,128)(2,1)S(1)} %get-tuple-element.52.refs_0_, bf16[4,3072]{1,0:T(4,128)(2,1)S(1)} %collective-permute-done.11.refs_1_), custom_call_target="tpu_custom_call" | custom-call | tf_op jit(solution)/shard_map/finish/pallas_call | solution.py:371
  (19 shorter events, 0.2 us)
Async XLA Ops:
  2.8 4.4 %collective-permute-start = (bf16[4,3200]{1,0:T(4,128)(2,1)S(1)}, bf16[4,3200]{1,0:T(4,128)(2,1)S(1)}, u32[]{:S(2)}, u32[]{:S(2)}) collective-permute-start(bf16[4,3200]{1,0:T(4,128)(2,1)S(1)} %get-tuple-element.29.refs_0_), channel_id=1, source_target_pairs={{0,9},{1,8},{8,1},{9,0},{2,11},{3,10},{10,3},{11,2},{4,13},{5,12},... | collective-permute-start | bytes 76808 | tf_op jit(solution)/shard_map/ppermute | solution.py:352
  7.1 10.2 %slice-start.3 = ((s8[12582912]{0:T(1024)(128)(4,1)}), s8[4194304]{0:T(1024)(128)(4,1)S(1)}, s32[]{:S(2)}) async-start(s8[12582912]{0:T(1024)(128)(4,1)} %bitcast.8), calls=%async_computation.3 | async-start | bytes 8388608
  7.2 10.1 %slice-start.4 = ((s8[12582912]{0:T(1024)(128)(4,1)}), s8[4194304]{0:T(1024)(128)(4,1)S(1)}, s32[]{:S(2)}) async-start(s8[12582912]{0:T(1024)(128)(4,1)} %bitcast.8), calls=%async_computation.4 | async-start | bytes 8388608
  7.2 10.1 %slice-start.5 = ((s8[12582912]{0:T(1024)(128)(4,1)}), s8[4194304]{0:T(1024)(128)(4,1)S(1)}, s32[]{:S(2)}) async-start(s8[12582912]{0:T(1024)(128)(4,1)} %bitcast.8), calls=%async_computation.5 | async-start | bytes 8388608
  7.2 7.5 %collective-permute-start.3 = (bf16[8,3200]{1,0:T(8,128)(2,1)S(1)}, bf16[8,3200]{1,0:T(8,128)(2,1)S(1)}, u32[]{:S(2)}, u32[]{:S(2)}) collective-permute-start(bf16[8,3200]{1,0:T(8,128)(2,1)S(1)} %pad_maximum_fusion.refs_0_), channel_id=1, source_target_pairs={{0,7},{1,6},{2,5},{3,4},{4,3},{5,2},{6,1},{7,0},{8,15},{9,14},{10,... | collective-permute-start | bytes 153608 | tf_op jit(solution)/shard_map/ppermute | solution.py:352
  11.2 3.6 %collective-permute-start.2 = (bf16[8,3200]{1,0:T(8,128)(2,1)S(1)}, bf16[8,3200]{1,0:T(8,128)(2,1)S(1)}, u32[]{:S(2)}, u32[]{:S(2)}) collective-permute-start(bf16[8,3200]{1,0:T(8,128)(2,1)S(1)} %pad_maximum_fusion.refs_0_), channel_id=1, source_target_pairs={{0,3},{1,2},{2,1},{3,0},{4,7},{5,6},{6,5},{7,4},{8,11},{9,10},{10,... | collective-permute-start | bytes 153608 | tf_op jit(solution)/shard_map/ppermute | solution.py:352
  11.2 4.5 %collective-permute-start.1 = (bf16[8,3200]{1,0:T(8,128)(2,1)S(1)}, bf16[8,3200]{1,0:T(8,128)(2,1)S(1)}, u32[]{:S(2)}, u32[]{:S(2)}) collective-permute-start(bf16[8,3200]{1,0:T(8,128)(2,1)S(1)} %pad_maximum_fusion.refs_0_), channel_id=1, source_target_pairs={{0,5},{1,4},{2,7},{3,6},{4,1},{5,0},{6,3},{7,2},{8,13},{9,12},{10,... | collective-permute-start | bytes 153608 | tf_op jit(solution)/shard_map/ppermute | solution.py:352
  15.8 1.5 %collective-permute-start.4 = (bf16[32,1664]{1,0:T(8,128)(2,1)S(1)}, bf16[32,1664]{1,0:T(8,128)(2,1)S(1)}, u32[]{:S(2)}, u32[]{:S(2)}) collective-permute-start(bf16[32,1664]{1,0:T(8,128)(2,1)S(1)} %get-tuple-element.36), channel_id=1, source_target_pairs={{0,1},{1,0},{2,3},{3,2},{4,5},{5,4},{6,7},{7,6},{8,9},{9,8},{10,11... | collective-permute-start | bytes 319496 | tf_op jit(solution)/shard_map/ppermute | solution.py:350
  17.3 4.4 %slice-start = ((s8[12582912]{0:T(1024)(128)(4,1)}), s8[4194304]{0:T(1024)(128)(4,1)S(1)}, s32[]{:S(2)}) async-start(s8[12582912]{0:T(1024)(128)(4,1)} %bitcast.6), calls=%async_computation | async-start | bytes 8388608
  17.4 4.4 %slice-start.1 = ((s8[12582912]{0:T(1024)(128)(4,1)}), s8[4194304]{0:T(1024)(128)(4,1)S(1)}, s32[]{:S(2)}) async-start(s8[12582912]{0:T(1024)(128)(4,1)} %bitcast.6), calls=%async_computation.1 | async-start | bytes 8388608
  19.3 2.5 %collective-permute-start.6 = (bf16[64,4096]{1,0:T(8,128)(2,1)S(1)}, bf16[64,4096]{1,0:T(8,128)(2,1)S(1)}, u32[]{:S(2)}, u32[]{:S(2)}) collective-permute-start(bf16[64,4096]{1,0:T(8,128)(2,1)S(1)} %gate_up.2.refs_2_), channel_id=1, source_target_pairs={{0,1},{1,0},{2,3},{3,2},{4,5},{5,4},{6,7},{7,6},{8,9},{9,8},{10,11... | collective-permute-start | bytes 1572872 | tf_op jit(solution)/shard_map/ppermute | solution.py:350
  19.7 2.5 %slice-start.2 = ((s8[12582912]{0:T(1024)(128)(4,1)}), s8[4194304]{0:T(1024)(128)(4,1)S(1)}, s32[]{:S(2)}) async-start(s8[12582912]{0:T(1024)(128)(4,1)} %bitcast.6), calls=%async_computation.2 | async-start | bytes 8388608
  21.6 2.0 %collective-permute-start.5 = (bf16[64,4096]{1,0:T(8,128)(2,1)S(1)}, bf16[64,4096]{1,0:T(8,128)(2,1)S(1)}, u32[]{:S(2)}, u32[]{:S(2)}) collective-permute-start(bf16[64,4096]{1,0:T(8,128)(2,1)S(1)} %gate_up.3.refs_2_), channel_id=1, source_target_pairs={{0,1},{1,0},{2,3},{3,2},{4,5},{5,4},{6,7},{7,6},{8,9},{9,8},{10,11... | collective-permute-start | bytes 1572872 | tf_op jit(solution)/shard_map/ppermute | solution.py:350
  24.7 1.4 %collective-permute-start.7 = (bf16[32,1536]{1,0:T(8,128)(2,1)S(1)}, bf16[32,1536]{1,0:T(8,128)(2,1)S(1)}, u32[]{:S(2)}, u32[]{:S(2)}) collective-permute-start(bf16[32,1536]{1,0:T(8,128)(2,1)S(1)} %get-tuple-element.46), channel_id=1, source_target_pairs={{0,1},{1,0},{2,3},{3,2},{4,5},{5,4},{6,7},{7,6},{8,9},{9,8},{10,11... | collective-permute-start | bytes 294920 | tf_op jit(solution)/shard_map/ppermute | solution.py:350
  26.1 4.7 %collective-permute-start.8 = (bf16[8,3072]{1,0:T(8,128)(2,1)S(1)}, bf16[8,3072]{1,0:T(8,128)(2,1)S(1)}, u32[]{:S(2)}, u32[]{:S(2)}) collective-permute-start(bf16[8,3072]{1,0:T(8,128)(2,1)S(1)} %get-tuple-element.48), channel_id=1, source_target_pairs={{0,5},{1,4},{2,7},{3,6},{4,1},{5,0},{6,3},{7,2},{8,13},{9,12},{10,... | collective-permute-start | bytes 147464 | tf_op jit(solution)/shard_map/ppermute | solution.py:352
  28.4 3.7 %collective-permute-start.9 = (bf16[8,3072]{1,0:T(8,128)(2,1)S(1)}, bf16[8,3072]{1,0:T(8,128)(2,1)S(1)}, u32[]{:S(2)}, u32[]{:S(2)}) collective-permute-start(bf16[8,3072]{1,0:T(8,128)(2,1)S(1)} %get-tuple-element.49), channel_id=1, source_target_pairs={{0,3},{1,2},{2,1},{3,0},{4,7},{5,6},{6,5},{7,4},{8,11},{9,10},{10,... | collective-permute-start | bytes 147464 | tf_op jit(solution)/shard_map/ppermute | solution.py:352
  29.0 5.4 %collective-permute-start.10 = (bf16[8,3072]{1,0:T(8,128)(2,1)S(1)}, bf16[8,3072]{1,0:T(8,128)(2,1)S(1)}, u32[]{:S(2)}, u32[]{:S(2)}) collective-permute-start(bf16[8,3072]{1,0:T(8,128)(2,1)S(1)} %get-tuple-element.50), channel_id=1, source_target_pairs={{0,7},{1,6},{2,5},{3,4},{4,3},{5,2},{6,1},{7,0},{8,15},{9,14},{10,... | collective-permute-start | bytes 147464 | tf_op jit(solution)/shard_map/ppermute | solution.py:352
  34.5 3.3 %collective-permute-start.11 = (bf16[4,3072]{1,0:T(4,128)(2,1)S(1)}, bf16[4,3072]{1,0:T(4,128)(2,1)S(1)}, u32[]{:S(2)}, u32[]{:S(2)}) collective-permute-start(bf16[4,3072]{1,0:T(4,128)(2,1)S(1)} %get-tuple-element.51), channel_id=1, source_target_pairs={{0,9},{1,8},{8,1},{9,0},{2,11},{3,10},{10,3},{11,2},{4,13},{5,12},... | collective-permute-start | bytes 73736 | tf_op jit(solution)/shard_map/ppermute | solution.py:352

commit v6 on v5

--- a/solution.py
+++ b/solution.py
@@ -20,9 +20,10 @@
 PIECES = 2
 VMEM_LIMIT = 16 << 20
 
-LOAD_ATTEND = 1
-LOAD_STEP = (1, 2)
+LOAD_ATTEND = 0
+LOAD_STEP = (1, 3)
 ORDER = (2, 1, 3)
+RETURN = (3, 2, 1)
 LOAD_GATE_UP = 2
 LOAD_DOWN = 1
 WIDTH = 512
@@ -326,12 +327,12 @@
         load.wait()
 
 
-def join_kernel(kept_ref, other_ref, *refs):
+def join_kernel(kept_ref, other_ref, *refs, blocks):
     half = D // 2
     first = lax.axis_index("sub") == 0
     count = refs[0].shape[0]
-    for i, ref in enumerate(refs):
-        at = slice(i * count, (i + 1) * count)
+    for block, ref in zip(blocks, refs):
+        at = slice(block * count, (block + 1) * count)
         kept, other = kept_ref[at, :], other_ref[at, :]
         ref[:, :half] = jnp.where(first, kept, other)
         ref[:, half:] = jnp.where(first, other, kept)
@@ -576,7 +577,10 @@
     axis, offsets = steps[-1]
     parts = 1 + len(offsets)
     piece = jax.ShapeDtypeStruct((count // parts, D), jnp.bfloat16)
-    pieces = local_call(join_kernel, (piece,) * parts, (kept, swap(sent, None, 0)), "join")
+    blocks = [0, *RETURN] if parts == 4 else list(range(parts))
+    offsets = tuple(offsets[block - 1] for block in blocks[1:])
+    joined = functools.partial(join_kernel, blocks=tuple(blocks))
+    pieces = local_call(joined, (piece,) * parts, (kept, swap(sent, None, 0)), "join")
     for following, _ in zip(reversed(steps[:-1]), steps[1:]):
         carried = add_bf16(returned_pieces(pieces, axis, offsets))
         axis, offsets = following

time: 38.6 us -> 37.7 us (0.977)
  waiting for transfers between devices: 9.37 us -> 7.84 us
  Pallas kernels: 14.2 us -> 14.9 us
    ppermute x8, waiting for transfers between devices: 7.12 us -> 5.46 us  [swap(): lax.ppermute(x, (axis, 'sub'), [(i, i ^ 2 * bit + 1) for i in range(count)])]
    pallas_call x7, Pallas kernels: 13.6 us -> 14.3 us  [call(): pl.pallas_call(functools.partial(kernel, places=tuple(((e, p) for _, e, p...]
  transfers between devices with their start and end apart: 12 -> 12, of which waited for: 8 -> 8; matrix products, arithmetic and copies ran while one was open for 0% -> 0% of each run, Pallas kernels for 20% -> 23%
where the time goes in v6:
time: 37.7 us; the launch traced here: 37.5 us
  Pallas kernels  14.9 us (40%)
  starting transfers between devices  14.1 us (37%)
  waiting for transfers between devices  7.84 us (21%)
  local copies, waits for them, and re-layouts  0.42 us (1%)
    pallas_call x7, Pallas kernels, call(): pl.pallas_call(functools.partial(kernel, places=tuple(((e, p) for _, e, p...  14.3 us
    ppermute x8, starting transfers between devices, swap(): lax.ppermute(x, (axis, 'sub'), [(i, i ^ 2 * bit + 1) for i in range(count)])  12.7 us
    ppermute x8, waiting for transfers between devices, swap(): lax.ppermute(x, (axis, 'sub'), [(i, i ^ 2 * bit + 1) for i in range(count)])  5.46 us
    ppermute x4, waiting for transfers between devices, swap(): return lax.ppermute(x, 'sub', [(0, 1), (1, 0)])  2.38 us
    ppermute x4, starting transfers between devices, swap(): return lax.ppermute(x, 'sub', [(0, 1), (1, 0)])  1.43 us
  transfers between devices with their start and end apart: 12, of which 8 were waited for; matrix products, arithmetic and copies ran while one was open for 0% of the time, Pallas kernels for 23%

profile of v6, /device:TPU:0, one launch (start us, length us, event | category | flops | bytes accessed | tf_op | source)
XLA Modules:
  0.0 37.5 jit_solution(2347249654105833563)
XLA Ops:
  0.0 2.5 %attend.1 = (bf16[4,3200]{1,0:T(4,128)(2,1)S(1)}, f32[4,3072]{1,0:T(4,128)S(1)}, f32[12,2,16]{2,1,0:T(2,128)S(1)}, f32[12,2,16]{2,1,0:T(2,128)S(1)}, f32[12,2,16]{2,1,0:T(2,128)S(1)}) custom-call(bf16[4,3072]{1,0:T(4,128)(2,1)} %refs_0_.1, bf16[4,1024]{1,0:T(4,128)(2,1)} %refs_1_.2, bf16[4,1024]{1,0:T(4,128)(2,1)} %refs_2_.2, s32[4]{0:T(128)} %refs_3_.2, ...), custom_call_target="tpu_custom_call" | custom-call | bytes 4194304 | tf_op jit(solution)/shard_map/attend/pallas_call | solution.py:418
  2.5 2.4 %collective-permute-start = (bf16[4,3200]{1,0:T(4,128)(2,1)S(1)}, bf16[4,3200]{1,0:T(4,128)(2,1)S(1)}, u32[]{:S(2)}, u32[]{:S(2)}) collective-permute-start(bf16[4,3200]{1,0:T(4,128)(2,1)S(1)} %get-tuple-element.29.refs_0_), channel_id=1, source_target_pairs={{0,9},{1,8},{8,1},{9,0},{2,11},{3,10},{10,3},{11,2},{4,13},{5,12},... | collective-permute-start | bytes 76808 | tf_op jit(solution)/shard_map/ppermute | solution.py:353
  4.9 1.9 %load.2 = (bf16[4,3200]{1,0:T(4,128)(2,1)S(1)}, f32[2,12,2048]{2,1,0:T(8,128)S(1)}, f32[2,12,2048]{2,1,0:T(8,128)S(1)}, f32[2,16,1536]{2,1,0:T(8,128)S(1)}, bf16[768,2048]{1,0:T(8,128)(2,1)S(1)}) custom-call(bf16[4,3200]{1,0:T(4,128)(2,1)S(1)} %get-tuple-element.29.refs_0_, f32[12,2,16]{2,1,0:T(2,128)S(1)} %get-tuple-element.30.refs_1_, ...), custom_call_target="tpu_custom_call" | custom-call | bytes 4194304 | tf_op jit(solution)/shard_map/load/pallas_call | solution.py:418
  6.8 0.0 collective-permute-done
  6.8 0.0 slice-start.3
  6.9 0.0 slice-start.4
  6.9 4.0 %collective-permute-start.3 = (bf16[8,3200]{1,0:T(8,128)(2,1)S(1)}, bf16[8,3200]{1,0:T(8,128)(2,1)S(1)}, u32[]{:S(2)}, u32[]{:S(2)}) collective-permute-start(bf16[8,3200]{1,0:T(8,128)(2,1)S(1)} %pad_maximum_fusion.refs_0_), channel_id=1, source_target_pairs={{0,7},{1,6},{2,5},{3,4},{4,3},{5,2},{6,1},{7,0},{8,15},{9,14},{10,... | collective-permute-start | bytes 153608 | tf_op jit(solution)/shard_map/ppermute | solution.py:353
  10.9 0.7 %collective-permute-start.1 = (bf16[8,3200]{1,0:T(8,128)(2,1)S(1)}, bf16[8,3200]{1,0:T(8,128)(2,1)S(1)}, u32[]{:S(2)}, u32[]{:S(2)}) collective-permute-start(bf16[8,3200]{1,0:T(8,128)(2,1)S(1)} %pad_maximum_fusion.refs_0_), channel_id=1, source_target_pairs={{0,5},{1,4},{2,7},{3,6},{4,1},{5,0},{6,3},{7,2},{8,13},{9,12},{10,... | collective-permute-start | bytes 153608 | tf_op jit(solution)/shard_map/ppermute | solution.py:353
  11.6 3.8 %load.3 = (bf16[8,3200]{1,0:T(8,128)(2,1)S(1)}, bf16[768,2048]{1,0:T(8,128)(2,1)S(1)}, bf16[768,2048]{1,0:T(8,128)(2,1)S(1)}, bf16[768,2048]{1,0:T(8,128)(2,1)S(1)}) custom-call(bf16[8,3200]{1,0:T(8,128)(2,1)S(1)} %pad_maximum_fusion.refs_0_, bf16[2,1536,2048]{2,1,0:T(8,128)(2,1)} %refs_3_.3, bf16[2,1536,2048]{2,1,0:T(8,128)(2,1)} %refs_3_.3, ...), custom_call_target="tpu_custom_call" | custom-call | bytes 10485760 | tf_op jit(solution)/shard_map/load/pallas_call | solution.py:418
  15.4 0.1 collective-permute-done.1.refs_1_
  15.5 0.6 %collective-permute-start.4 = (bf16[32,1664]{1,0:T(8,128)(2,1)S(1)}, bf16[32,1664]{1,0:T(8,128)(2,1)S(1)}, u32[]{:S(2)}, u32[]{:S(2)}) collective-permute-start(bf16[32,1664]{1,0:T(8,128)(2,1)S(1)} %get-tuple-element.36), channel_id=1, source_target_pairs={{0,1},{1,0},{2,3},{3,2},{4,5},{5,4},{6,7},{7,6},{8,9},{9,8},{10,11... | collective-permute-start | bytes 319496 | tf_op jit(solution)/shard_map/ppermute | solution.py:351
  16.1 1.0 %collective-permute-done.4.refs_1_ = bf16[32,1664]{1,0:T(8,128)(2,1)S(1)} collective-permute-done((bf16[32,1664]{1,0:T(8,128)(2,1)S(1)}, bf16[32,1664]{1,0:T(8,128)(2,1)S(1)}, u32[]{:S(2)}, u32[]{:S(2)}) %collective-permute-start.4) | collective-permute-done | bytes 106528 | tf_op jit(solution)/shard_map/ppermute | solution.py:351
  17.0 0.0 slice-start
  17.1 0.0 slice-start.1
  17.1 1.9 %gate_up.2.refs_2_ = bf16[64,4096]{1,0:T(8,128)(2,1)S(1)} custom-call(bf16[32,1664]{1,0:T(8,128)(2,1)S(1)} %get-tuple-element.35.refs_0_, bf16[32,1664]{1,0:T(8,128)(2,1)S(1)} %collective-permute-done.4.refs_1_, f32[2,12,2048]{2,1,0:T(8,128)S(1)} %get-tuple-element.37.refs_2_, f32[2,12,2048]{2,1,0:T(8,128)S(1)} %get-tuple-element.38.refs_3_, ...), custom_call_target="tpu_custom_call" | custom-call | bytes 2097152 | tf_op jit(solution)/shard_map/gate_up/pallas_call | solution.py:418
  19.0 0.4 %collective-permute-start.6 = (bf16[64,4096]{1,0:T(8,128)(2,1)S(1)}, bf16[64,4096]{1,0:T(8,128)(2,1)S(1)}, u32[]{:S(2)}, u32[]{:S(2)}) collective-permute-start(bf16[64,4096]{1,0:T(8,128)(2,1)S(1)} %gate_up.2.refs_2_), channel_id=1, source_target_pairs={{0,1},{1,0},{2,3},{3,2},{4,5},{5,4},{6,7},{7,6},{8,9},{9,8},{10,11... | collective-permute-start | bytes 1572872 | tf_op jit(solution)/shard_map/ppermute | solution.py:351
  19.4 1.9 %gate_up.3.refs_2_ = bf16[64,4096]{1,0:T(8,128)(2,1)S(1)} custom-call(bf16[32,1664]{1,0:T(8,128)(2,1)S(1)} %get-tuple-element.35.refs_0_, bf16[32,1664]{1,0:T(8,128)(2,1)S(1)} %collective-permute-done.4.refs_1_, f32[2,12,2048]{2,1,0:T(8,128)S(1)} %get-tuple-element.37.refs_2_, f32[2,12,2048]{2,1,0:T(8,128)S(1)} %get-tuple-element.38.refs_3_, ...), custom_call_target="tpu_custom_call" | custom-call | bytes 2097152 | tf_op jit(solution)/shard_map/gate_up/pallas_call | solution.py:418
  21.4 0.2 collective-permute-start.5
  21.6 0.4 slice-done.2
  21.9 1.1 %down.2.refs_6_ = f32[64,1536]{1,0:T(8,128)S(1)} custom-call(bf16[32,1664]{1,0:T(8,128)(2,1)S(1)} %get-tuple-element.35.refs_0_, bf16[32,1664]{1,0:T(8,128)(2,1)S(1)} %collective-permute-done.4.refs_1_, bf16[64,4096]{1,0:T(8,128)(2,1)S(1)} %gate_up.2.refs_2_, bf16[64,4096]{1,0:T(8,128)(2,1)S(1)} %collective-permute-done.6.refs_3_, ...), custom_call_target="tpu_custom_call" | custom-call | bytes 4194304 | tf_op jit(solution)/shard_map/down/pallas_call | solution.py:418
  23.1 0.3 collective-permute-done.5.refs_3_
  23.3 1.1 %down.3 = (bf16[32,1536]{1,0:T(8,128)(2,1)S(1)}, bf16[32,1536]{1,0:T(8,128)(2,1)S(1)}) custom-call(bf16[32,1664]{1,0:T(8,128)(2,1)S(1)} %get-tuple-element.35.refs_0_, bf16[32,1664]{1,0:T(8,128)(2,1)S(1)} %collective-permute-done.4.refs_1_, bf16[64,4096]{1,0:T(8,128)(2,1)S(1)} %gate_up.3.refs_2_, bf16[64,4096]{1,0:T(8,128)(2,1)S(1)} %collective-permute-done.5.refs_3_, ...), custom_call_target="tpu_custom_call" | custom-call | bytes 4194304 | tf_op jit(solution)/shard_map/down/pallas_call | solution.py:418
  24.5 0.2 collective-permute-start.7
  24.7 1.2 %collective-permute-done.7.other_ref = bf16[32,1536]{1,0:T(8,128)(2,1)S(1)} collective-permute-done((bf16[32,1536]{1,0:T(8,128)(2,1)S(1)}, bf16[32,1536]{1,0:T(8,128)(2,1)S(1)}, u32[]{:S(2)}, u32[]{:S(2)}) %collective-permute-start.7) | collective-permute-done | bytes 98336 | tf_op jit(solution)/shard_map/ppermute | solution.py:351
  25.9 3.1 %collective-permute-start.8 = (bf16[8,3072]{1,0:T(8,128)(2,1)S(1)}, bf16[8,3072]{1,0:T(8,128)(2,1)S(1)}, u32[]{:S(2)}, u32[]{:S(2)}) collective-permute-start(bf16[8,3072]{1,0:T(8,128)(2,1)S(1)} %get-tuple-element.48), channel_id=1, source_target_pairs={{0,7},{1,6},{2,5},{3,4},{4,3},{5,2},{6,1},{7,0},{8,15},{9,14},{10,... | collective-permute-start | bytes 147464 | tf_op jit(solution)/shard_map/ppermute | solution.py:353
  29.0 0.8 %collective-permute-start.10 = (bf16[8,3072]{1,0:T(8,128)(2,1)S(1)}, bf16[8,3072]{1,0:T(8,128)(2,1)S(1)}, u32[]{:S(2)}, u32[]{:S(2)}) collective-permute-start(bf16[8,3072]{1,0:T(8,128)(2,1)S(1)} %get-tuple-element.50), channel_id=1, source_target_pairs={{0,5},{1,4},{2,7},{3,6},{4,1},{5,0},{6,3},{7,2},{8,13},{9,12},{10,... | collective-permute-start | bytes 147464 | tf_op jit(solution)/shard_map/ppermute | solution.py:353
  29.8 1.7 %collective-permute-done.8 = bf16[8,3072]{1,0:T(8,128)(2,1)S(1)} collective-permute-done((bf16[8,3072]{1,0:T(8,128)(2,1)S(1)}, bf16[8,3072]{1,0:T(8,128)(2,1)S(1)}, u32[]{:S(2)}, u32[]{:S(2)}) %collective-permute-start.8) | collective-permute-done | bytes 49184 | tf_op jit(solution)/shard_map/ppermute | solution.py:353
  31.6 1.0 %collective-permute-done.9 = bf16[8,3072]{1,0:T(8,128)(2,1)S(1)} collective-permute-done((bf16[8,3072]{1,0:T(8,128)(2,1)S(1)}, bf16[8,3072]{1,0:T(8,128)(2,1)S(1)}, u32[]{:S(2)}, u32[]{:S(2)}) %collective-permute-start.9) | collective-permute-done | bytes 49184 | tf_op jit(solution)/shard_map/ppermute | solution.py:353
  32.5 1.0 %collective-permute-done.10 = bf16[8,3072]{1,0:T(8,128)(2,1)S(1)} collective-permute-done((bf16[8,3072]{1,0:T(8,128)(2,1)S(1)}, bf16[8,3072]{1,0:T(8,128)(2,1)S(1)}, u32[]{:S(2)}, u32[]{:S(2)}) %collective-permute-start.10) | collective-permute-done | bytes 49184 | tf_op jit(solution)/shard_map/ppermute | solution.py:353
  33.6 1.6 %collective-permute-start.11 = (bf16[4,3072]{1,0:T(4,128)(2,1)S(1)}, bf16[4,3072]{1,0:T(4,128)(2,1)S(1)}, u32[]{:S(2)}, u32[]{:S(2)}) collective-permute-start(bf16[4,3072]{1,0:T(4,128)(2,1)S(1)} %get-tuple-element.51), channel_id=1, source_target_pairs={{0,9},{1,8},{8,1},{9,0},{2,11},{3,10},{10,3},{11,2},{4,13},{5,12},... | collective-permute-start | bytes 73736 | tf_op jit(solution)/shard_map/ppermute | solution.py:353
  35.2 1.7 %collective-permute-done.11.refs_1_ = bf16[4,3072]{1,0:T(4,128)(2,1)S(1)} collective-permute-done((bf16[4,3072]{1,0:T(4,128)(2,1)S(1)}, bf16[4,3072]{1,0:T(4,128)(2,1)S(1)}, u32[]{:S(2)}, u32[]{:S(2)}) %collective-permute-start.11) | collective-permute-done | bytes 24608 | tf_op jit(solution)/shard_map/ppermute | solution.py:353
  36.9 0.6 %finish.1 = bf16[4,3072]{1,0:T(4,128)(2,1)} custom-call(f32[4,3072]{1,0:T(4,128)S(1)} %get-tuple-element.28.stream_ref, bf16[4,3072]{1,0:T(4,128)(2,1)S(1)} %get-tuple-element.52.refs_0_, bf16[4,3072]{1,0:T(4,128)(2,1)S(1)} %collective-permute-done.11.refs_1_), custom_call_target="tpu_custom_call" | custom-call | tf_op jit(solution)/shard_map/finish/pallas_call | solution.py:372
  (19 shorter events, 0.2 us)
Async XLA Ops:
  2.5 4.4 %collective-permute-start = (bf16[4,3200]{1,0:T(4,128)(2,1)S(1)}, bf16[4,3200]{1,0:T(4,128)(2,1)S(1)}, u32[]{:S(2)}, u32[]{:S(2)}) collective-permute-start(bf16[4,3200]{1,0:T(4,128)(2,1)S(1)} %get-tuple-element.29.refs_0_), channel_id=1, source_target_pairs={{0,9},{1,8},{8,1},{9,0},{2,11},{3,10},{10,3},{11,2},{4,13},{5,12},... | collective-permute-start | bytes 76808 | tf_op jit(solution)/shard_map/ppermute | solution.py:353
  6.8 10.2 %slice-start.3 = ((s8[12582912]{0:T(1024)(128)(4,1)}), s8[4194304]{0:T(1024)(128)(4,1)S(1)}, s32[]{:S(2)}) async-start(s8[12582912]{0:T(1024)(128)(4,1)} %bitcast.8), calls=%async_computation.3 | async-start | bytes 8388608
  6.9 10.1 %slice-start.4 = ((s8[12582912]{0:T(1024)(128)(4,1)}), s8[4194304]{0:T(1024)(128)(4,1)S(1)}, s32[]{:S(2)}) async-start(s8[12582912]{0:T(1024)(128)(4,1)} %bitcast.8), calls=%async_computation.4 | async-start | bytes 8388608
  6.9 10.1 %slice-start.5 = ((s8[12582912]{0:T(1024)(128)(4,1)}), s8[4194304]{0:T(1024)(128)(4,1)S(1)}, s32[]{:S(2)}) async-start(s8[12582912]{0:T(1024)(128)(4,1)} %bitcast.8), calls=%async_computation.5 | async-start | bytes 8388608
  6.9 8.5 %collective-permute-start.3 = (bf16[8,3200]{1,0:T(8,128)(2,1)S(1)}, bf16[8,3200]{1,0:T(8,128)(2,1)S(1)}, u32[]{:S(2)}, u32[]{:S(2)}) collective-permute-start(bf16[8,3200]{1,0:T(8,128)(2,1)S(1)} %pad_maximum_fusion.refs_0_), channel_id=1, source_target_pairs={{0,7},{1,6},{2,5},{3,4},{4,3},{5,2},{6,1},{7,0},{8,15},{9,14},{10,... | collective-permute-start | bytes 153608 | tf_op jit(solution)/shard_map/ppermute | solution.py:353
  10.9 4.5 %collective-permute-start.2 = (bf16[8,3200]{1,0:T(8,128)(2,1)S(1)}, bf16[8,3200]{1,0:T(8,128)(2,1)S(1)}, u32[]{:S(2)}, u32[]{:S(2)}) collective-permute-start(bf16[8,3200]{1,0:T(8,128)(2,1)S(1)} %pad_maximum_fusion.refs_0_), channel_id=1, source_target_pairs={{0,3},{1,2},{2,1},{3,0},{4,7},{5,6},{6,5},{7,4},{8,11},{9,10},{10,... | collective-permute-start | bytes 153608 | tf_op jit(solution)/shard_map/ppermute | solution.py:353
  10.9 4.5 %collective-permute-start.1 = (bf16[8,3200]{1,0:T(8,128)(2,1)S(1)}, bf16[8,3200]{1,0:T(8,128)(2,1)S(1)}, u32[]{:S(2)}, u32[]{:S(2)}) collective-permute-start(bf16[8,3200]{1,0:T(8,128)(2,1)S(1)} %pad_maximum_fusion.refs_0_), channel_id=1, source_target_pairs={{0,5},{1,4},{2,7},{3,6},{4,1},{5,0},{6,3},{7,2},{8,13},{9,12},{10,... | collective-permute-start | bytes 153608 | tf_op jit(solution)/shard_map/ppermute | solution.py:353
  15.5 1.5 %collective-permute-start.4 = (bf16[32,1664]{1,0:T(8,128)(2,1)S(1)}, bf16[32,1664]{1,0:T(8,128)(2,1)S(1)}, u32[]{:S(2)}, u32[]{:S(2)}) collective-permute-start(bf16[32,1664]{1,0:T(8,128)(2,1)S(1)} %get-tuple-element.36), channel_id=1, source_target_pairs={{0,1},{1,0},{2,3},{3,2},{4,5},{5,4},{6,7},{7,6},{8,9},{9,8},{10,11... | collective-permute-start | bytes 319496 | tf_op jit(solution)/shard_map/ppermute | solution.py:351
  17.0 4.5 %slice-start = ((s8[12582912]{0:T(1024)(128)(4,1)}), s8[4194304]{0:T(1024)(128)(4,1)S(1)}, s32[]{:S(2)}) async-start(s8[12582912]{0:T(1024)(128)(4,1)} %bitcast.6), calls=%async_computation | async-start | bytes 8388608
  17.1 4.5 %slice-start.1 = ((s8[12582912]{0:T(1024)(128)(4,1)}), s8[4194304]{0:T(1024)(128)(4,1)S(1)}, s32[]{:S(2)}) async-start(s8[12582912]{0:T(1024)(128)(4,1)} %bitcast.6), calls=%async_computation.1 | async-start | bytes 8388608
  19.0 2.6 %collective-permute-start.6 = (bf16[64,4096]{1,0:T(8,128)(2,1)S(1)}, bf16[64,4096]{1,0:T(8,128)(2,1)S(1)}, u32[]{:S(2)}, u32[]{:S(2)}) collective-permute-start(bf16[64,4096]{1,0:T(8,128)(2,1)S(1)} %gate_up.2.refs_2_), channel_id=1, source_target_pairs={{0,1},{1,0},{2,3},{3,2},{4,5},{5,4},{6,7},{7,6},{8,9},{9,8},{10,11... | collective-permute-start | bytes 1572872 | tf_op jit(solution)/shard_map/ppermute | solution.py:351
  19.4 2.5 %slice-start.2 = ((s8[12582912]{0:T(1024)(128)(4,1)}), s8[4194304]{0:T(1024)(128)(4,1)S(1)}, s32[]{:S(2)}) async-start(s8[12582912]{0:T(1024)(128)(4,1)} %bitcast.6), calls=%async_computation.2 | async-start | bytes 8388608
  21.4 2.0 %collective-permute-start.5 = (bf16[64,4096]{1,0:T(8,128)(2,1)S(1)}, bf16[64,4096]{1,0:T(8,128)(2,1)S(1)}, u32[]{:S(2)}, u32[]{:S(2)}) collective-permute-start(bf16[64,4096]{1,0:T(8,128)(2,1)S(1)} %gate_up.3.refs_2_), channel_id=1, source_target_pairs={{0,1},{1,0},{2,3},{3,2},{4,5},{5,4},{6,7},{7,6},{8,9},{9,8},{10,11... | collective-permute-start | bytes 1572872 | tf_op jit(solution)/shard_map/ppermute | solution.py:351
  24.5 1.4 %collective-permute-start.7 = (bf16[32,1536]{1,0:T(8,128)(2,1)S(1)}, bf16[32,1536]{1,0:T(8,128)(2,1)S(1)}, u32[]{:S(2)}, u32[]{:S(2)}) collective-permute-start(bf16[32,1536]{1,0:T(8,128)(2,1)S(1)} %get-tuple-element.46), channel_id=1, source_target_pairs={{0,1},{1,0},{2,3},{3,2},{4,5},{5,4},{6,7},{7,6},{8,9},{9,8},{10,11... | collective-permute-start | bytes 294920 | tf_op jit(solution)/shard_map/ppermute | solution.py:351
  25.9 5.7 %collective-permute-start.8 = (bf16[8,3072]{1,0:T(8,128)(2,1)S(1)}, bf16[8,3072]{1,0:T(8,128)(2,1)S(1)}, u32[]{:S(2)}, u32[]{:S(2)}) collective-permute-start(bf16[8,3072]{1,0:T(8,128)(2,1)S(1)} %get-tuple-element.48), channel_id=1, source_target_pairs={{0,7},{1,6},{2,5},{3,4},{4,3},{5,2},{6,1},{7,0},{8,15},{9,14},{10,... | collective-permute-start | bytes 147464 | tf_op jit(solution)/shard_map/ppermute | solution.py:353
  29.0 3.5 %collective-permute-start.9 = (bf16[8,3072]{1,0:T(8,128)(2,1)S(1)}, bf16[8,3072]{1,0:T(8,128)(2,1)S(1)}, u32[]{:S(2)}, u32[]{:S(2)}) collective-permute-start(bf16[8,3072]{1,0:T(8,128)(2,1)S(1)} %get-tuple-element.49), channel_id=1, source_target_pairs={{0,3},{1,2},{2,1},{3,0},{4,7},{5,6},{6,5},{7,4},{8,11},{9,10},{10,... | collective-permute-start | bytes 147464 | tf_op jit(solution)/shard_map/ppermute | solution.py:353
  29.0 4.5 %collective-permute-start.10 = (bf16[8,3072]{1,0:T(8,128)(2,1)S(1)}, bf16[8,3072]{1,0:T(8,128)(2,1)S(1)}, u32[]{:S(2)}, u32[]{:S(2)}) collective-permute-start(bf16[8,3072]{1,0:T(8,128)(2,1)S(1)} %get-tuple-element.50), channel_id=1, source_target_pairs={{0,5},{1,4},{2,7},{3,6},{4,1},{5,0},{6,3},{7,2},{8,13},{9,12},{10,... | collective-permute-start | bytes 147464 | tf_op jit(solution)/shard_map/ppermute | solution.py:353
  33.6 3.3 %collective-permute-start.11 = (bf16[4,3072]{1,0:T(4,128)(2,1)S(1)}, bf16[4,3072]{1,0:T(4,128)(2,1)S(1)}, u32[]{:S(2)}, u32[]{:S(2)}) collective-permute-start(bf16[4,3072]{1,0:T(4,128)(2,1)S(1)} %get-tuple-element.51), channel_id=1, source_target_pairs={{0,9},{1,8},{8,1},{9,0},{2,11},{3,10},{10,3},{11,2},{4,13},{5,12},... | collective-permute-start | bytes 73736 | tf_op jit(solution)/shard_map/ppermute | solution.py:353

commit v7 on v6

--- a/solution.py
+++ b/solution.py
@@ -21,9 +21,9 @@
 VMEM_LIMIT = 16 << 20
 
 LOAD_ATTEND = 0
-LOAD_STEP = (1, 3)
-ORDER = (2, 1, 3)
-RETURN = (3, 2, 1)
+LOAD_STEP = (2, 2)
+ORDER = ((1, 0), (0, 1), (1, 1))
+RETURN = (3, 1, 2)
 LOAD_GATE_UP = 2
 LOAD_DOWN = 1
 WIDTH = 512
@@ -346,26 +346,27 @@
     out_ref[...] = total.astype(jnp.bfloat16)
 
 
-def swap(x, axis, bit):
-    if axis is None:
+def swap(x, offset):
+    if offset is None:
         return lax.ppermute(x, "sub", [(0, 1), (1, 0)])
-    count = 2 * lax.axis_size(axis)
-    return lax.ppermute(x, (axis, "sub"), [(i, i ^ (2 * bit + 1)) for i in range(count)])
-
-
-def digits(axis, base):
-    size, unit, rounds = lax.axis_size(axis), 1, []
-    while unit < size:
-        span = min(base, size // unit)
-        order = ORDER if span == 4 else (1,)
-        rounds.append((axis, tuple(unit * i for i in order)))
-        unit *= span
-    return rounds
-
-
-def returned_pieces(pieces, axis, offsets):
+    roles, columns = lax.axis_size("role"), lax.axis_size("tp")
+    flip = 2 * (offset[0] * columns + offset[1]) + 1
+    pairs = [(i, i ^ flip) for i in range(2 * roles * columns)]
+    return lax.ppermute(x, ("role", "tp", "sub"), pairs)
+
+
+def rounds():
+    roles, columns = lax.axis_size("role"), lax.axis_size("tp")
+    bits = [1 << b for b in reversed(range(1, max(roles, columns).bit_length()))]
+    steps = [((0, bit),) for bit in bits if bit < columns]
+    steps += [((bit, 0),) for bit in bits if bit < roles]
+    lowest = [pair for pair in ORDER if pair[0] < roles and pair[1] < columns]
+    return steps + [tuple(lowest)]
+
+
+def returned_pieces(pieces, offsets):
     near, *far = pieces
-    return [near, *[swap(piece, axis, offset) for piece, offset in zip(far, offsets)]]
+    return [near, *[swap(piece, offset) for piece, offset in zip(far, offsets)]]
 
 
 def local_call(kernel, outputs, inputs, name):
@@ -520,13 +521,13 @@
         "attend",
         4 << 20,
     )
-    steps = digits("role", 2) + digits("tp", 4)
+    steps = rounds()
     spread_scales = None
     near, far = x, []
-    for number, (axis, offsets) in enumerate(steps):
+    for number, offsets in enumerate(steps):
         if far:
             near = jnp.concatenate([near, *far], axis=0)
-        far = [swap(near, axis, offset) for offset in offsets]
+        far = [swap(near, offset) for offset in offsets]
         taken = loader.take(LOAD_STEP[min(number, len(LOAD_STEP) - 1)])
         if spread_scales is None:
             near, *spread_scales = load_more(loader, taken, near, scales)
@@ -536,7 +537,7 @@
     count = (1 + len(far)) * near.shape[0]
     piece = jax.ShapeDtypeStruct((count, extended), jnp.bfloat16)
     kept, sent = local_call(split_kernel, (piece, piece), (near, *far), "split")
-    other = swap(sent, None, 0)
+    other = swap(sent, None)
     parts = []
     before = other
     for e in range(experts):
@@ -554,7 +555,7 @@
             2 << 20,
             expert=e,
         )
-        parts.append((part, swap(part, None, 0)))
+        parts.append((part, swap(part, None)))
         before, _ = lax.optimization_barrier((before, part))
     carried = []
     for e in range(experts):
@@ -574,19 +575,19 @@
             experts=experts,
         )
     kept, sent = carried
-    axis, offsets = steps[-1]
+    offsets = steps[-1]
     parts = 1 + len(offsets)
     piece = jax.ShapeDtypeStruct((count // parts, D), jnp.bfloat16)
     blocks = [0, *RETURN] if parts == 4 else list(range(parts))
     offsets = tuple(offsets[block - 1] for block in blocks[1:])
     joined = functools.partial(join_kernel, blocks=tuple(blocks))
-    pieces = local_call(joined, (piece,) * parts, (kept, swap(sent, None, 0)), "join")
+    pieces = local_call(joined, (piece,) * parts, (kept, swap(sent, None)), "join")
     for following, _ in zip(reversed(steps[:-1]), steps[1:]):
-        carried = add_bf16(returned_pieces(pieces, axis, offsets))
-        axis, offsets = following
+        carried = add_bf16(returned_pieces(pieces, offsets))
+        offsets = following
         pieces = jnp.split(carried, 1 + len(offsets))
     out = jax.ShapeDtypeStruct((rows, D), jnp.bfloat16)
-    return local_call(finish_kernel, out, (stream, *returned_pieces(pieces, axis, offsets)), "finish")
+    return local_call(finish_kernel, out, (stream, *returned_pieces(pieces, offsets)), "finish")
 
 
 def solution(mesh):

time: 37.7 us -> 37.4 us (level)
  starting transfers between devices: 14.1 us -> 13.6 us
  transfers between devices with their start and end apart: 12 -> 12, of which waited for: 8 -> 7; matrix products, arithmetic and copies ran while one was open for 0% -> 0% of each run, Pallas kernels for 23% -> 24%
where the time goes in v7:
time: 37.4 us; the launch traced here: 37.2 us
  Pallas kernels  14.9 us (40%)
  starting transfers between devices  13.6 us (36%)
  waiting for transfers between devices  7.97 us (21%)
  local copies, waits for them, and re-layouts  0.51 us (1%)
    pallas_call x7, Pallas kernels, call(): pl.pallas_call(functools.partial(kernel, places=tuple(((e, p) for _, e, p...  14.2 us
    ppermute x8, starting transfers between devices, swap(): return lax.ppermute(x, ('role', 'tp', 'sub'), pairs)  12.4 us
    ppermute x8, waiting for transfers between devices, swap(): return lax.ppermute(x, ('role', 'tp', 'sub'), pairs)  5.83 us
    ppermute x4, waiting for transfers between devices, swap(): return lax.ppermute(x, 'sub', [(0, 1), (1, 0)])  2.14 us
    ppermute x4, starting transfers between devices, swap(): return lax.ppermute(x, 'sub', [(0, 1), (1, 0)])  1.27 us
  transfers between devices with their start and end apart: 12, of which 7 were waited for; matrix products, arithmetic and copies ran while one was open for 0% of the time, Pallas kernels for 24%

profile of v7, /device:TPU:0, one launch (start us, length us, event | category | flops | bytes accessed | tf_op | source)
XLA Modules:
  0.0 37.2 jit_solution(780160212888212552)
XLA Ops:
  0.0 2.5 %attend.1 = (bf16[4,3200]{1,0:T(4,128)(2,1)S(1)}, f32[4,3072]{1,0:T(4,128)S(1)}, f32[12,2,16]{2,1,0:T(2,128)S(1)}, f32[12,2,16]{2,1,0:T(2,128)S(1)}, f32[12,2,16]{2,1,0:T(2,128)S(1)}) custom-call(bf16[4,3072]{1,0:T(4,128)(2,1)} %refs_0_.1, bf16[4,1024]{1,0:T(4,128)(2,1)} %refs_1_.2, bf16[4,1024]{1,0:T(4,128)(2,1)} %refs_2_.2, s32[4]{0:T(128)} %refs_3_.1, ...), custom_call_target="tpu_custom_call" | custom-call | bytes 4194304 | tf_op jit(solution)/shard_map/attend/pallas_call | solution.py:419
  2.5 3.5 %collective-permute-start = (bf16[4,3200]{1,0:T(4,128)(2,1)S(1)}, bf16[4,3200]{1,0:T(4,128)(2,1)S(1)}, u32[]{:S(2)}, u32[]{:S(2)}) collective-permute-start(bf16[4,3200]{1,0:T(4,128)(2,1)S(1)} %get-tuple-element.29.refs_0_), channel_id=1, source_target_pairs={{0,5},{1,4},{2,7},{3,6},{4,1},{5,0},{6,3},{7,2},{8,13},{9,12},{10,... | collective-permute-start | bytes 76808 | tf_op jit(solution)/shard_map/ppermute | solution.py:355
  6.0 2.9 %load.2 = (bf16[4,3200]{1,0:T(4,128)(2,1)S(1)}, f32[2,12,2048]{2,1,0:T(8,128)S(1)}, f32[2,12,2048]{2,1,0:T(8,128)S(1)}, f32[2,16,1536]{2,1,0:T(8,128)S(1)}, bf16...) custom-call(bf16[4,3200]{1,0:T(4,128)(2,1)S(1)} %get-tuple-element.29.refs_0_, ...), custom_call_target="tpu_custom_call" | custom-call | bytes 7340032 | tf_op jit(solution)/shard_map/load/pallas_call | solution.py:419
  8.9 0.0 slice-start.3
  9.0 0.0 slice-start.4
  9.0 2.8 %collective-permute-start.3 = (bf16[8,3200]{1,0:T(8,128)(2,1)S(1)}, bf16[8,3200]{1,0:T(8,128)(2,1)S(1)}, u32[]{:S(2)}, u32[]{:S(2)}) collective-permute-start(bf16[8,3200]{1,0:T(8,128)(2,1)S(1)} %pad_maximum_fusion.refs_0_), channel_id=1, source_target_pairs={{0,11},{1,10},{2,9},{3,8},{4,15},{5,14},{6,13},{7,12},{8,3},{9,2},... | collective-permute-start | bytes 153608 | tf_op jit(solution)/shard_map/ppermute | solution.py:355
  11.8 0.7 %collective-permute-start.1 = (bf16[8,3200]{1,0:T(8,128)(2,1)S(1)}, bf16[8,3200]{1,0:T(8,128)(2,1)S(1)}, u32[]{:S(2)}, u32[]{:S(2)}) collective-permute-start(bf16[8,3200]{1,0:T(8,128)(2,1)S(1)} %pad_maximum_fusion.refs_0_), channel_id=1, source_target_pairs={{0,9},{1,8},{2,11},{3,10},{4,13},{5,12},{6,15},{7,14},{8,1},{9,0},... | collective-permute-start | bytes 153608 | tf_op jit(solution)/shard_map/ppermute | solution.py:355
  12.5 2.9 %load.3 = (bf16[8,3200]{1,0:T(8,128)(2,1)S(1)}, bf16[768,2048]{1,0:T(8,128)(2,1)S(1)}, bf16[768,2048]{1,0:T(8,128)(2,1)S(1)}) custom-call(bf16[8,3200]{1,0:T(8,128)(2,1)S(1)} %pad_maximum_fusion.refs_0_, bf16[2,1536,2048]{2,1,0:T(8,128)(2,1)} %refs_2_.3, bf16[2,1536,2048]{2,1,0:T(8,128)(2,1)} %refs_2_.3), custom_call_target="tpu_custom_call" | custom-call | bytes 7340032 | tf_op jit(solution)/shard_map/load/pallas_call | solution.py:419
  15.4 0.5 %collective-permute-done.2.refs_2_ = bf16[8,3200]{1,0:T(8,128)(2,1)S(1)} collective-permute-done((bf16[8,3200]{1,0:T(8,128)(2,1)S(1)}, bf16[8,3200]{1,0:T(8,128)(2,1)S(1)}, u32[]{:S(2)}, u32[]{:S(2)}) %collective-permute-start.2) | collective-permute-done | bytes 51232 | tf_op jit(solution)/shard_map/ppermute | solution.py:355
  15.9 0.3 collective-permute-start.4
  16.2 1.1 %collective-permute-done.4.refs_1_ = bf16[32,1664]{1,0:T(8,128)(2,1)S(1)} collective-permute-done((bf16[32,1664]{1,0:T(8,128)(2,1)S(1)}, bf16[32,1664]{1,0:T(8,128)(2,1)S(1)}, u32[]{:S(2)}, u32[]{:S(2)}) %collective-permute-start.4) | collective-permute-done | bytes 106528 | tf_op jit(solution)/shard_map/ppermute | solution.py:351
  17.3 0.0 slice-start
  17.3 0.0 slice-start.1
  17.4 1.9 %gate_up.2.refs_2_ = bf16[64,4096]{1,0:T(8,128)(2,1)S(1)} custom-call(bf16[32,1664]{1,0:T(8,128)(2,1)S(1)} %get-tuple-element.35.refs_0_, bf16[32,1664]{1,0:T(8,128)(2,1)S(1)} %collective-permute-done.4.refs_1_, f32[2,12,2048]{2,1,0:T(8,128)S(1)} %get-tuple-element.37.refs_2_, f32[2,12,2048]{2,1,0:T(8,128)S(1)} %get-tuple-element.38.refs_3_, ...), custom_call_target="tpu_custom_call" | custom-call | bytes 2097152 | tf_op jit(solution)/shard_map/gate_up/pallas_call | solution.py:419
  19.2 0.3 collective-permute-start.6
  19.5 1.9 %gate_up.3.refs_2_ = bf16[64,4096]{1,0:T(8,128)(2,1)S(1)} custom-call(bf16[32,1664]{1,0:T(8,128)(2,1)S(1)} %get-tuple-element.35.refs_0_, bf16[32,1664]{1,0:T(8,128)(2,1)S(1)} %collective-permute-done.4.refs_1_, f32[2,12,2048]{2,1,0:T(8,128)S(1)} %get-tuple-element.37.refs_2_, f32[2,12,2048]{2,1,0:T(8,128)S(1)} %get-tuple-element.38.refs_3_, ...), custom_call_target="tpu_custom_call" | custom-call | bytes 2097152 | tf_op jit(solution)/shard_map/gate_up/pallas_call | solution.py:419
  21.4 0.3 collective-permute-start.5
  21.7 0.5 %slice-done.2 = s8[4194304]{0:T(1024)(128)(4,1)S(1)} async-done(((s8[12582912]{0:T(1024)(128)(4,1)}), s8[4194304]{0:T(1024)(128)(4,1)S(1)}, s32[]{:S(2)}) %slice-start.2) | async-done | bytes 4194328
  22.2 1.1 %down.2.refs_6_ = f32[64,1536]{1,0:T(8,128)S(1)} custom-call(bf16[32,1664]{1,0:T(8,128)(2,1)S(1)} %get-tuple-element.35.refs_0_, bf16[32,1664]{1,0:T(8,128)(2,1)S(1)} %collective-permute-done.4.refs_1_, bf16[64,4096]{1,0:T(8,128)(2,1)S(1)} %gate_up.2.refs_2_, bf16[64,4096]{1,0:T(8,128)(2,1)S(1)} %collective-permute-done.6.refs_3_, ...), custom_call_target="tpu_custom_call" | custom-call | bytes 4194304 | tf_op jit(solution)/shard_map/down/pallas_call | solution.py:419
  23.3 0.0 collective-permute-done.5.refs_3_
  23.4 1.1 %down.3 = (bf16[32,1536]{1,0:T(8,128)(2,1)S(1)}, bf16[32,1536]{1,0:T(8,128)(2,1)S(1)}) custom-call(bf16[32,1664]{1,0:T(8,128)(2,1)S(1)} %get-tuple-element.35.refs_0_, bf16[32,1664]{1,0:T(8,128)(2,1)S(1)} %collective-permute-done.4.refs_1_, bf16[64,4096]{1,0:T(8,128)(2,1)S(1)} %gate_up.3.refs_2_, bf16[64,4096]{1,0:T(8,128)(2,1)S(1)} %collective-permute-done.5.refs_3_, ...), custom_call_target="tpu_custom_call" | custom-call | bytes 4194304 | tf_op jit(solution)/shard_map/down/pallas_call | solution.py:419
  24.5 0.3 collective-permute-start.7
  24.9 1.0 %collective-permute-done.7.other_ref = bf16[32,1536]{1,0:T(8,128)(2,1)S(1)} collective-permute-done((bf16[32,1536]{1,0:T(8,128)(2,1)S(1)}, bf16[32,1536]{1,0:T(8,128)(2,1)S(1)}, u32[]{:S(2)}, u32[]{:S(2)}) %collective-permute-start.7) | collective-permute-done | bytes 98336 | tf_op jit(solution)/shard_map/ppermute | solution.py:351
  25.9 2.3 %collective-permute-start.8 = (bf16[8,3072]{1,0:T(8,128)(2,1)S(1)}, bf16[8,3072]{1,0:T(8,128)(2,1)S(1)}, u32[]{:S(2)}, u32[]{:S(2)}) collective-permute-start(bf16[8,3072]{1,0:T(8,128)(2,1)S(1)} %get-tuple-element.48), channel_id=1, source_target_pairs={{0,11},{1,10},{2,9},{3,8},{4,15},{5,14},{6,13},{7,12},{8,3},{9,2},... | collective-permute-start | bytes 147464 | tf_op jit(solution)/shard_map/ppermute | solution.py:355
  28.2 0.4 %collective-permute-start.9 = (bf16[8,3072]{1,0:T(8,128)(2,1)S(1)}, bf16[8,3072]{1,0:T(8,128)(2,1)S(1)}, u32[]{:S(2)}, u32[]{:S(2)}) collective-permute-start(bf16[8,3072]{1,0:T(8,128)(2,1)S(1)} %get-tuple-element.49), channel_id=1, source_target_pairs={{0,9},{1,8},{2,11},{3,10},{4,13},{5,12},{6,15},{7,14},{8,1},{9,0},... | collective-permute-start | bytes 147464 | tf_op jit(solution)/shard_map/ppermute | solution.py:355
  28.6 0.4 %collective-permute-start.10 = (bf16[8,3072]{1,0:T(8,128)(2,1)S(1)}, bf16[8,3072]{1,0:T(8,128)(2,1)S(1)}, u32[]{:S(2)}, u32[]{:S(2)}) collective-permute-start(bf16[8,3072]{1,0:T(8,128)(2,1)S(1)} %get-tuple-element.50), channel_id=1, source_target_pairs={{0,3},{1,2},{2,1},{3,0},{4,7},{5,6},{6,5},{7,4},{8,11},{9,10},{10,... | collective-permute-start | bytes 147464 | tf_op jit(solution)/shard_map/ppermute | solution.py:355
  29.1 1.5 %collective-permute-done.8 = bf16[8,3072]{1,0:T(8,128)(2,1)S(1)} collective-permute-done((bf16[8,3072]{1,0:T(8,128)(2,1)S(1)}, bf16[8,3072]{1,0:T(8,128)(2,1)S(1)}, u32[]{:S(2)}, u32[]{:S(2)}) %collective-permute-start.8) | collective-permute-done | bytes 49184 | tf_op jit(solution)/shard_map/ppermute | solution.py:355
  30.5 1.3 %collective-permute-done.9 = bf16[8,3072]{1,0:T(8,128)(2,1)S(1)} collective-permute-done((bf16[8,3072]{1,0:T(8,128)(2,1)S(1)}, bf16[8,3072]{1,0:T(8,128)(2,1)S(1)}, u32[]{:S(2)}, u32[]{:S(2)}) %collective-permute-start.9) | collective-permute-done | bytes 49184 | tf_op jit(solution)/shard_map/ppermute | solution.py:355
  31.8 0.5 %collective-permute-done.10 = bf16[8,3072]{1,0:T(8,128)(2,1)S(1)} collective-permute-done((bf16[8,3072]{1,0:T(8,128)(2,1)S(1)}, bf16[8,3072]{1,0:T(8,128)(2,1)S(1)}, u32[]{:S(2)}, u32[]{:S(2)}) %collective-permute-start.10) | collective-permute-done | bytes 49184 | tf_op jit(solution)/shard_map/ppermute | solution.py:355
  32.4 2.1 %collective-permute-start.11 = (bf16[4,3072]{1,0:T(4,128)(2,1)S(1)}, bf16[4,3072]{1,0:T(4,128)(2,1)S(1)}, u32[]{:S(2)}, u32[]{:S(2)}) collective-permute-start(bf16[4,3072]{1,0:T(4,128)(2,1)S(1)} %get-tuple-element.51), channel_id=1, source_target_pairs={{0,5},{1,4},{2,7},{3,6},{4,1},{5,0},{6,3},{7,2},{8,13},{9,12},{10,... | collective-permute-start | bytes 73736 | tf_op jit(solution)/shard_map/ppermute | solution.py:355
  34.5 2.1 %collective-permute-done.11.refs_1_ = bf16[4,3072]{1,0:T(4,128)(2,1)S(1)} collective-permute-done((bf16[4,3072]{1,0:T(4,128)(2,1)S(1)}, bf16[4,3072]{1,0:T(4,128)(2,1)S(1)}, u32[]{:S(2)}, u32[]{:S(2)}) %collective-permute-start.11) | collective-permute-done | bytes 24608 | tf_op jit(solution)/shard_map/ppermute | solution.py:355
  36.6 0.6 %finish.1 = bf16[4,3072]{1,0:T(4,128)(2,1)} custom-call(f32[4,3072]{1,0:T(4,128)S(1)} %get-tuple-element.28.stream_ref, bf16[4,3072]{1,0:T(4,128)(2,1)S(1)} %get-tuple-element.52.refs_0_, bf16[4,3072]{1,0:T(4,128)(2,1)S(1)} %collective-permute-done.11.refs_1_), custom_call_target="tpu_custom_call" | custom-call | tf_op jit(solution)/shard_map/finish/pallas_call | solution.py:373
  (19 shorter events, 0.2 us)
Async XLA Ops:
  2.5 6.4 %collective-permute-start = (bf16[4,3200]{1,0:T(4,128)(2,1)S(1)}, bf16[4,3200]{1,0:T(4,128)(2,1)S(1)}, u32[]{:S(2)}, u32[]{:S(2)}) collective-permute-start(bf16[4,3200]{1,0:T(4,128)(2,1)S(1)} %get-tuple-element.29.refs_0_), channel_id=1, source_target_pairs={{0,5},{1,4},{2,7},{3,6},{4,1},{5,0},{6,3},{7,2},{8,13},{9,12},{10,... | collective-permute-start | bytes 76808 | tf_op jit(solution)/shard_map/ppermute | solution.py:355
  8.9 8.4 %slice-start.3 = ((s8[12582912]{0:T(1024)(128)(4,1)}), s8[4194304]{0:T(1024)(128)(4,1)S(1)}, s32[]{:S(2)}) async-start(s8[12582912]{0:T(1024)(128)(4,1)} %bitcast.8), calls=%async_computation.3 | async-start | bytes 8388608
  9.0 8.4 %slice-start.4 = ((s8[12582912]{0:T(1024)(128)(4,1)}), s8[4194304]{0:T(1024)(128)(4,1)S(1)}, s32[]{:S(2)}) async-start(s8[12582912]{0:T(1024)(128)(4,1)} %bitcast.8), calls=%async_computation.4 | async-start | bytes 8388608
  9.0 8.3 %slice-start.5 = ((s8[12582912]{0:T(1024)(128)(4,1)}), s8[4194304]{0:T(1024)(128)(4,1)S(1)}, s32[]{:S(2)}) async-start(s8[12582912]{0:T(1024)(128)(4,1)} %bitcast.8), calls=%async_computation.5 | async-start | bytes 8388608
  9.0 6.5 %collective-permute-start.3 = (bf16[8,3200]{1,0:T(8,128)(2,1)S(1)}, bf16[8,3200]{1,0:T(8,128)(2,1)S(1)}, u32[]{:S(2)}, u32[]{:S(2)}) collective-permute-start(bf16[8,3200]{1,0:T(8,128)(2,1)S(1)} %pad_maximum_fusion.refs_0_), channel_id=1, source_target_pairs={{0,11},{1,10},{2,9},{3,8},{4,15},{5,14},{6,13},{7,12},{8,3},{9,2},... | collective-permute-start | bytes 153608 | tf_op jit(solution)/shard_map/ppermute | solution.py:355
  11.8 4.1 %collective-permute-start.2 = (bf16[8,3200]{1,0:T(8,128)(2,1)S(1)}, bf16[8,3200]{1,0:T(8,128)(2,1)S(1)}, u32[]{:S(2)}, u32[]{:S(2)}) collective-permute-start(bf16[8,3200]{1,0:T(8,128)(2,1)S(1)} %pad_maximum_fusion.refs_0_), channel_id=1, source_target_pairs={{0,3},{1,2},{2,1},{3,0},{4,7},{5,6},{6,5},{7,4},{8,11},{9,10},{10,... | collective-permute-start | bytes 153608 | tf_op jit(solution)/shard_map/ppermute | solution.py:355
  11.8 4.1 %collective-permute-start.1 = (bf16[8,3200]{1,0:T(8,128)(2,1)S(1)}, bf16[8,3200]{1,0:T(8,128)(2,1)S(1)}, u32[]{:S(2)}, u32[]{:S(2)}) collective-permute-start(bf16[8,3200]{1,0:T(8,128)(2,1)S(1)} %pad_maximum_fusion.refs_0_), channel_id=1, source_target_pairs={{0,9},{1,8},{2,11},{3,10},{4,13},{5,12},{6,15},{7,14},{8,1},{9,0},... | collective-permute-start | bytes 153608 | tf_op jit(solution)/shard_map/ppermute | solution.py:355
  15.9 1.4 %collective-permute-start.4 = (bf16[32,1664]{1,0:T(8,128)(2,1)S(1)}, bf16[32,1664]{1,0:T(8,128)(2,1)S(1)}, u32[]{:S(2)}, u32[]{:S(2)}) collective-permute-start(bf16[32,1664]{1,0:T(8,128)(2,1)S(1)} %get-tuple-element.36), channel_id=1, source_target_pairs={{0,1},{1,0},{2,3},{3,2},{4,5},{5,4},{6,7},{7,6},{8,9},{9,8},{10,11... | collective-permute-start | bytes 319496 | tf_op jit(solution)/shard_map/ppermute | solution.py:351
  17.3 4.4 %slice-start = ((s8[12582912]{0:T(1024)(128)(4,1)}), s8[4194304]{0:T(1024)(128)(4,1)S(1)}, s32[]{:S(2)}) async-start(s8[12582912]{0:T(1024)(128)(4,1)} %bitcast.6), calls=%async_computation | async-start | bytes 8388608
  17.3 4.4 %slice-start.1 = ((s8[12582912]{0:T(1024)(128)(4,1)}), s8[4194304]{0:T(1024)(128)(4,1)S(1)}, s32[]{:S(2)}) async-start(s8[12582912]{0:T(1024)(128)(4,1)} %bitcast.6), calls=%async_computation.1 | async-start | bytes 8388608
  19.2 2.5 %collective-permute-start.6 = (bf16[64,4096]{1,0:T(8,128)(2,1)S(1)}, bf16[64,4096]{1,0:T(8,128)(2,1)S(1)}, u32[]{:S(2)}, u32[]{:S(2)}) collective-permute-start(bf16[64,4096]{1,0:T(8,128)(2,1)S(1)} %gate_up.2.refs_2_), channel_id=1, source_target_pairs={{0,1},{1,0},{2,3},{3,2},{4,5},{5,4},{6,7},{7,6},{8,9},{9,8},{10,11... | collective-permute-start | bytes 1572872 | tf_op jit(solution)/shard_map/ppermute | solution.py:351
  19.5 2.7 %slice-start.2 = ((s8[12582912]{0:T(1024)(128)(4,1)}), s8[4194304]{0:T(1024)(128)(4,1)S(1)}, s32[]{:S(2)}) async-start(s8[12582912]{0:T(1024)(128)(4,1)} %bitcast.6), calls=%async_computation.2 | async-start | bytes 8388608
  21.4 2.0 %collective-permute-start.5 = (bf16[64,4096]{1,0:T(8,128)(2,1)S(1)}, bf16[64,4096]{1,0:T(8,128)(2,1)S(1)}, u32[]{:S(2)}, u32[]{:S(2)}) collective-permute-start(bf16[64,4096]{1,0:T(8,128)(2,1)S(1)} %gate_up.3.refs_2_), channel_id=1, source_target_pairs={{0,1},{1,0},{2,3},{3,2},{4,5},{5,4},{6,7},{7,6},{8,9},{9,8},{10,11... | collective-permute-start | bytes 1572872 | tf_op jit(solution)/shard_map/ppermute | solution.py:351
  24.5 1.4 %collective-permute-start.7 = (bf16[32,1536]{1,0:T(8,128)(2,1)S(1)}, bf16[32,1536]{1,0:T(8,128)(2,1)S(1)}, u32[]{:S(2)}, u32[]{:S(2)}) collective-permute-start(bf16[32,1536]{1,0:T(8,128)(2,1)S(1)} %get-tuple-element.46), channel_id=1, source_target_pairs={{0,1},{1,0},{2,3},{3,2},{4,5},{5,4},{6,7},{7,6},{8,9},{9,8},{10,11... | collective-permute-start | bytes 294920 | tf_op jit(solution)/shard_map/ppermute | solution.py:351
  25.9 4.6 %collective-permute-start.8 = (bf16[8,3072]{1,0:T(8,128)(2,1)S(1)}, bf16[8,3072]{1,0:T(8,128)(2,1)S(1)}, u32[]{:S(2)}, u32[]{:S(2)}) collective-permute-start(bf16[8,3072]{1,0:T(8,128)(2,1)S(1)} %get-tuple-element.48), channel_id=1, source_target_pairs={{0,11},{1,10},{2,9},{3,8},{4,15},{5,14},{6,13},{7,12},{8,3},{9,2},... | collective-permute-start | bytes 147464 | tf_op jit(solution)/shard_map/ppermute | solution.py:355
  28.2 3.6 %collective-permute-start.9 = (bf16[8,3072]{1,0:T(8,128)(2,1)S(1)}, bf16[8,3072]{1,0:T(8,128)(2,1)S(1)}, u32[]{:S(2)}, u32[]{:S(2)}) collective-permute-start(bf16[8,3072]{1,0:T(8,128)(2,1)S(1)} %get-tuple-element.49), channel_id=1, source_target_pairs={{0,9},{1,8},{2,11},{3,10},{4,13},{5,12},{6,15},{7,14},{8,1},{9,0},... | collective-permute-start | bytes 147464 | tf_op jit(solution)/shard_map/ppermute | solution.py:355
  28.6 3.7 %collective-permute-start.10 = (bf16[8,3072]{1,0:T(8,128)(2,1)S(1)}, bf16[8,3072]{1,0:T(8,128)(2,1)S(1)}, u32[]{:S(2)}, u32[]{:S(2)}) collective-permute-start(bf16[8,3072]{1,0:T(8,128)(2,1)S(1)} %get-tuple-element.50), channel_id=1, source_target_pairs={{0,3},{1,2},{2,1},{3,0},{4,7},{5,6},{6,5},{7,4},{8,11},{9,10},{10,... | collective-permute-start | bytes 147464 | tf_op jit(solution)/shard_map/ppermute | solution.py:355
  32.4 4.2 %collective-permute-start.11 = (bf16[4,3072]{1,0:T(4,128)(2,1)S(1)}, bf16[4,3072]{1,0:T(4,128)(2,1)S(1)}, u32[]{:S(2)}, u32[]{:S(2)}) collective-permute-start(bf16[4,3072]{1,0:T(4,128)(2,1)S(1)} %get-tuple-element.51), channel_id=1, source_target_pairs={{0,5},{1,4},{2,7},{3,6},{4,1},{5,0},{6,3},{7,2},{8,13},{9,12},{10,... | collective-permute-start | bytes 73736 | tf_op jit(solution)/shard_map/ppermute | solution.py:355
